TPU v7x, 256 devices: a whole 4x4x8 slice. The times are simulated.
256 devices in a mesh: seg: 8 (over z_lo, core), slab: 32 (over z_hi, y, x).
Axes of the slice: x: 4, y: 4, z: 8 (z_hi: 2, z_lo: 4; z = z_hi * 4 + z_lo), core: 2. Of those that a mesh axis runs over, the one named last changes fastest.
Arguments:
- activity: float32 [2048, 2048], P('slab'), may hold values from 0.5 to 1.5
- measured: float32 [32, 8, 64, 32, 384], P('seg', None, 'slab'), may hold values from 0.5 to 4
- randoms: int32 [32, 8, 2048, 384], P('seg', None, 'slab'), may hold values from 0 to 8
- footprint: bfloat16 [8, 2048, 384], replicated, may hold values from 0 to 577, as said below
- kernel: float32 [16, 9], replicated, may hold values from 0.03 to 0.3
- dead_counts: int32 [65536], replicated, may hold values from 0 to 1000
- crystals: int32 [2, 8, 384], replicated, may hold values from 0 to 65535
- sensitivity: float32 [2048, 2048], P('slab'), may hold values from 30 to 120
Outputs:
- new_activity: float32 [2048, 2048], P('slab')
Inputs may be any that keep to these rules, and one draw needn't show every extreme that they name: footprint weights are non-negative.
All inputs are finite; a program needn't handle non-finite values.
Results may differ from a plain program's by a relative error of at most 0.0003.
Values sent between devices are 32-bit elements; how exact they have to be, the bound alone decides.
No kernel may reach another device: no remote copies, remote signals or barrier semaphores. Data moves between devices by JAX's collectives and lax.ppermute only.
A program may use at most 128 MiB of HBM per device.

v0:
```python
import jax
import jax.numpy as jnp
from jax import lax
from jax.sharding import PartitionSpec as P

dead_time_tau = 0.001


def padded(cells, sides, width):
    for axis, dim in sides:
        count = lax.axis_size(axis)
        ends = count - 1
        head = lax.slice_in_dim(cells, 0, width, axis=dim)
        tail = lax.slice_in_dim(cells, cells.shape[dim] - width, cells.shape[dim], axis=dim)
        cells = jnp.concatenate(
            [
                lax.ppermute(tail, axis, [(i, (i + 1) % count) for i in range(ends)]),
                cells,
                lax.ppermute(head, axis, [((i + 1) % count, i) for i in range(ends)]),
            ],
            axis=dim,
        )
    return cells


def local(activity, measured, randoms, footprint, kernel, dead_counts, crystals, sensitivity):
    seg_dev = measured.shape[0]
    view_count = measured.shape[1]
    bin_count = measured.shape[4]
    slab_rows = activity.shape[0]
    pixel_count = activity.shape[1]
    tap_count = kernel.shape[1]
    margin = (tap_count - 1) // 2
    relaid = lax.all_to_all(measured, "slab", split_axis=3, concat_axis=2, tiled=True)
    measured_rows = relaid.reshape(seg_dev, view_count, slab_rows, bin_count)
    group_index = lax.axis_index("seg")
    half_groups = lax.axis_size("seg") // 2
    first_row = group_index % half_groups * seg_dev
    plain_weights = lax.dynamic_slice_in_dim(kernel, first_row, seg_dev, 0)
    axial_weights = jnp.where(group_index >= half_groups, plain_weights[:, ::-1], plain_weights)
    counts = dead_counts[crystals].astype(jnp.float32)
    efficiency = 1.0 / ((1.0 + dead_time_tau * counts[0]) * (1.0 + dead_time_tau * counts[1]))
    extended = padded(activity, (("slab", 0),), margin)
    axial_rows = jnp.zeros((seg_dev, slab_rows, pixel_count), jnp.float32)
    for offset in range(tap_count):
        axial_rows = (
            axial_rows
            + axial_weights[:, offset, None, None] * extended[None, offset : offset + slab_rows]
        )
    axial_rows = axial_rows.astype(jnp.bfloat16)
    projected = (
        jnp.einsum("gzp,vpb->gvzb", axial_rows, footprint, preferred_element_type=jnp.float32)
        / pixel_count
    )
    expected = efficiency[None, :, None, :] * projected + 0.25 * (randoms.astype(jnp.float32) + 1.0)
    weighted = (efficiency[None, :, None, :] * measured_rows / expected).astype(jnp.bfloat16)
    spread = (
        jnp.einsum("gvzb,vpb->gzp", weighted, footprint, preferred_element_type=jnp.float32)
        / pixel_count
    )
    spread_ext = padded(spread, (("slab", 1),), margin)
    accumulated = jnp.zeros((seg_dev, slab_rows, pixel_count), jnp.float32)
    for offset in range(tap_count):
        start = 2 * margin - offset
        accumulated = (
            accumulated
            + axial_weights[:, offset, None, None] * spread_ext[:, start : start + slab_rows]
        )
    summed = jnp.sum(accumulated, axis=0)
    combined = lax.psum(summed, "seg")
    return activity * combined / sensitivity


def solution(mesh):
    placed = (
        P("slab", None),
        P("seg", None, "slab", None, None),
        P("seg", None, "slab", None),
        P(),
        P(),
        P(),
        P(),
        P("slab", None),
    )
    return jax.shard_map(
        local, mesh=mesh, in_specs=placed, out_specs=P("slab", None), check_vma=False
    )
```

profile of v0, /device:TPU:31, one launch (start us, length us, event | category | flops | bytes accessed | tf_op | source)
XLA Modules:
  0.0 238.2 jit_solution(16008035822630291747)
XLA Ops:
  6.5 0.0 copy-start
  6.5 5.4 %copy.13 = f32[4,8,2,32,384]{4,1,2,0,3:T(8,128)} copy(f32[4,8,2,32,384]{4,3,2,1,0:T(8,128)} %param.9) | data formatting | bytes 6291456 | tf_op args[1]
  12.0 13.4 %all-to-all-start = ((f32[4,8,2,32,384]{4,1,2,0,3:T(8,128)}), f32[4,8,2,32,384]{4,1,2,0,3:T(8,128)S(1)}, u32[]{:S(2)}, u32[]{:S(2)}) async-start(f32[4,8,2,32,384]{4,1,2,0,3:T(8,128)} %copy.13), calls=%async_computation | async-start | bytes 6291456 | tf_op jit(solution)/shard_map/all_to_all | solution.py:34
  25.4 0.0 all-reduce.2.cloned.1.call-start
  25.4 1.5 fusion.90
  26.9 7.0 %collective-permute-start = (f32[4,2048]{1,0:T(4,128)}, f32[4,2048]{1,0:T(4,128)S(1)}, u32[]{:S(2)}, u32[]{:S(2)}) collective-permute-start(f32[4,2048]{1,0:T(4,128)} %get-tuple-element.25), channel_id=1, source_target_pairs={{0,1},{1,2},{2,3},{3,4},{4,5},{5,6},{6,7},{7,8},{8,9},{9,10},{10,1... | collective-permute-start | bytes 98312 | tf_op jit(solution)/shard_map/ppermute | solution.py:17
  33.9 1.9 collective-permute-start.1
  35.9 0.7 constant_dynamic-slice_fusion
  36.6 0.7 rev.3
  37.2 0.0 copy-done.3
  37.3 0.0 copy-done
  37.3 34.3 %gather_fusion = s32[6144]{0:T(1024)S(1)} fusion(s32[65536]{0:T(1024)S(1)} %copy-done, s32[6144]{0:T(1024)S(1)} %broadcast_clamp_fusion), kind=kCustom, calls=%fused_computation | custom fusion | bytes 73728 | tf_op jit(solution)/shard_map/gather | solution.py:41
  71.6 0.7 broadcast_select_fusion
  72.3 0.9 slice_reduce_fusion.8
  73.2 0.0 collective-permute-done
  73.2 3.6 %fusion.80 = (f32[64,2048]{1,0:T(8,128)}, f32[64,2048]{1,0:T(8,128)}, f32[64,2048]{1,0:T(8,128)}, f32[64,2048]{1,0:T(8,128)}, f32[68,2048]{1,0:T(8,128)S(1)}) fusion(f32[64,2048]{1,0:T(8,128)} %param.8, f32[4,2048]{1,0:T(4,128)S(1)} %collective-permute-done), kind=kLoop, calls=%fused_computation.78 | loop fusion | flops 524287 | bytes 3178496 | tf_op jit(solution)/shard_map/concatenate | solution.py:15
  76.8 0.0 collective-permute-done.1
  76.8 1.4 fusion.89
  78.2 0.0 all-to-all-done
  78.2 3.3 %copy.14 = f32[4,8,32,2,1,384]{5,3,2,1,0,4:T(2,128)} copy(f32[4,8,32,2,1,384]{5,1,3,0,2,4:T(8,128)S(1)} %bitcast.41) | data formatting | bytes 6291456 | tf_op jit(solution)/shard_map/all_to_all | solution.py:34
  81.5 3.9 %reshape.47 = f32[4,8,64,384]{3,2,1,0:T(8,128)S(1)} reshape(f32[4,8,32,2,1,384]{5,3,2,1,0,4:T(2,128)} %copy.14) | data formatting | bytes 6291456 | tf_op jit(solution)/shard_map/reshape | solution.py:35
  85.4 0.0 copy-done.4
  85.5 20.0 %broadcast_multiply_fusion = (f32[4,64,2048]{2,1,0:T(8,128)}, f32[4,64,2048]{2,1,0:T(8,128)}) fusion(bf16[8,2048,384]{2,1,0:T(8,128)(2,1)} %param.11, s32[4,8,64,384]{3,2,1,0:T(8,128)} %param.10, f32[4,8,64,384]{3,2,1,0:T(8,128)S(1)} %reshape.47, f32[8,384]{1,0:T(8,128)S(1)} %broadcast_multiply_fusion.1, f32[8,384]{1,0:T(8,128)S(1)} %div.25, ...), kind=kOutput, calls=%fused_computation.55 | convolution fusion | flops 6458703872 | bytes 27811984 | tf_op jit(solution)/shard_map/gvzb,vpb->gzp/dot_general | solution.py:58
  105.5 1.1 fusion.88
  106.6 1.9 collective-permute-start.2
  108.5 11.5 %collective-permute-start.3 = (f32[4,4,2048]{2,1,0:T(4,128)S(1)}, f32[4,4,2048]{2,1,0:T(4,128)S(1)}, u32[]{:S(2)}, u32[]{:S(2)}) collective-permute-start(f32[4,4,2048]{2,1,0:T(4,128)S(1)} %get-tuple-element.15), channel_id=1, source_target_pairs={{0,1},{1,2},{2,3},{3,4},{4,5},{5,6},{6,7},{7,8},{8,9},{9,10},{10,1... | collective-permute-start | bytes 393224 | tf_op jit(solution)/shard_map/ppermute | solution.py:17
  120.0 0.4 collective-permute-done.2
  120.4 1.5 collective-permute-done.3
  121.9 11.4 %fusion.13 = f32[64,2048]{1,0:T(8,128)} fusion(f32[4,64,2048]{2,1,0:T(8,128)} %get-tuple-element.27, f32[4,4,2048]{2,1,0:T(4,128)S(1)} %collective-permute-done.3, f32[4,4,2048]{2,1,0:T(4,128)S(1)} %collective-permute-done.2, f32[4,64,2048]{2,1,0:T(8,128)} %get-tuple-element.28, f32[4]{0:T(128)S(1)} %broadcast_multiply_fusion.2, f32[4]{0:T(128)S(1)} %get-tuple-element.6, ...), kind=kLoop, calls=%fused_computation.25 | loop fusion | flops 13500416 | bytes 4980880 | tf_op jit(solution)/shard_map/reduce_sum | solution.py:69
  133.3 0.0 all-reduce.2.cloned.1.call-update
  133.4 96.0 %all-reduce.2.cloned.1.call-done = f32[64,2048]{1,0:T(8,128)} async-done(((f32[64,2048]{1,0:T(8,128)}), f32[64,2048]{1,0:T(8,128)}) %all-reduce.2.cloned.1.call-update) | async-done | bytes 524304 | tf_op jit(solution)/shard_map/psum | solution.py:70
  229.4 1.9 multiply_divide_fusion
  (19 shorter events, 0.1 us)
Async XLA Ops:
  6.5 30.7 %copy-start = (s32[65536]{0:T(1024)S(1)}, s32[65536]{0:T(1024)}, u32[]{:S(2)}) copy-start(s32[65536]{0:T(1024)} %param.13) | copy-start | bytes 786436
  12.0 25.3 %copy-start.3 = (s32[2,8,384]{2,1,0:T(8,128)S(1)}, s32[2,8,384]{2,1,0:T(8,128)}, u32[]{:S(2)}) copy-start(s32[2,8,384]{2,1,0:T(8,128)} %param.14) | copy-start | bytes 73732
  12.0 66.2 %all-to-all-start = ((f32[4,8,2,32,384]{4,1,2,0,3:T(8,128)}), f32[4,8,2,32,384]{4,1,2,0,3:T(8,128)S(1)}, u32[]{:S(2)}, u32[]{:S(2)}) async-start(f32[4,8,2,32,384]{4,1,2,0,3:T(8,128)} %copy.13), calls=%async_computation | async-start | bytes 6291456 | tf_op jit(solution)/shard_map/all_to_all | solution.py:34
  25.4 204.0 %all-reduce.2.cloned.1.call-start = ((), (), s32[]{:S(2)}) async-start(), calls=%async_computation.1 | async-start | bytes 1048576 | tf_op jit(solution)/shard_map/psum | solution.py:70
  26.9 46.3 %collective-permute-start = (f32[4,2048]{1,0:T(4,128)}, f32[4,2048]{1,0:T(4,128)S(1)}, u32[]{:S(2)}, u32[]{:S(2)}) collective-permute-start(f32[4,2048]{1,0:T(4,128)} %get-tuple-element.25), channel_id=1, source_target_pairs={{0,1},{1,2},{2,3},{3,4},{4,5},{5,6},{6,7},{7,8},{8,9},{9,10},{10,1... | collective-permute-start | bytes 98312 | tf_op jit(solution)/shard_map/ppermute | solution.py:17
  33.9 42.9 %collective-permute-start.1 = (f32[4,2048]{1,0:T(4,128)S(1)}, f32[4,2048]{1,0:T(4,128)S(1)}, u32[]{:S(2)}, u32[]{:S(2)}) collective-permute-start(f32[4,2048]{1,0:T(4,128)S(1)} %get-tuple-element.26), channel_id=1, source_target_pairs={{1,0},{2,1},{3,2},{4,3},{5,4},{6,5},{7,6},{8,7},{9,8},{10,9},{11,1... | collective-permute-start | bytes 98312 | tf_op jit(solution)/shard_map/ppermute | solution.py:19
  81.5 3.9 %copy-start.4 = (f32[4]{0:T(128)S(1)}, f32[4]{0:T(128)}, u32[]{:S(2)}) copy-start(f32[4]{0:T(128)} %get-tuple-element.12) | copy-start | bytes 52
  81.5 3.9 %copy-start.5 = (f32[4]{0:T(128)S(1)}, f32[4]{0:T(128)}, u32[]{:S(2)}) copy-start(f32[4]{0:T(128)} %get-tuple-element.13) | copy-start | bytes 52
  81.5 4.0 %copy-start.6 = (f32[4]{0:T(128)S(1)}, f32[4]{0:T(128)}, u32[]{:S(2)}) copy-start(f32[4]{0:T(128)} %get-tuple-element.10) | copy-start | bytes 52
  106.6 13.8 %collective-permute-start.2 = (f32[4,4,2048]{2,1,0:T(4,128)S(1)}, f32[4,4,2048]{2,1,0:T(4,128)S(1)}, u32[]{:S(2)}, u32[]{:S(2)}) collective-permute-start(f32[4,4,2048]{2,1,0:T(4,128)S(1)} %get-tuple-element.14), channel_id=1, source_target_pairs={{1,0},{2,1},{3,2},{4,3},{5,4},{6,5},{7,6},{8,7},{9,8},{10,9},{11,1... | collective-permute-start | bytes 393224 | tf_op jit(solution)/shard_map/ppermute | solution.py:19
  108.5 13.4 %collective-permute-start.3 = (f32[4,4,2048]{2,1,0:T(4,128)S(1)}, f32[4,4,2048]{2,1,0:T(4,128)S(1)}, u32[]{:S(2)}, u32[]{:S(2)}) collective-permute-start(f32[4,4,2048]{2,1,0:T(4,128)S(1)} %get-tuple-element.15), channel_id=1, source_target_pairs={{0,1},{1,2},{2,3},{3,4},{4,5},{5,6},{6,7},{7,8},{8,9},{9,10},{10,1... | collective-permute-start | bytes 393224 | tf_op jit(solution)/shard_map/ppermute | solution.py:17
  121.9 107.5 %copy-start.1 = (f32[64,2048]{1,0:T(8,128)S(1)}, f32[64,2048]{1,0:T(8,128)}, u32[]{:S(2)}) copy-start(f32[64,2048]{1,0:T(8,128)} %param.8) | copy-start | bytes 1572868
  121.9 107.5 %copy-start.2 = (f32[64,2048]{1,0:T(8,128)S(1)}, f32[64,2048]{1,0:T(8,128)}, u32[]{:S(2)}) copy-start(f32[64,2048]{1,0:T(8,128)} %param.15) | copy-start | bytes 1572868
Sparse Core Ops, SparseCore 0:
  133.5 95.8 all-reduce.1
where the time goes:
time: 241 us; the launch traced here: 238 us
  waiting for transfers between devices  98 us (41%)
  local copies, waits for them, and re-layouts  53.1 us (22%)
  starting transfers between devices  35.8 us (15%)
  matrix products  20 us (8%)
  other arithmetic  17.7 us (7%)
  between operations  13.6 us (6%)
    psum x1, waiting for transfers between devices, local(): combined = lax.psum(summed, 'seg')  96 us
    gather x1, local copies, waits for them, and re-layouts, local(): counts = dead_counts[crystals].astype(jnp.float32)  34.3 us
    dot_general x1, matrix products, local(): jnp.einsum('gvzb,vpb->gzp', weighted, footprint, preferred_element_type=j...  20 us
    ppermute x2, starting transfers between devices, padded(): lax.ppermute(tail, axis, [(i, (i + 1) % count) for i in range(ends)])  18.5 us
    all_to_all x1, starting transfers between devices, local(): lax.all_to_all(measured, 'slab', split_axis=3, concat_axis=2, tiled=True)  13.4 us
    reduce_sum x1, other arithmetic, local(): summed = jnp.sum(accumulated, axis=0)  11.4 us
    unnamed x15, local copies, waits for them, and re-layouts  5.45 us
  transfers between devices with their start and end apart: 6, of which 3 were waited for; matrix products, arithmetic and copies ran while one was open for 18% of the time, Pallas kernels for 0%

commit v1 on v0

v1 whole, which is shorter than its diff:
```python
import functools
import jax
import jax.numpy as jnp
from jax import lax
from jax.experimental import pallas as pl
from jax.experimental.pallas import tpu as pltpu
from jax.sharding import PartitionSpec as P

dead_time_tau = 0.001
f32 = jnp.float32
bf16 = jnp.bfloat16
LANES = 128
VMEM = pl.BlockSpec(memory_space=pltpu.VMEM)
SMEM = pl.BlockSpec(memory_space=pltpu.SMEM)


def params(mib):
    return pltpu.CompilerParams(vmem_limit_bytes=mib << 20)


def lane_blocks(bins):
    return bins // LANES


def relay_kernel(*refs):
    *m_refs, o_ref = refs
    segs, _, inner, slabs, _ = m_refs[0].shape
    rows = segs * inner

    for lane, m_ref in enumerate(m_refs):
        flat = m_ref.reshape(rows * slabs, LANES)
        for s in range(slabs):
            o_ref[s, 0, :, lane * LANES : (lane + 1) * LANES] = flat[pl.ds(s, rows, stride=slabs), :]


def relay(measured):
    segs, views, inner, slabs, bins = measured.shape
    rows = segs * inner
    lanes = [
        pl.BlockSpec((segs, 1, inner, slabs, LANES), lambda v, lane=lane: (0, v, 0, 0, lane))
        for lane in range(lane_blocks(bins))
    ]
    return pl.pallas_call(
        relay_kernel,
        grid=(views,),
        in_specs=lanes,
        out_specs=pl.BlockSpec((slabs, 1, rows, bins), lambda v: (0, v, 0, 0)),
        out_shape=jax.ShapeDtypeStruct((slabs, views, rows, bins), f32),
        compiler_params=params(16),
    )(*[measured] * len(lanes))


def split_two(x):
    hi = x.astype(bf16)
    return hi, (x - hi.astype(f32)).astype(bf16)


def efficiency_kernel(t_ref, c_ref, o_ref):
    lanes, depth = t_ref.shape
    views = o_ref.shape[0]
    bins = c_ref.shape[-1]
    table = t_ref[...].astype(f32)
    first = table.astype(bf16)
    rest = table - first.astype(f32)
    second = rest.astype(bf16)
    third = (rest - second.astype(f32)).astype(bf16)
    pieces = jnp.concatenate([first, second, third], axis=0)
    depth_ids = lax.broadcasted_iota(jnp.int32, (depth, bins), 0)
    lane_ids = lax.broadcasted_iota(jnp.int32, (lanes, bins), 0)

    def look(index):
        row = index // lanes
        hot = jnp.where(depth_ids == row, 1.0, 0.0).astype(bf16)
        got = jnp.dot(pieces, hot, preferred_element_type=f32)
        value = got[:lanes] + got[lanes : 2 * lanes] + got[2 * lanes :]
        return jnp.sum(jnp.where(lane_ids == index - row * lanes, value, 0.0), axis=0, keepdims=True)

    def one_view(v, carry):
        first_factor = 1.0 + dead_time_tau * look(c_ref[0, v])
        second_factor = 1.0 + dead_time_tau * look(c_ref[1, v])
        o_ref[v] = 1.0 / (first_factor * second_factor)
        return carry

    lax.fori_loop(0, views, one_view, 0)


def efficiency_of(dead_counts, crystals):
    _, views, bins = crystals.shape
    table = dead_counts.reshape(-1, 128).T
    return pl.pallas_call(
        efficiency_kernel,
        in_specs=[VMEM, VMEM],
        out_specs=VMEM,
        out_shape=jax.ShapeDtypeStruct((views, 1, bins), f32),
        compiler_params=params(16),
    )(table, crystals.reshape(2, views, 1, bins))


def forward_kernel(op_ref, ext_ref, foot_ref, eff_ref, *refs):
    lanes = len(refs) // 2 - 1
    rand_refs, o_ref, rows_ref, order_refs = refs[:lanes], refs[lanes], refs[lanes + 1], refs[lanes + 2 :]
    segs, _, slices, _ = rand_refs[0].shape
    pixels = ext_ref.shape[1]
    inner = 2
    count = slices // inner

    @pl.when(pl.program_id(0) == 0)
    def _():
        rows_ref[...] = jnp.dot(
            op_ref[...], ext_ref[...], preferred_element_type=f32, precision=lax.Precision.HIGHEST
        ).astype(bf16)

    projected = jnp.dot(rows_ref[...], foot_ref[0], preferred_element_type=f32) * (1.0 / pixels)
    for lane in range(lanes):
        flat = rand_refs[lane].reshape(segs * slices, LANES)
        order_ref = order_refs[lane]
        for g in range(segs):
            for a in range(inner):
                got = flat[pl.ds(g * slices + a, count, stride=inner), :].astype(f32)
                order_ref[pl.ds(g * inner + a, count, stride=segs * inner), :] = 0.25 * (got + 1.0)
        cols = slice(lane * LANES, (lane + 1) * LANES)
        eff = eff_ref[0, :, cols]
        o_ref[0, :, cols] = eff / (eff * projected[:, cols] + order_ref[...])


def forward(operator, extended, footprint, randoms, efficiency):
    segs, views, slices, bins = randoms.shape
    pixels = footprint.shape[1]
    rows = segs * slices
    lanes = [
        pl.BlockSpec((segs, 1, slices, LANES), lambda v, lane=lane: (0, v, 0, lane))
        for lane in range(lane_blocks(bins))
    ]
    return pl.pallas_call(
        forward_kernel,
        grid=(views,),
        in_specs=[
            VMEM,
            VMEM,
            pl.BlockSpec((1, pixels, bins), lambda v: (v, 0, 0)),
            pl.BlockSpec((1, 1, bins), lambda v: (v, 0, 0)),
        ]
        + lanes,
        out_specs=pl.BlockSpec((1, rows, bins), lambda v: (v, 0, 0)),
        out_shape=jax.ShapeDtypeStruct((views, rows, bins), f32),
        scratch_shapes=[pltpu.VMEM((rows, pixels), bf16)] + [pltpu.VMEM((rows, LANES), f32)] * len(lanes),
        compiler_params=params(32),
        cost_estimate=pl.CostEstimate(
            flops=2 * rows * pixels * bins * views, bytes_accessed=20 << 20, transcendentals=0
        ),
    )(operator, extended, footprint, efficiency, *[randoms] * len(lanes))


def back_kernel(me_ref, opt_ref, x_ref, factor_ref, foot_ref, *refs):
    mine_refs, other_ref = refs[:4], refs[4]
    split_ref, acc_ref = refs[5], refs[6]
    ext = opt_ref.shape[0]
    pixels = acc_ref.shape[1]
    step = pl.program_id(0)
    rows = factor_ref.shape[1]

    @pl.when(step == 0)
    def _():
        hi, lo = split_two(opt_ref[...])
        split_ref[:ext] = hi
        split_ref[ext:] = lo
        acc_ref[...] = jnp.zeros_like(acc_ref)

    weighted = (factor_ref[0] * x_ref[:, 0].reshape(rows, -1)).astype(bf16)
    both = jnp.dot(split_ref[...], weighted, preferred_element_type=f32)
    hi, lo = split_two(both[:ext] + both[ext:])
    spread = lax.dot_general(
        jnp.concatenate([hi, lo], axis=0), foot_ref[0], (((1,), (1,)), ((), ())), preferred_element_type=f32
    )
    acc_ref[...] += spread[:ext] + spread[ext:]

    @pl.when(step == pl.num_programs(0) - 1)
    def _():
        kept, width = mine_refs[0].shape
        for k in range(4):
            for c in range(2):
                block = me_ref[0] ^ (2 * k + c)
                part = acc_ref[:kept, pl.ds(pl.multiple_of(block * width, width), width)] * (1.0 / pixels)
                if c == 0:
                    mine_refs[k][...] = part
                else:
                    other_ref[k] = part


def back(me, operator_t, rows_in, factor, footprint, kept):
    views, rows, bins = factor.shape
    slabs, _, inner, _ = rows_in.shape
    pixels = footprint.shape[1]
    width = pixels // 8
    ext = operator_t.shape[0]
    return pl.pallas_call(
        back_kernel,
        grid=(views,),
        in_specs=[
            SMEM,
            VMEM,
            pl.BlockSpec((slabs, 1, inner, bins), lambda v: (0, v, 0, 0)),
            pl.BlockSpec((1, rows, bins), lambda v: (v, 0, 0)),
            pl.BlockSpec((1, pixels, bins), lambda v: (v, 0, 0)),
        ],
        out_specs=[VMEM] * 5,
        out_shape=[jax.ShapeDtypeStruct((kept, width), f32)] * 4
        + [jax.ShapeDtypeStruct((4, kept, width), f32)],
        scratch_shapes=[pltpu.VMEM((2 * ext, rows), bf16), pltpu.VMEM((ext, pixels), f32)],
        compiler_params=params(32),
        cost_estimate=pl.CostEstimate(
            flops=4 * ext * pixels * bins * views, bytes_accessed=20 << 20, transcendentals=0
        ),
    )(me, operator_t, rows_in, factor, footprint)


def assemble_kernel(me_ref, *refs):
    near_refs, far_ref, o_ref = refs[:4], refs[4], refs[5]
    width = near_refs[0].shape[1]
    for k in range(4):
        for c in range(2):
            block = me_ref[0] ^ (2 * k + c)
            part = near_refs[k][...] if c == 0 else far_ref[k]
            o_ref[:, pl.ds(pl.multiple_of(block * width, width), width)] = part


def assemble(me, near, far):
    slices, width = near[0].shape
    return pl.pallas_call(
        assemble_kernel,
        in_specs=[SMEM] + [VMEM] * 5,
        out_specs=VMEM,
        out_shape=jax.ShapeDtypeStruct((slices, width * 8), f32),
        compiler_params=params(16),
    )(me, *near, far)


def local(activity, measured, randoms, footprint, kernel, dead_counts, crystals, sensitivity):
    segs, views, inner, slabs, bins = measured.shape
    slices, pixels = activity.shape
    taps = kernel.shape[1]
    margin = (taps - 1) // 2
    width = pixels // 8
    group = lax.axis_index("seg")
    me = group.astype(jnp.int32).reshape(1)
    halves = lax.axis_size("seg") // 2

    def swap(x, k):
        return lax.ppermute(x, "seg", [(i, i ^ k) for i in range(2 * halves)])

    def shift(x, up):
        pairs = [(i + 1, i) if up else (i, i + 1) for i in range(slabs - 1)]
        return lax.ppermute(x, "slab", pairs)

    rows_out = relay(measured)
    rows_in = lax.all_to_all(rows_out, "slab", split_axis=0, concat_axis=0, tiled=True)

    plain = lax.dynamic_slice_in_dim(kernel, group % halves * segs, segs, 0)
    weights = jnp.where(group >= halves, plain[:, ::-1], plain)
    ext = slices + 2 * margin
    ext_pad = ext + 8
    tap = jnp.arange(ext_pad)[None, None, None, :] - (
        inner * jnp.arange(slabs)[:, None, None, None] + jnp.arange(inner)[None, None, :, None]
    )
    operator = jnp.zeros((slabs, segs, inner, ext_pad), f32)
    for k in range(taps):
        operator = operator + jnp.where(tap == k, weights[None, :, k, None, None], 0.0)
    operator = operator.reshape(slabs * segs * inner, ext_pad)

    extended = jnp.concatenate(
        [
            shift(activity[slices - margin :], False),
            activity,
            shift(activity[:margin], True),
            jnp.zeros((ext_pad - ext, pixels), f32),
        ],
        axis=0,
    )
    efficiency = efficiency_of(dead_counts, crystals)
    factor = forward(operator, extended, footprint, randoms, efficiency)

    *mine, other = back(me, operator.T, rows_in, factor, footprint, ext)
    theirs = swap(other, 1)
    pair = [mine[k] + theirs[k] for k in range(4)]
    total = pair[0]
    for k in range(1, 4):
        total = total + swap(pair[k], 2 * k)
    above = shift(total[ext - margin :], False)
    below = shift(total[:margin], True)
    summed = jnp.concatenate(
        [
            total[margin : 2 * margin] + above,
            total[2 * margin : slices],
            total[slices : slices + margin] + below,
        ],
        axis=0,
    )
    start = group * width
    ratio = lax.dynamic_slice_in_dim(activity, start, width, 1) / lax.dynamic_slice_in_dim(
        sensitivity, start, width, 1
    )
    block = summed * ratio
    near = [block] + [swap(block, 2 * k) for k in range(1, 4)]
    far = swap(jnp.stack(near), 1)
    return assemble(me, near, far)


def solution(mesh):
    placed = (
        P("slab", None),
        P("seg", None, "slab", None, None),
        P("seg", None, "slab", None),
        P(),
        P(),
        P(),
        P(),
        P("slab", None),
    )
    return jax.shard_map(
        local, mesh=mesh, in_specs=placed, out_specs=P("slab", None), check_vma=False
    )
```

time: 241 us -> 171 us (0.71)
  waiting for transfers between devices: 98 us -> 45.8 us
  starting transfers between devices: 35.8 us -> 70.3 us
  local copies, waits for them, and re-layouts: 53.1 us -> 24.3 us
  Pallas kernels: 0 us -> 26.7 us
  matrix products: 20 us -> 0 us
  other arithmetic: 17.7 us -> 2.56 us
  between operations: 13.6 us -> 0.42 us
    psum x1 -> x0, waiting for transfers between devices: 96 us -> none  [local(): combined = lax.psum(summed, 'seg')]
    ppermute x4 -> x12, waiting for transfers between devices: 1.92 us -> 45.8 us  [the longest x4 33.3 us: shift(): return lax.ppermute(x, 'slab', pairs)]
    ppermute x4 -> x12, starting transfers between devices: 22.3 us -> 56.8 us  [the longest x8 37.8 us: swap(): return lax.ppermute(x, 'seg', [(i, i ^ k) for i in range(2 * halves)])]
    gather x1 -> x0, local copies, waits for them, and re-layouts: 34.3 us -> none  [local(): counts = dead_counts[crystals].astype(jnp.float32)]
    pallas_call x0 -> x5, Pallas kernels: none -> 26.7 us  [the longest x1 8.26 us: back(): pl.pallas_call(back_kernel, grid=(views,), in_specs=[SMEM, VMEM, pl.Block...]
    dot_general x1 -> x0, matrix products: 20 us -> none  [local(): jnp.einsum('gvzb,vpb->gzp', weighted, footprint, preferred_element_type=j...]
    reduce_sum x1 -> x0, other arithmetic: 11.4 us -> none  [local(): summed = jnp.sum(accumulated, axis=0)]
    unnamed x15 -> x16, local copies, waits for them, and re-layouts: 5.45 us -> 15.5 us
  transfers between devices with their start and end apart: 6 -> 13, of which waited for: 3 -> 9; matrix products, arithmetic and copies ran while one was open for 18% -> 6% of each run, Pallas kernels for 0% -> 8%
where the time goes in v1:
time: 171 us; the launch traced here: 170 us
  starting transfers between devices  70.3 us (41%)
  waiting for transfers between devices  45.8 us (27%)
  Pallas kernels  26.7 us (16%)
  local copies, waits for them, and re-layouts  24.3 us (14%)
  other arithmetic  2.56 us (1%)
    ppermute x8, starting transfers between devices, swap(): return lax.ppermute(x, 'seg', [(i, i ^ k) for i in range(2 * halves)])  37.8 us
    ppermute x4, waiting for transfers between devices, shift(): return lax.ppermute(x, 'slab', pairs)  33.3 us
    ppermute x4, starting transfers between devices, shift(): return lax.ppermute(x, 'slab', pairs)  18.9 us
    unnamed x16, local copies, waits for them, and re-layouts  15.5 us
    all_to_all x1, starting transfers between devices, local(): lax.all_to_all(rows_out, 'slab', split_axis=0, concat_axis=0, tiled=True)  13.5 us
    ppermute x8, waiting for transfers between devices, swap(): return lax.ppermute(x, 'seg', [(i, i ^ k) for i in range(2 * halves)])  12.5 us
    pallas_call x1, Pallas kernels, back(): pl.pallas_call(back_kernel, grid=(views,), in_specs=[SMEM, VMEM, pl.Block...  8.26 us
    pallas_call x1, Pallas kernels, forward(): pl.pallas_call(forward_kernel, grid=(views,), in_specs=[VMEM, VMEM, pl.Bl...  8.11 us
  transfers between devices with their start and end apart: 13, of which 9 were waited for; matrix products, arithmetic and copies ran while one was open for 6% of the time, Pallas kernels for 8%

profile of v1, /device:TPU:31, one launch (start us, length us, event | category | flops | bytes accessed | tf_op | source)
XLA Modules:
  0.0 170.1 jit_solution(4911168713437169212)
XLA Ops:
  0.0 1.9 %copy-done.3 = f32[4,8,2,32,384]{4,3,2,1,0:T(8,128)S(1)} copy-done((f32[4,8,2,32,384]{4,3,2,1,0:T(8,128)S(1)}, f32[4,8,2,32,384]{4,3,2,1,0:T(8,128)}, u32[]{:S(2)}) %copy-start.3) | copy-done | bytes 3145752
  1.9 4.6 %shard_map.82 = f32[32,8,8,384]{3,2,1,0:T(8,128)} custom-call(f32[4,8,2,32,384]{4,3,2,1,0:T(8,128)S(1)} %copy-done.3, f32[4,8,2,32,384]{4,3,2,1,0:T(8,128)S(1)} %copy-done.3, f32[4,8,2,32,384]{4,3,2,1,0:T(8,128)S(1)} %copy-done.3), custom_call_target="tpu_custom_call" | custom-call | tf_op jit(solution)/shard_map/pallas_call | solution.py:43
  6.5 13.5 %all-to-all-start = ((f32[32,8,8,384]{3,2,1,0:T(8,128)}), f32[32,8,8,384]{3,2,1,0:T(8,128)}, u32[]{:S(2)}, u32[]{:S(2)}) async-start(f32[32,8,8,384]{3,2,1,0:T(8,128)} %shard_map.82), calls=%async_computation | async-start | bytes 6291456 | tf_op jit(solution)/shard_map/all_to_all | solution.py:256
  20.0 1.6 fusion.16
  21.6 2.5 %collective-permute-start.1 = (f32[4,2048]{1,0:T(4,128)}, f32[4,2048]{1,0:T(4,128)S(1)}, u32[]{:S(2)}, u32[]{:S(2)}) collective-permute-start(f32[4,2048]{1,0:T(4,128)} %get-tuple-element.25), channel_id=1, source_target_pairs={{1,0},{2,1},{3,2},{4,3},{5,4},{6,5},{7,6},{8,7},{9,8},{10,9},{11,1... | collective-permute-start | bytes 98312 | tf_op jit(solution)/shard_map/ppermute | solution.py:253
  24.1 10.9 %collective-permute-start = (f32[4,2048]{1,0:T(4,128)}, f32[4,2048]{1,0:T(4,128)S(1)}, u32[]{:S(2)}, u32[]{:S(2)}) collective-permute-start(f32[4,2048]{1,0:T(4,128)} %get-tuple-element.24), channel_id=1, source_target_pairs={{0,1},{1,2},{2,3},{3,4},{4,5},{5,6},{6,7},{7,8},{8,9},{9,10},{10,1... | collective-permute-start | bytes 98312 | tf_op jit(solution)/shard_map/ppermute | solution.py:253
  41.0 1.1 copy.19
  42.9 4.9 %shard_map.83.eff_ref = f32[8,1,384]{2,1,0:T(1,128)S(1)} custom-call(s32[128,512]{1,0:T(8,128)S(1)} %bitcast.30, s32[2,8,1,384]{3,2,1,0:T(1,128)S(1)} %reshape.102.c_ref), custom_call_target="tpu_custom_call" | custom-call | tf_op jit(solution)/shard_map/pallas_call | solution.py:90
  47.8 21.7 %collective-permute-done.1 = f32[4,2048]{1,0:T(4,128)S(1)} collective-permute-done((f32[4,2048]{1,0:T(4,128)}, f32[4,2048]{1,0:T(4,128)S(1)}, u32[]{:S(2)}, u32[]{:S(2)}) %collective-permute-start.1) | collective-permute-done | bytes 32800 | tf_op jit(solution)/shard_map/ppermute | solution.py:253
  69.6 1.2 maximum_maximum_fusion.ext_ref
  70.7 4.6 %copy-done = bf16[8,2048,384]{2,1,0:T(8,128)(2,1)S(1)} copy-done((bf16[8,2048,384]{2,1,0:T(8,128)(2,1)S(1)}, bf16[8,2048,384]{2,1,0:T(8,128)(2,1)}, u32[]{:S(2)}) %copy-start) | copy-done | bytes 12582936
  75.3 0.9 copy-done.6
  76.2 8.1 %shard_map.84.factor_ref = f32[8,256,384]{2,1,0:T(8,128)S(1)} custom-call(f32[256,80]{1,0:T(8,128)S(1)} %copy-done.6, f32[80,2048]{1,0:T(8,128)S(1)} %maximum_maximum_fusion.ext_ref, bf16[8,2048,384]{2,1,0:T(8,128)(2,1)S(1)} %copy-done, f32[8,1,384]{2,1,0:T(1,128)S(1)} %shard_map.83.eff_ref, s32[4,8,64,384]{3,2,1,0:T(8,128)S(1)} %copy-done.2, ...), custom_call_target="tpu_custom_call" | custom-call | flops 3221225472 | bytes 20971520 | tf_op jit(solution)/shard_map/pallas_call | solution.py:134
  84.3 1.7 copy-done.4
  86.0 4.6 %copy-done.1 = bf16[8,2048,384]{2,1,0:T(8,128)(2,1)S(1)} copy-done((bf16[8,2048,384]{2,1,0:T(8,128)(2,1)S(1)}, bf16[8,2048,384]{2,1,0:T(8,128)(2,1)}, u32[]{:S(2)}) %copy-start.1) | copy-done | bytes 12582936
  90.6 1.9 %copy-done.5 = f32[8,256,384]{2,1,0:T(8,128)S(1)} copy-done((f32[8,256,384]{2,1,0:T(8,128)S(1)}, f32[8,256,384]{2,1,0:T(8,128)}, u32[]{:S(2)}) %copy-start.5) | copy-done | bytes 3145752
  92.5 8.3 %shard_map.85 = (f32[72,256]{1,0:T(8,128)S(1)}, f32[72,256]{1,0:T(8,128)S(1)}, f32[72,256]{1,0:T(8,128)S(1)}, f32[72,256]{1,0:T(8,128)S(1)}, f32[4,72,256]{2,1,0:T(8,128)S(1)}) custom-call(s32[1]{0:T(128)} %bitcast.me_ref, f32[80,256]{1,0:T(8,128)S(1)} %bitcast.31, f32[32,8,8,384]{3,2,1,0:T(8,128)} %all-to-all-done.x_ref, f32[8,256,384]{2,1,0:T(8,128)S(1)} %copy-done.5, ...), custom_call_target="tpu_custom_call" | custom-call | flops 2013265920 | bytes 20971520 | tf_op jit(solution)/shard_map/pallas_call | solution.py:196
  100.8 24.9 %collective-permute-start.2 = (f32[4,72,256]{2,1,0:T(8,128)S(1)}, f32[4,72,256]{2,1,0:T(8,128)S(1)}, u32[]{:S(2)}, u32[]{:S(2)}) collective-permute-start(f32[4,72,256]{2,1,0:T(8,128)S(1)} %get-tuple-element.11), channel_id=1, source_target_pairs={{0,32},{32,0},{64,96},{96,64},{128,160},{160,128},{192,224},{224,1... | collective-permute-start | bytes 884744 | tf_op jit(solution)/shard_map/ppermute | solution.py:249
  125.6 1.2 collective-permute-done.2
  126.9 1.7 %collective-permute-start.5 = (f32[72,256]{1,0:T(8,128)S(1)}, f32[72,256]{1,0:T(8,128)S(1)}, u32[]{:S(2)}, u32[]{:S(2)}) collective-permute-start(f32[72,256]{1,0:T(8,128)S(1)} %get-tuple-element.27), channel_id=1, source_target_pairs={{0,192},{32,224},{64,128},{96,160},{128,64},{160,96},{192,0},{224,... | collective-permute-start | bytes 221192 | tf_op jit(solution)/shard_map/ppermute | solution.py:249
  128.6 1.5 collective-permute-start.4
  130.5 1.6 collective-permute-done.5
  132.1 5.3 %collective-permute-done.4 = f32[72,256]{1,0:T(8,128)S(1)} collective-permute-done((f32[72,256]{1,0:T(8,128)S(1)}, f32[72,256]{1,0:T(8,128)S(1)}, u32[]{:S(2)}, u32[]{:S(2)}) %collective-permute-start.4) | collective-permute-done | bytes 73760 | tf_op jit(solution)/shard_map/ppermute | solution.py:249
  137.4 3.6 %collective-permute-start.6 = (f32[4,256]{1,0:T(4,128)S(1)}, f32[4,256]{1,0:T(4,128)S(1)}, u32[]{:S(2)}, u32[]{:S(2)}) collective-permute-start(f32[4,256]{1,0:T(4,128)S(1)} %slice.85), channel_id=1, source_target_pairs={{0,1},{1,2},{2,3},{3,4},{4,5},{5,6},{6,7},{7,8},{8,9},{9,10},{10,1... | collective-permute-start | bytes 12296 | tf_op jit(solution)/shard_map/ppermute | solution.py:253
  141.8 1.9 %collective-permute-start.7 = (f32[4,256]{1,0:T(4,128)S(1)}, f32[4,256]{1,0:T(4,128)S(1)}, u32[]{:S(2)}, u32[]{:S(2)}) collective-permute-start(f32[4,256]{1,0:T(4,128)S(1)} %get-tuple-element.30), channel_id=1, source_target_pairs={{1,0},{2,1},{3,2},{4,3},{5,4},{6,5},{7,6},{8,7},{9,8},{10,9},{11,1... | collective-permute-start | bytes 12296 | tf_op jit(solution)/shard_map/ppermute | solution.py:253
  143.7 10.8 %collective-permute-done.7 = f32[4,256]{1,0:T(4,128)S(1)} collective-permute-done((f32[4,256]{1,0:T(4,128)S(1)}, f32[4,256]{1,0:T(4,128)S(1)}, u32[]{:S(2)}, u32[]{:S(2)}) %collective-permute-start.7) | collective-permute-done | bytes 4128 | tf_op jit(solution)/shard_map/ppermute | solution.py:253
  154.5 0.9 maximum_multiply_fusion.refs_0_
  155.8 1.7 collective-permute-start.9
  157.4 1.6 collective-permute-start.10
  159.8 2.6 %collective-permute-done.10.refs_3_ = f32[64,256]{1,0:T(8,128)S(1)} collective-permute-done((f32[64,256]{1,0:T(8,128)S(1)}, f32[64,256]{1,0:T(8,128)S(1)}, u32[]{:S(2)}, u32[]{:S(2)}) %collective-permute-start.10) | collective-permute-done | bytes 65568 | tf_op jit(solution)/shard_map/ppermute | solution.py:249
  162.4 5.7 %collective-permute-start.11 = (f32[4,64,256]{2,1,0:T(8,128)S(1)}, f32[4,64,256]{2,1,0:T(8,128)S(1)}, u32[]{:S(2)}, u32[]{:S(2)}) collective-permute-start(f32[4,64,256]{2,1,0:T(8,128)S(1)} %pad_maximum_fusion), channel_id=1, source_target_pairs={{0,32},{32,0},{64,96},{96,64},{128,160},{160,128},{192,224},{224,1... | collective-permute-start | bytes 786440 | tf_op jit(solution)/shard_map/ppermute | solution.py:249
  168.1 1.2 collective-permute-done.11.refs_4_
  (83 shorter events, 9.7 us)
Async XLA Ops:
  0.0 1.9 %copy-start.3 = (f32[4,8,2,32,384]{4,3,2,1,0:T(8,128)S(1)}, f32[4,8,2,32,384]{4,3,2,1,0:T(8,128)}, u32[]{:S(2)}) copy-start(f32[4,8,2,32,384]{4,3,2,1,0:T(8,128)} %refs_2_.2) | copy-start | bytes 9437188
  6.5 31.1 %copy-start.7 = (f32[16,9]{1,0:T(8,128)S(1)}, f32[16,9]{1,0:T(8,128)}, u32[]{:S(2)}) copy-start(f32[16,9]{1,0:T(8,128)} %param.12) | copy-start | bytes 1732
  6.5 79.6 %all-to-all-start = ((f32[32,8,8,384]{3,2,1,0:T(8,128)}), f32[32,8,8,384]{3,2,1,0:T(8,128)}, u32[]{:S(2)}, u32[]{:S(2)}) async-start(f32[32,8,8,384]{3,2,1,0:T(8,128)} %shard_map.82), calls=%async_computation | async-start | bytes 6291456 | tf_op jit(solution)/shard_map/all_to_all | solution.py:256
  20.0 50.8 %copy-start.2 = (s32[4,8,64,384]{3,2,1,0:T(8,128)S(1)}, s32[4,8,64,384]{3,2,1,0:T(8,128)}, u32[]{:S(2)}) copy-start(s32[4,8,64,384]{3,2,1,0:T(8,128)} %refs_2_.3) | copy-start | bytes 9437188
  21.6 47.9 %collective-permute-start.1 = (f32[4,2048]{1,0:T(4,128)}, f32[4,2048]{1,0:T(4,128)S(1)}, u32[]{:S(2)}, u32[]{:S(2)}) collective-permute-start(f32[4,2048]{1,0:T(4,128)} %get-tuple-element.25), channel_id=1, source_target_pairs={{1,0},{2,1},{3,2},{4,3},{5,4},{6,5},{7,6},{8,7},{9,8},{10,9},{11,1... | collective-permute-start | bytes 98312 | tf_op jit(solution)/shard_map/ppermute | solution.py:253
  24.1 45.5 %collective-permute-start = (f32[4,2048]{1,0:T(4,128)}, f32[4,2048]{1,0:T(4,128)S(1)}, u32[]{:S(2)}, u32[]{:S(2)}) collective-permute-start(f32[4,2048]{1,0:T(4,128)} %get-tuple-element.24), channel_id=1, source_target_pairs={{0,1},{1,2},{2,3},{3,4},{4,5},{5,6},{6,7},{7,8},{8,9},{9,10},{10,1... | collective-permute-start | bytes 98312 | tf_op jit(solution)/shard_map/ppermute | solution.py:253
  70.7 4.6 %copy-start = (bf16[8,2048,384]{2,1,0:T(8,128)(2,1)S(1)}, bf16[8,2048,384]{2,1,0:T(8,128)(2,1)}, u32[]{:S(2)}) copy-start(bf16[8,2048,384]{2,1,0:T(8,128)(2,1)} %foot_ref.3) | copy-start | bytes 37748740
  75.3 0.9 copy-start.6
  84.3 1.7 copy-start.4
  86.0 4.6 %copy-start.1 = (bf16[8,2048,384]{2,1,0:T(8,128)(2,1)S(1)}, bf16[8,2048,384]{2,1,0:T(8,128)(2,1)}, u32[]{:S(2)}) copy-start(bf16[8,2048,384]{2,1,0:T(8,128)(2,1)} %foot_ref.3) | copy-start | bytes 37748740
  90.6 1.9 %copy-start.5 = (f32[8,256,384]{2,1,0:T(8,128)S(1)}, f32[8,256,384]{2,1,0:T(8,128)}, u32[]{:S(2)}) copy-start(f32[8,256,384]{2,1,0:T(8,128)} %copy-done.4) | copy-start | bytes 9437188
  100.8 26.1 %collective-permute-start.2 = (f32[4,72,256]{2,1,0:T(8,128)S(1)}, f32[4,72,256]{2,1,0:T(8,128)S(1)}, u32[]{:S(2)}, u32[]{:S(2)}) collective-permute-start(f32[4,72,256]{2,1,0:T(8,128)S(1)} %get-tuple-element.11), channel_id=1, source_target_pairs={{0,32},{32,0},{64,96},{96,64},{128,160},{160,128},{192,224},{224,1... | collective-permute-start | bytes 884744 | tf_op jit(solution)/shard_map/ppermute | solution.py:249
  126.9 5.2 %collective-permute-start.5 = (f32[72,256]{1,0:T(8,128)S(1)}, f32[72,256]{1,0:T(8,128)S(1)}, u32[]{:S(2)}, u32[]{:S(2)}) collective-permute-start(f32[72,256]{1,0:T(8,128)S(1)} %get-tuple-element.27), channel_id=1, source_target_pairs={{0,192},{32,224},{64,128},{96,160},{128,64},{160,96},{192,0},{224,... | collective-permute-start | bytes 221192 | tf_op jit(solution)/shard_map/ppermute | solution.py:249
  128.6 8.8 %collective-permute-start.4 = (f32[72,256]{1,0:T(8,128)S(1)}, f32[72,256]{1,0:T(8,128)S(1)}, u32[]{:S(2)}, u32[]{:S(2)}) collective-permute-start(f32[72,256]{1,0:T(8,128)S(1)} %get-tuple-element.28), channel_id=1, source_target_pairs={{0,128},{32,160},{64,192},{96,224},{128,0},{160,32},{192,64},{224,... | collective-permute-start | bytes 221192 | tf_op jit(solution)/shard_map/ppermute | solution.py:249
  130.1 7.3 %collective-permute-start.3 = (f32[72,256]{1,0:T(8,128)S(1)}, f32[72,256]{1,0:T(8,128)S(1)}, u32[]{:S(2)}, u32[]{:S(2)}) collective-permute-start(f32[72,256]{1,0:T(8,128)S(1)} %get-tuple-element.26), channel_id=1, source_target_pairs={{0,64},{32,96},{64,0},{96,32},{128,192},{160,224},{192,128},{224,1... | collective-permute-start | bytes 221192 | tf_op jit(solution)/shard_map/ppermute | solution.py:249
  137.4 4.4 %collective-permute-start.6 = (f32[4,256]{1,0:T(4,128)S(1)}, f32[4,256]{1,0:T(4,128)S(1)}, u32[]{:S(2)}, u32[]{:S(2)}) collective-permute-start(f32[4,256]{1,0:T(4,128)S(1)} %slice.85), channel_id=1, source_target_pairs={{0,1},{1,2},{2,3},{3,4},{4,5},{5,6},{6,7},{7,8},{8,9},{9,10},{10,1... | collective-permute-start | bytes 12296 | tf_op jit(solution)/shard_map/ppermute | solution.py:253
  141.8 12.7 %collective-permute-start.7 = (f32[4,256]{1,0:T(4,128)S(1)}, f32[4,256]{1,0:T(4,128)S(1)}, u32[]{:S(2)}, u32[]{:S(2)}) collective-permute-start(f32[4,256]{1,0:T(4,128)S(1)} %get-tuple-element.30), channel_id=1, source_target_pairs={{1,0},{2,1},{3,2},{4,3},{5,4},{6,5},{7,6},{8,7},{9,8},{10,9},{11,1... | collective-permute-start | bytes 12296 | tf_op jit(solution)/shard_map/ppermute | solution.py:253
  155.4 3.6 %collective-permute-start.8 = (f32[64,256]{1,0:T(8,128)S(1)}, f32[64,256]{1,0:T(8,128)S(1)}, u32[]{:S(2)}, u32[]{:S(2)}) collective-permute-start(f32[64,256]{1,0:T(8,128)S(1)} %maximum_multiply_fusion.refs_0_), channel_id=1, source_target_pairs={{0,64},{32,96},{64,0},{96,32},{128,192},{160,224},{192,128},{224,1... | collective-permute-start | bytes 196616 | tf_op jit(solution)/shard_map/ppermute | solution.py:249
  155.8 4.0 %collective-permute-start.9 = (f32[64,256]{1,0:T(8,128)S(1)}, f32[64,256]{1,0:T(8,128)S(1)}, u32[]{:S(2)}, u32[]{:S(2)}) collective-permute-start(f32[64,256]{1,0:T(8,128)S(1)} %maximum_multiply_fusion.refs_0_), channel_id=1, source_target_pairs={{0,128},{32,160},{64,192},{96,224},{128,0},{160,32},{192,64},{224,... | collective-permute-start | bytes 196616 | tf_op jit(solution)/shard_map/ppermute | solution.py:249
  157.4 4.9 %collective-permute-start.10 = (f32[64,256]{1,0:T(8,128)S(1)}, f32[64,256]{1,0:T(8,128)S(1)}, u32[]{:S(2)}, u32[]{:S(2)}) collective-permute-start(f32[64,256]{1,0:T(8,128)S(1)} %maximum_multiply_fusion.refs_0_), channel_id=1, source_target_pairs={{0,192},{32,224},{64,128},{96,160},{128,64},{160,96},{192,0},{224,... | collective-permute-start | bytes 196616 | tf_op jit(solution)/shard_map/ppermute | solution.py:249
  162.4 6.9 %collective-permute-start.11 = (f32[4,64,256]{2,1,0:T(8,128)S(1)}, f32[4,64,256]{2,1,0:T(8,128)S(1)}, u32[]{:S(2)}, u32[]{:S(2)}) collective-permute-start(f32[4,64,256]{2,1,0:T(8,128)S(1)} %pad_maximum_fusion), channel_id=1, source_target_pairs={{0,32},{32,0},{64,96},{96,64},{128,160},{160,128},{192,224},{224,1... | collective-permute-start | bytes 786440 | tf_op jit(solution)/shard_map/ppermute | solution.py:249

commit v2 on v1

v2 whole, which is shorter than its diff:
```python
import functools
import jax
import jax.numpy as jnp
from jax import lax
from jax.experimental import pallas as pl
from jax.experimental.pallas import tpu as pltpu
from jax.sharding import PartitionSpec as P

dead_time_tau = 0.001
f32 = jnp.float32
bf16 = jnp.bfloat16
LANES = 128
VMEM = pl.BlockSpec(memory_space=pltpu.VMEM)
SMEM = pl.BlockSpec(memory_space=pltpu.SMEM)
HBM = pl.BlockSpec(memory_space=pltpu.HBM)
SMALL = pl.CostEstimate(flops=1, bytes_accessed=1, transcendentals=0)
LARGE = pl.CostEstimate(flops=10**12, bytes_accessed=1 << 20, transcendentals=0)


def params(mib):
    return pltpu.CompilerParams(vmem_limit_bytes=mib << 20)


def lane_blocks(bins):
    return bins // LANES


def relay_kernel(sides, lanes, half_ref, *refs):
    m_refs, o_ref = refs[:lanes], refs[-1]
    segs, _, inner, slabs, _ = m_refs[0].shape
    rows = segs * inner
    count = o_ref.shape[0]
    for lane, m_ref in enumerate(m_refs):
        flat = m_ref.reshape(rows * slabs, LANES)
        cols = slice(lane * LANES, (lane + 1) * LANES)
        for slot, side in enumerate(sides):
            first = 0 if slabs == count else (half_ref[0] ^ side) * count
            for s in range(count):
                o_ref[s, slot, :, cols] = flat[pl.ds(first + s, rows, stride=slabs), :]


def relay(half, measured, sides, first_view, views, count, into=None, slot=0, slots=None, after=None, cost=SMALL):
    segs, _, inner, slabs, bins = measured.shape
    rows = segs * inner
    slots = len(sides) if slots is None else slots
    specs = [
        pl.BlockSpec((segs, 1, inner, slabs, LANES), lambda v, lane=lane: (0, first_view + v, 0, 0, lane))
        for lane in range(lane_blocks(bins))
    ]
    lanes = len(specs)
    operands = [half] + [measured] * lanes
    aliases = {}
    if into is not None:
        aliases = {len(operands): 0}
        operands.append(into)
    if after is not None:
        operands.append(after)
    specs = [SMEM] + specs + [pl.BlockSpec(memory_space=pl.ANY)] * (len(operands) - 1 - lanes)
    return pl.pallas_call(
        functools.partial(relay_kernel, sides, lanes),
        grid=(views,),
        in_specs=specs,
        out_specs=pl.BlockSpec((count, len(sides), rows, bins), lambda v: (0, v * slots // len(sides) + slot, 0, 0)),
        out_shape=jax.ShapeDtypeStruct((count, views * slots, rows, bins), f32),
        input_output_aliases=aliases,
        compiler_params=params(52),
        cost_estimate=cost,
    )(*operands)


def split_two(x):
    hi = x.astype(bf16)
    return hi, (x - hi.astype(f32)).astype(bf16)


def axial_entries(weight, slices, margin, segs, inner, row, column):
    place = jnp.where(
        column < slices, column + margin, jnp.where(column < slices + margin, column - slices, column)
    )
    group = (row // inner) % segs
    tap = place - (row // (inner * segs) * inner + row % inner)
    entries = jnp.zeros(row.shape, f32)
    for k in range(2 * margin + 1):
        value = jnp.full(row.shape, weight(0, k), f32)
        for g in range(1, segs):
            value = jnp.where(group == g, weight(g, k), value)
        entries = jnp.where(tap == k, value, entries)
    return entries


def setup_kernel(slices, segs, inner, halves, me_ref, k_ref, t_ref, c_ref, o_ref, op_ref, opt_ref):
    lanes, depth = t_ref.shape
    views = o_ref.shape[0]
    bins = c_ref.shape[-1]
    taps = k_ref.shape[1]
    margin = (taps - 1) // 2
    first_row = me_ref[0] % halves * segs
    turned = me_ref[0] >= halves

    def weight(g, k):
        return jnp.where(turned, k_ref[first_row + g, taps - 1 - k], k_ref[first_row + g, k])

    def ids(shape, dim):
        return lax.broadcasted_iota(jnp.int32, shape, dim)

    shape = op_ref.shape
    op_ref[...] = axial_entries(weight, slices, margin, segs, inner, ids(shape, 0), ids(shape, 1))
    _, ext, part = opt_ref.shape
    for h in range(2):
        opt_ref[h] = axial_entries(
            weight, slices, margin, segs, inner, ids((ext, part), 1) + h * part, ids((ext, part), 0)
        )

    table = t_ref[...].astype(f32)
    first = table.astype(bf16)
    rest = table - first.astype(f32)
    second = rest.astype(bf16)
    third = (rest - second.astype(f32)).astype(bf16)
    pieces = jnp.concatenate([first, second, third], axis=0)
    depth_ids = ids((depth, bins), 0)
    lane_ids = ids((lanes, bins), 0)

    def look(index):
        row = index // lanes
        hot = jnp.where(depth_ids == row, 1.0, 0.0).astype(bf16)
        got = jnp.dot(pieces, hot, preferred_element_type=f32)
        value = got[:lanes] + got[lanes : 2 * lanes] + got[2 * lanes :]
        return jnp.sum(jnp.where(lane_ids == index - row * lanes, value, 0.0), axis=0, keepdims=True)

    def one_view(v, carry):
        first_factor = 1.0 + dead_time_tau * look(c_ref[0, v])
        second_factor = 1.0 + dead_time_tau * look(c_ref[1, v])
        o_ref[v] = 1.0 / (first_factor * second_factor)
        return carry

    lax.fori_loop(0, views, one_view, 0)


def setup(me, kernel, dead_counts, crystals, slices, segs, inner, halves):
    _, views, bins = crystals.shape
    taps = kernel.shape[1]
    rows = slices * segs
    ext = slices + taps - 1 + 8
    table = dead_counts.reshape(-1, LANES).T
    return pl.pallas_call(
        functools.partial(setup_kernel, slices, segs, inner, halves),
        in_specs=[SMEM, SMEM, VMEM, VMEM],
        out_specs=[VMEM] * 3,
        out_shape=[
            jax.ShapeDtypeStruct((views, 1, bins), f32),
            jax.ShapeDtypeStruct((rows, ext), f32),
            jax.ShapeDtypeStruct((2, ext, rows // 2), f32),
        ],
        compiler_params=params(24),
        cost_estimate=SMALL,
    )(me, kernel, table, crystals.reshape(2, views, 1, bins))


def forward_kernel(op_ref, ext_ref, foot_hbm, eff_ref, _, *refs):
    lanes = (len(refs) - 4) // 2
    rand_refs, o_ref, foot_ref, rows_ref = refs[:lanes], refs[lanes], refs[lanes + 1], refs[lanes + 2]
    order_refs, sems = refs[lanes + 3 : -1], refs[-1]
    segs, _, slices, _ = rand_refs[0].shape
    pixels = ext_ref.shape[1]
    inner = 2
    count = slices // inner
    view = pl.program_id(0)

    def fetch(v):
        return pltpu.make_async_copy(foot_hbm.at[v], foot_ref.at[v], sems.at[v])

    @pl.when(view == 0)
    def _():
        for v in range(foot_ref.shape[0]):
            fetch(v).start()
        rows_ref[...] = jnp.dot(
            op_ref[...], ext_ref[...], preferred_element_type=f32, precision=lax.Precision.HIGHEST
        ).astype(bf16)

    fetch(view).wait()
    projected = jnp.dot(rows_ref[...], foot_ref[view], preferred_element_type=f32) * (1.0 / pixels)
    for lane in range(lanes):
        flat = rand_refs[lane].reshape(segs * slices, LANES)
        order_ref = order_refs[lane]
        for g in range(segs):
            for a in range(inner):
                got = flat[pl.ds(g * slices + a, count, stride=inner), :].astype(f32)
                order_ref[pl.ds(g * inner + a, count, stride=segs * inner), :] = 0.25 * (got + 1.0)
        cols = slice(lane * LANES, (lane + 1) * LANES)
        eff = eff_ref[0, :, cols]
        value = eff / (eff * projected[:, cols] + order_ref[...])
        o_ref[0, :, :, :, cols] = value.reshape(*o_ref.shape[1:4], LANES)


def forward(operator, extended, footprint, randoms, efficiency, after):
    segs, views, slices, bins = randoms.shape
    pixels = footprint.shape[1]
    rows = segs * slices
    inner = 2 * segs
    lanes = [
        pl.BlockSpec((segs, 1, slices, LANES), lambda v, lane=lane: (0, v, 0, lane))
        for lane in range(lane_blocks(bins))
    ]
    return pl.pallas_call(
        forward_kernel,
        grid=(views,),
        in_specs=[
            VMEM,
            VMEM,
            pl.BlockSpec(memory_space=pltpu.HBM),
            pl.BlockSpec((1, 1, bins), lambda v: (v, 0, 0)),
            pl.BlockSpec(memory_space=pl.ANY),
        ]
        + lanes,
        out_specs=pl.BlockSpec((1, 2, rows // inner // 2, inner, bins), lambda v: (v, 0, 0, 0, 0)),
        out_shape=jax.ShapeDtypeStruct((views, 2, rows // inner // 2, inner, bins), f32),
        scratch_shapes=[pltpu.VMEM(footprint.shape, footprint.dtype), pltpu.VMEM((rows, pixels), bf16)]
        + [pltpu.VMEM((rows, LANES), f32)] * len(lanes)
        + [pltpu.SemaphoreType.DMA((views,))],
        compiler_params=params(40),
        cost_estimate=SMALL,
    )(operator, extended, footprint, efficiency, after, *[randoms] * len(lanes))


def back_project(operator, weighted, foot):
    ext = operator.shape[0]
    hi, lo = split_two(operator)
    both = jnp.dot(jnp.concatenate([hi, lo], axis=0), weighted, preferred_element_type=f32)
    hi, lo = split_two(both[:ext] + both[ext:])
    spread = lax.dot_general(
        jnp.concatenate([hi, lo], axis=0), foot, (((1,), (1,)), ((), ())), preferred_element_type=f32
    )
    return spread[:ext] + spread[ext:]


def ratio(factor, rows_in):
    scaled = factor * rows_in
    return scaled.reshape(-1, scaled.shape[-1]).astype(bf16)


def start_all(copies):
    for copy in copies:
        copy.start()


def back_staged_kernel(
    edge, half_ref, op_ref, staged_hbm, part_ref, factor_hbm, foot_hbm, acc_ref, own_ref, factor_ref, foot_ref, sems
):
    half = half_ref[0]
    views, count, inner, bins = own_ref.shape
    firsts = factor_hbm.shape[0] - views

    def copies(v):
        return [
            pltpu.make_async_copy(staged_hbm.at[:, 2 * v], own_ref.at[v], sems.at[v, 0]),
            pltpu.make_async_copy(factor_hbm.at[firsts + v], factor_ref.at[v], sems.at[v, 1]),
            pltpu.make_async_copy(foot_hbm.at[firsts + v], foot_ref.at[v], sems.at[v, 2]),
        ]

    for v in range(views):
        start_all(copies(v))
    middles = (part_ref.shape[0] - 2 * edge * views) // (count - 2 * edge)
    operator = jnp.concatenate([op_ref[half], op_ref[1 - half]], axis=1)
    for v in range(views):
        for copy in copies(v):
            copy.wait()
        far = factor_ref[v, 1 - half]
        own = ratio(factor_ref[v, half], own_ref[v])
        low = ratio(far[:edge], part_ref[2 * edge * v : 2 * edge * v + edge])
        high = ratio(far[count - edge :], part_ref[2 * edge * v + edge : 2 * edge * (v + 1)])
        if v < middles:
            first = 2 * edge * views + (count - 2 * edge) * v
            middle = ratio(far[edge : count - edge], part_ref[first : first + count - 2 * edge])
        else:
            middle = jnp.zeros(((count - 2 * edge) * inner, bins), bf16)
        spread = back_project(operator, jnp.concatenate([own, low, middle, high], axis=0), foot_ref[v])
        if v == 0:
            acc_ref[...] = spread
        else:
            acc_ref[...] += spread


def back_staged(half, operator, staged, part, factor, footprint, edge):
    ext = operator.shape[1]
    count, slots, inner, bins = staged.shape
    views = slots // 2
    pixels = footprint.shape[1]
    return pl.pallas_call(
        functools.partial(back_staged_kernel, edge),
        in_specs=[SMEM, VMEM, HBM, VMEM, HBM, HBM],
        out_specs=VMEM,
        out_shape=jax.ShapeDtypeStruct((ext, pixels), f32),
        scratch_shapes=[
            pltpu.VMEM((views, count, inner, bins), f32),
            pltpu.VMEM((views, 2, count, inner, bins), f32),
            pltpu.VMEM((views, pixels, bins), bf16),
            pltpu.SemaphoreType.DMA((views, 3)),
        ],
        compiler_params=params(52),
        cost_estimate=LARGE,
    )(half, operator, staged, part, factor, footprint)


def back_near_kernel(
    half_ref, me_ref, op_ref, near_hbm, factor_hbm, foot_hbm, in_ref, acc_ref, keep_ref, give_ref, *scratch
):
    near_ref, factor_ref, foot_ref, sum_ref, sems = scratch
    half = half_ref[0]
    views = near_ref.shape[0]

    def copies(v):
        return [
            pltpu.make_async_copy(near_hbm.at[:, pl.ds(2 * v, 2)], near_ref.at[v], sems.at[v, 0]),
            pltpu.make_async_copy(factor_hbm.at[v], factor_ref.at[v], sems.at[v, 1]),
            pltpu.make_async_copy(foot_hbm.at[v], foot_ref.at[v], sems.at[v, 2]),
        ]

    for v in range(views):
        start_all(copies(v))
    operator = jnp.concatenate([op_ref[half], op_ref[1 - half]], axis=1)
    sum_ref[...] = in_ref[...]
    for v in range(views):
        for copy in copies(v):
            copy.wait()
        own = ratio(factor_ref[v, half], near_ref[v, :, 0])
        far = ratio(factor_ref[v, 1 - half], near_ref[v, :, 1])
        sum_ref[...] += back_project(operator, jnp.concatenate([own, far], axis=0), foot_ref[v])
    slices, pixels = acc_ref.shape
    margin, width = keep_ref.shape[2:]
    acc_ref[...] = sum_ref[:slices]
    core = me_ref[0] % 2
    for k in range(4):
        for c in range(2):
            block = me_ref[0] ^ (2 * k + c)
            cols = pl.ds(pl.multiple_of(block * width, width), width)
            pair = sum_ref[slices : slices + 2 * margin, cols] * (1.0 / pixels)
            up, down = pair[:margin], pair[margin:]
            keep_ref[c, k] = jnp.where(core == 0, down, up)
            give_ref[c, k] = jnp.where(core == 0, up, down)


def back_near(half, me, operator, near, factor, footprint, acc, slices, margin):
    count, slots, inner, bins = near.shape
    views = slots // 2
    pixels = footprint.shape[1]
    halo = jax.ShapeDtypeStruct((2, 4, margin, pixels // 8), f32)
    return pl.pallas_call(
        back_near_kernel,
        in_specs=[SMEM, SMEM, VMEM, HBM, HBM, HBM, VMEM],
        out_specs=[VMEM] * 3,
        out_shape=[jax.ShapeDtypeStruct((slices, pixels), f32), halo, halo],
        scratch_shapes=[
            pltpu.VMEM((views, count, 2, inner, bins), f32),
            pltpu.VMEM((views, 2, count, inner, bins), f32),
            pltpu.VMEM((views, pixels, bins), bf16),
            pltpu.VMEM(acc.shape, f32),
            pltpu.SemaphoreType.DMA((views, 3)),
        ],
        compiler_params=params(52),
        cost_estimate=SMALL,
    )(half, me, operator, near, factor, footprint, acc)


def pieces_kernel(edge, views, staged_hbm, part_ref, last_ref, sems):
    count = staged_hbm.shape[0]
    middle = count - 2 * edge
    copies = []

    def add(slices, v, target):
        copies.append(pltpu.make_async_copy(staged_hbm.at[slices, 2 * v + 1], target, sems.at[len(copies)]))

    lasts = last_ref.shape[1]
    for v in range(views):
        add(pl.ds(0, edge), v, part_ref.at[pl.ds(2 * edge * v, edge)])
        add(pl.ds(count - edge, edge), v, part_ref.at[pl.ds(2 * edge * v + edge, edge)])
        if v < views - lasts:
            add(pl.ds(edge, middle), v, part_ref.at[pl.ds(2 * edge * views + middle * v, middle)])
        else:
            add(pl.ds(edge, middle), v, last_ref.at[:, v - views + lasts])
    start_all(copies)
    for copy in copies:
        copy.wait()


def pieces(staged, edge, lasts):
    count, slots, inner, bins = staged.shape
    views = slots // 2
    middle = count - 2 * edge
    part = 2 * edge * views + middle * (views - lasts)
    return pl.pallas_call(
        functools.partial(pieces_kernel, edge, views),
        in_specs=[HBM],
        out_specs=[VMEM] * 2,
        out_shape=[
            pltpu.VMEM((part, inner, bins), f32),
            pltpu.VMEM((middle, lasts, inner, bins), f32),
        ],
        scratch_shapes=[pltpu.SemaphoreType.DMA((3 * views,))],
        compiler_params=params(16),
        cost_estimate=SMALL,
    )(staged)


def mark_kernel(x_ref, o_ref):
    o_ref[...] = jnp.zeros_like(o_ref)


def mark(x):
    return pl.pallas_call(
        mark_kernel,
        in_specs=[pl.BlockSpec(memory_space=pl.ANY)],
        out_specs=VMEM,
        out_shape=jax.ShapeDtypeStruct((8, LANES), f32),
        compiler_params=params(16),
        cost_estimate=LARGE,
    )(x)


def back_last_kernel(half_ref, me_ref, op_ref, x_ref, factor_ref, foot_ref, in_ref, *refs):
    mine_refs, other_ref, acc_ref = refs[:4], refs[4], refs[5]
    slices, pixels = acc_ref.shape
    middle, views, inner, bins = x_ref.shape
    count = factor_ref.shape[2]
    edge = (count - middle) // 2
    far = 1 - half_ref[0]
    gap = jnp.zeros((edge * inner, bins), bf16)
    operator = op_ref[far, :slices]
    acc_ref[...] = in_ref[...]
    for v in range(views):
        weighted = ratio(factor_ref[v, far, edge : count - edge], x_ref[:, v])
        acc_ref[...] += back_project(operator, jnp.concatenate([gap, weighted, gap], axis=0), foot_ref[v])
    width = mine_refs[0].shape[1]
    for k in range(4):
        for c in range(2):
            block = me_ref[0] ^ (2 * k + c)
            part = acc_ref[:, pl.ds(pl.multiple_of(block * width, width), width)] * (1.0 / pixels)
            if c == 0:
                mine_refs[k][...] = part
            else:
                other_ref[k] = part


def back_last(half, me, operator, rows_in, factor, footprint, acc):
    slices, pixels = acc.shape
    width = pixels // 8
    return pl.pallas_call(
        back_last_kernel,
        in_specs=[SMEM, SMEM] + [VMEM] * 5,
        out_specs=[VMEM] * 5,
        out_shape=[pltpu.VMEM((slices, width), f32)] * 4 + [pltpu.VMEM((4, slices, width), f32)],
        scratch_shapes=[pltpu.VMEM((slices, pixels), f32)],
        compiler_params=params(24),
        cost_estimate=SMALL,
    )(half, me, operator, rows_in, factor, footprint, acc)


def pair_kernel(me_ref, *refs):
    mine_refs, theirs_ref, halo_ref, across_ref, out_refs = refs[:4], refs[4], refs[5], refs[6], refs[7:]
    core = me_ref[0] % 2
    slices, _ = mine_refs[0].shape
    margin = halo_ref.shape[2]
    for k in range(4):
        here, there = halo_ref[0, k], across_ref[k]
        above = jnp.where(core == 0, here, there)
        below = jnp.where(core == 0, there, here)
        out_refs[k][...] = mine_refs[k][...] + theirs_ref[k]
        out_refs[k][:margin] += above
        out_refs[k][slices - margin :] += below


def pair_sum(me, mine, theirs, halo, across):
    return pl.pallas_call(
        pair_kernel,
        in_specs=[SMEM] + [VMEM] * 7,
        out_specs=[VMEM] * 4,
        out_shape=[pltpu.VMEM(x.shape, f32) for x in mine],
        compiler_params=params(16),
        cost_estimate=SMALL,
    )(me, *mine, theirs, halo, across)


def assemble_kernel(me_ref, *refs):
    near_refs, far_ref, o_ref = refs[:4], refs[4], refs[5]
    width = near_refs[0].shape[1]
    for k in range(4):
        for c in range(2):
            block = me_ref[0] ^ (2 * k + c)
            part = near_refs[k][...] if c == 0 else far_ref[k]
            o_ref[:, pl.ds(pl.multiple_of(block * width, width), width)] = part


def assemble(me, near, far):
    slices, width = near[0].shape
    return pl.pallas_call(
        assemble_kernel,
        in_specs=[SMEM] + [VMEM] * 5,
        out_specs=VMEM,
        out_shape=jax.ShapeDtypeStruct((slices, width * 8), f32),
        compiler_params=params(16),
    )(me, *near, far)


def local(activity, measured, randoms, footprint, kernel, dead_counts, crystals, sensitivity):
    segs, views, inner, slabs, bins = measured.shape
    slices, pixels = activity.shape
    taps = kernel.shape[1]
    margin = (taps - 1) // 2
    width = pixels // 8
    group = lax.axis_index("seg")
    me = group.astype(jnp.int32).reshape(1)
    halves = lax.axis_size("seg") // 2

    def swap(x, k):
        return lax.ppermute(x, "seg", [(i, i ^ k) for i in range(2 * halves)])

    def outward(x):
        pairs = []
        for j in range(2 * halves):
            for i in range(slabs - 1):
                source, target = (i, i + 1) if j % 2 == 0 else (i + 1, i)
                pairs.append((j * slabs + source, j * slabs + target))
        return lax.ppermute(x, ("seg", "slab"), pairs)

    count = slabs // 2
    half = (lax.axis_index("slab").astype(jnp.int32) // count).reshape(1)
    edge = margin // inner
    firsts = views // 2
    lasts = 2

    def cross(x):
        return lax.ppermute(x, "slab", [(i, (i + count) % slabs) for i in range(slabs)])

    def exchange(x):
        groups = [[h * count + i for i in range(count)] for h in range(2)]
        return lax.all_to_all(x, "slab", split_axis=0, concat_axis=0, tiled=True, axis_index_groups=groups)

    ext = slices + 2 * margin
    early = lax.dynamic_slice_in_dim(measured[:, :firsts], (1 - half[0]) * count, count, 3)
    early = cross(early)
    staged = relay(half, measured, (0, 1), firsts, views - firsts, count)
    staged, near_activity = lax.optimization_barrier((staged, activity))
    staged = exchange(staged)
    near = relay(half, measured, (0,), 0, firsts, count, slots=2, cost=SMALL)
    efficiency, operator, operator_t = setup(me, kernel, dead_counts, crystals, slices, segs, inner, halves)
    even = group % 2 == 0
    halo = outward(jnp.where(even, near_activity[slices - margin :], near_activity[:margin]))
    across = swap(halo, 1)
    extended = jnp.concatenate(
        [
            activity,
            jnp.where(even, halo, across),
            jnp.where(even, across, halo),
            jnp.zeros((8, pixels), f32),
        ],
        axis=0,
    )

    staged, near, begun = lax.optimization_barrier((staged, near, mark(early)))
    part, rows_last = pieces(staged, edge, lasts)
    part = cross(part)
    near = relay(half, early, (1,), 0, firsts, count, into=near, slot=1, slots=2, after=begun)
    rows_last, near = lax.optimization_barrier((rows_last, near))
    rows_last = cross(rows_last)
    near = exchange(near)
    factor = forward(operator, extended, footprint, randoms, efficiency, begun)

    last_factor, last_foot = factor[views - lasts :], footprint[views - lasts :]
    acc = back_staged(half, operator_t, staged, part, factor, footprint, edge)
    acc, last_factor, last_foot = lax.optimization_barrier((acc, last_factor, last_foot))
    acc, keep, give = back_near(half, me, operator_t, near, factor, footprint, acc, slices, margin)
    halo = outward(keep + swap(give, 1)[::-1])
    across = swap(halo[1], 1)
    *mine, other = back_last(half, me, operator_t, rows_last, last_factor, last_foot, acc)
    pair = pair_sum(me, mine, swap(other, 1), halo, across)
    total = pair[0]
    for k in range(1, 4):
        total = total + swap(pair[k], 2 * k)
    start = group * width
    gain = lax.dynamic_slice_in_dim(activity, start, width, 1) / lax.dynamic_slice_in_dim(
        sensitivity, start, width, 1
    )
    block = total * gain
    near = [block] + [swap(block, 2 * k) for k in range(1, 4)]
    far = swap(jnp.stack(near), 1)
    return assemble(me, near, far)


def solution(mesh):
    placed = (
        P("slab", None),
        P("seg", None, "slab", None, None),
        P("seg", None, "slab", None),
        P(),
        P(),
        P(),
        P(),
        P("slab", None),
    )
    return jax.shard_map(
        local, mesh=mesh, in_specs=placed, out_specs=P("slab", None), check_vma=False
    )
```

time: 171 us -> 134 us (0.78)
  the two profiles are of different devices: /device:TPU:31 before, /device:TPU:129 now
where the time goes in v2:
time: 134 us; the launch traced here: 133 us
  starting transfers between devices  62 us (46%)
  Pallas kernels  38.3 us (29%)
  waiting for transfers between devices  18 us (13%)
  local copies, waits for them, and re-layouts  10.9 us (8%)
  other arithmetic  3.55 us (3%)
    ppermute x11, starting transfers between devices, swap(): return lax.ppermute(x, 'seg', [(i, i ^ k) for i in range(2 * halves)])  29.4 us
    ppermute x2, starting transfers between devices, outward(): return lax.ppermute(x, ('seg', 'slab'), pairs)  18 us
    ppermute x11, waiting for transfers between devices, swap(): return lax.ppermute(x, 'seg', [(i, i ^ k) for i in range(2 * halves)])  13.1 us
    all_to_all x2, starting transfers between devices, exchange(): lax.all_to_all(x, 'slab', split_axis=0, concat_axis=0, tiled=True, axis_i...  9.1 us
    pallas_call x3, Pallas kernels, relay(): pl.pallas_call(functools.partial(relay_kernel, sides, lanes), grid=(views...  8.46 us
    pallas_call x1, Pallas kernels, forward(): pl.pallas_call(forward_kernel, grid=(views,), in_specs=[VMEM, VMEM, pl.Bl...  8.08 us
    pallas_call x1, Pallas kernels, setup(): pl.pallas_call(functools.partial(setup_kernel, slices, segs, inner, halve...  5.97 us
    pallas_call x1, Pallas kernels, back_staged(): pl.pallas_call(functools.partial(back_staged_kernel, edge), in_specs=[SME...  5.59 us
  transfers between devices with their start and end apart: 18, of which 7 were waited for; matrix products, arithmetic and copies ran while one was open for 5% of the time, Pallas kernels for 28%

profile of v2, /device:TPU:129, one launch (start us, length us, event | category | flops | bytes accessed | tf_op | source)
XLA Modules:
  0.0 133.1 jit_solution(4699229107378325227)
XLA Ops:
  0.0 1.4 %slice-done = f32[4,4,2,32,384]{4,3,2,1,0:T(8,128)S(1)} async-done(((f32[4,8,2,32,384]{4,3,2,1,0:T(8,128)}), f32[4,4,2,32,384]{4,3,2,1,0:T(8,128)S(1)}, s32[]{:S(2)}) %slice-start) | async-done | bytes 1572888 | tf_op jit(solution)/shard_map/slice | solution.py:538
  1.4 1.0 constant_dynamic-slice_fusion
  2.4 4.1 %shard_map.83 = f32[16,8,8,384]{3,2,1,0:T(8,128)} custom-call(s32[1]{0:T(128)} %bitcast.1.half_ref, f32[4,8,2,32,384]{4,3,2,1,0:T(8,128)} %refs_2_.4, f32[4,8,2,32,384]{4,3,2,1,0:T(8,128)} %refs_2_.4, f32[4,8,2,32,384]{4,3,2,1,0:T(8,128)} %refs_2_.4), custom_call_target="tpu_custom_call" | custom-call | flops 1 | bytes 1 | tf_op jit(solution)/shard_map/pallas_call | solution.py:59
  7.4 11.9 %collective-permute-start.3 = (f32[4,2048]{1,0:T(4,128)S(1)}, f32[4,2048]{1,0:T(4,128)}, u32[]{:S(2)}, u32[]{:S(2)}) collective-permute-start(f32[4,2048]{1,0:T(4,128)S(1)} %slice_select_fusion), channel_id=1, source_target_pairs={{0,1},{1,2},{2,3},{3,4},{4,5},{5,6},{6,7},{7,8},{8,9},{9,10},{10,1... | collective-permute-start | bytes 98312 | tf_op jit(solution)/shard_map/ppermute | solution.py:522
  19.3 4.4 %all-to-all-start = ((f32[16,8,8,384]{3,2,1,0:T(8,128)}), f32[16,8,8,384]{3,2,1,0:T(8,128)}, u32[]{:S(2)}, u32[]{:S(2)}) async-start(f32[16,8,8,384]{3,2,1,0:T(8,128)} %shard_map.83), calls=%async_computation | async-start | bytes 3145728 | tf_op jit(solution)/shard_map/all_to_all | solution.py:535
  23.8 2.6 %shard_map.84.refs_3_ = f32[16,8,8,384]{3,2,1,0:T(8,128)S(1)} custom-call(s32[1]{0:T(128)} %bitcast.1.half_ref, f32[4,8,2,32,384]{4,3,2,1,0:T(8,128)} %refs_2_.4, f32[4,8,2,32,384]{4,3,2,1,0:T(8,128)} %refs_2_.4, f32[4,8,2,32,384]{4,3,2,1,0:T(8,128)} %refs_2_.4), custom_call_target="tpu_custom_call" | custom-call | flops 1 | bytes 1 | tf_op jit(solution)/shard_map/pallas_call | solution.py:59
  26.5 1.2 copy-done.2
  27.8 6.0 %shard_map.82 = (f32[8,1,384]{2,1,0:T(1,128)S(1)}, f32[256,80]{1,0:T(8,128)S(1)}, f32[2,80,128]{2,1,0:T(8,128)S(1)}) custom-call(s32[1]{0:T(128)} %bitcast.me_ref, f32[16,9]{1,0:T(8,128)S(1)} %copy-done.5, s32[128,512]{1,0:T(8,128)S(1)} %bitcast.10, s32[2,8,1,384]{3,2,1,0:T(1,128)S(1)} %reshape.15.c_ref), custom_call_target="tpu_custom_call" | custom-call | flops 1 | bytes 1 | tf_op jit(solution)/shard_map/pallas_call | solution.py:145
  33.8 3.8 %slice.22.foot_ref = bf16[2,2048,384]{2,1,0:T(8,128)(2,1)} slice(bf16[8,2048,384]{2,1,0:T(8,128)(2,1)} %foot_hbm.5), slice={[6:8], [0:2048], [0:384]} | slice | bytes 6291456 | tf_op jit(solution)/shard_map/slice | solution.py:567
  38.2 9.6 %collective-permute-start.4 = (f32[4,2048]{1,0:T(4,128)}, f32[4,2048]{1,0:T(4,128)}, u32[]{:S(2)}, u32[]{:S(2)}) collective-permute-start(f32[4,2048]{1,0:T(4,128)} %collective-permute-done.3), channel_id=1, source_target_pairs={{0,32},{32,0},{64,96},{96,64},{128,160},{160,128},{192,224},{224,1... | collective-permute-start | bytes 98312 | tf_op jit(solution)/shard_map/ppermute | solution.py:514
  47.9 2.2 %shard_map.86 = (f32[40,8,384]{2,1,0:T(8,128)}, f32[12,2,8,384]{3,2,1,0:T(8,128)S(1)}) custom-call(f32[16,8,8,384]{3,2,1,0:T(8,128)} %all-to-all-done.staged_hbm), custom_call_target="tpu_custom_call" | custom-call | flops 1 | bytes 1 | tf_op jit(solution)/shard_map/pallas_call | solution.py:390
  52.0 1.7 %shard_map.87 = f32[16,8,8,384]{3,2,1,0:T(8,128)} custom-call(s32[1]{0:T(128)} %bitcast.1.half_ref, f32[4,4,2,16,384]{4,3,2,1,0:T(8,128)S(1)} %collective-permute-done.x_ref.refs_0_.refs_1_.refs_2_, f32[4,4,2,16,384]{4,3,2,1,0:T(8,128)S(1)} %collective-permute-done.x_ref.refs_0_.refs_1_.refs_2_, ...), custom_call_target="tpu_custom_call", output_to_operand_aliasing={{}: (4, {})} | custom-call | flops 1 | bytes 1 | tf_op jit(solution)/shard_map/pallas_call | solution.py:59
  53.7 4.7 %all-to-all-start.1 = ((f32[16,8,8,384]{3,2,1,0:T(8,128)}), f32[16,8,8,384]{3,2,1,0:T(8,128)}, u32[]{:S(2)}, u32[]{:S(2)}) async-start(f32[16,8,8,384]{3,2,1,0:T(8,128)} %shard_map.87), calls=%async_computation.1 | async-start | bytes 3145728 | tf_op jit(solution)/shard_map/all_to_all | solution.py:535
  58.3 5.4 %collective-permute-start.1 = (f32[12,2,8,384]{3,2,1,0:T(8,128)}, f32[12,2,8,384]{3,2,1,0:T(8,128)}, u32[]{:S(2)}, u32[]{:S(2)}) collective-permute-start(f32[12,2,8,384]{3,2,1,0:T(8,128)} %copy-done.6), channel_id=1, source_target_pairs={{0,16},{1,17},{2,18},{3,19},{4,20},{5,21},{6,22},{7,23},{8,24},{9,... | collective-permute-start | bytes 884744 | tf_op jit(solution)/shard_map/ppermute | solution.py:531
  63.8 1.1 copy-done.4
  64.9 8.1 %shard_map.88.factor_hbm = f32[8,2,16,8,384]{4,3,2,1,0:T(8,128)S(1)} custom-call(f32[256,80]{1,0:T(8,128)S(1)} %get-tuple-element.40.op_ref, f32[80,2048]{1,0:T(8,128)S(1)} %copy-done.4, bf16[8,2048,384]{2,1,0:T(8,128)(2,1)} %foot_hbm.5, f32[8,1,384]{2,1,0:T(1,128)S(1)} %get-tuple-element.42.eff_ref, f32[8,128]{1,0:T(8,128)S(1)} %shard_map.85.refs_4_._, ...), custom_call_target="tpu_custom_call" | custom-call | flops 1 | bytes 1 | tf_op jit(solution)/shard_map/pallas_call | solution.py:204
  73.0 1.6 %copy-done.1 = f32[8,2,16,8,384]{4,3,2,1,0:T(8,128)} copy-done((f32[8,2,16,8,384]{4,3,2,1,0:T(8,128)}, f32[8,2,16,8,384]{4,3,2,1,0:T(8,128)S(1)}, u32[]{:S(2)}) %copy-start.1) | copy-done | bytes 3145752
  74.6 5.6 %shard_map.89.in_ref = f32[80,2048]{1,0:T(8,128)S(1)} custom-call(s32[1]{0:T(128)} %bitcast.1.half_ref, f32[2,80,128]{2,1,0:T(8,128)S(1)} %get-tuple-element.32.op_ref, f32[16,8,8,384]{3,2,1,0:T(8,128)} %all-to-all-done.staged_hbm, f32[40,8,384]{2,1,0:T(8,128)} %collective-permute-done.2.part_ref, f32[8,2,16,8,384]{4,3,2,1,0:T(8,128)} %copy-done.1, ...), custom_call_target="tpu_custom_call" | custom-call | flops 999999995904 | bytes 1048576 | tf_op jit(solution)/shard_map/pallas_call | solution.py:288
  80.2 4.8 %all-to-all-done.1.near_hbm = f32[16,8,8,384]{3,2,1,0:T(8,128)} async-done(((f32[16,8,8,384]{3,2,1,0:T(8,128)}), f32[16,8,8,384]{3,2,1,0:T(8,128)}, u32[]{:S(2)}, u32[]{:S(2)}) %all-to-all-start.1) | async-done | bytes 1572896 | tf_op jit(solution)/shard_map/all_to_all | solution.py:535
  85.1 4.8 %shard_map.90 = (f32[64,2048]{1,0:T(8,128)S(1)}, f32[2,4,4,256]{3,2,1,0:T(4,128)S(1)}, f32[2,4,4,256]{3,2,1,0:T(4,128)S(1)}) custom-call(s32[1]{0:T(128)} %bitcast.1.half_ref, s32[1]{0:T(128)} %bitcast.me_ref, f32[2,80,128]{2,1,0:T(8,128)S(1)} %get-tuple-element.32.op_ref, f32[16,8,8,384]{3,2,1,0:T(8,128)} %all-to-all-done.1.near_hbm, ...), custom_call_target="tpu_custom_call" | custom-call | flops 1 | bytes 1 | tf_op jit(solution)/shard_map/pallas_call | solution.py:347
  91.7 6.1 %collective-permute-start.7 = (f32[2,4,4,256]{3,2,1,0:T(4,128)S(1)}, f32[2,4,4,256]{3,2,1,0:T(4,128)S(1)}, u32[]{:S(2)}, u32[]{:S(2)}) collective-permute-start(f32[2,4,4,256]{3,2,1,0:T(4,128)S(1)} %reverse_add_fusion), channel_id=1, source_target_pairs={{0,1},{1,2},{2,3},{3,4},{4,5},{5,6},{6,7},{7,8},{8,9},{9,10},{10,1... | collective-permute-start | bytes 98312 | tf_op jit(solution)/shard_map/ppermute | solution.py:522
  97.8 2.3 %shard_map.91 = (f32[64,256]{1,0:T(8,128)S(1)}, f32[64,256]{1,0:T(8,128)S(1)}, f32[64,256]{1,0:T(8,128)S(1)}, f32[64,256]{1,0:T(8,128)S(1)}, f32[4,64,256]{2,1,0:T(8,128)S(1)}) custom-call(s32[1]{0:T(128)} %bitcast.1.half_ref, s32[1]{0:T(128)} %bitcast.me_ref, f32[2,80,128]{2,1,0:T(8,128)S(1)} %get-tuple-element.32.op_ref, ...), custom_call_target="tpu_custom_call" | custom-call | flops 1 | bytes 1 | tf_op jit(solution)/shard_map/pallas_call | solution.py:446
  100.4 5.6 %collective-permute-start.8 = (f32[4,4,256]{2,1,0:T(4,128)S(1)}, f32[4,4,256]{2,1,0:T(4,128)S(1)}, u32[]{:S(2)}, u32[]{:S(2)}) collective-permute-start(f32[4,4,256]{2,1,0:T(4,128)S(1)} %slice_bitcast_fusion), channel_id=1, source_target_pairs={{0,32},{32,0},{64,96},{96,64},{128,160},{160,128},{192,224},{224,1... | collective-permute-start | bytes 49160 | tf_op jit(solution)/shard_map/ppermute | solution.py:514
  106.9 5.7 %collective-permute-start.9 = (f32[64,256]{1,0:T(8,128)S(1)}, f32[64,256]{1,0:T(8,128)S(1)}, u32[]{:S(2)}, u32[]{:S(2)}) collective-permute-start(f32[64,256]{1,0:T(8,128)S(1)} %get-tuple-element.56), channel_id=1, source_target_pairs={{0,64},{32,96},{64,0},{96,32},{128,192},{160,224},{192,128},{224,1... | collective-permute-start | bytes 196616 | tf_op jit(solution)/shard_map/ppermute | solution.py:514
  113.1 1.6 %collective-permute-start.11 = (f32[64,256]{1,0:T(8,128)S(1)}, f32[64,256]{1,0:T(8,128)S(1)}, u32[]{:S(2)}, u32[]{:S(2)}) collective-permute-start(f32[64,256]{1,0:T(8,128)S(1)} %get-tuple-element.58), channel_id=1, source_target_pairs={{0,192},{32,224},{64,128},{96,160},{128,64},{160,96},{192,0},{224,... | collective-permute-start | bytes 196616 | tf_op jit(solution)/shard_map/ppermute | solution.py:514
  114.7 5.1 %collective-permute-done.10 = f32[64,256]{1,0:T(8,128)S(1)} collective-permute-done((f32[64,256]{1,0:T(8,128)S(1)}, f32[64,256]{1,0:T(8,128)S(1)}, u32[]{:S(2)}, u32[]{:S(2)}) %collective-permute-start.10) | collective-permute-done | bytes 65568 | tf_op jit(solution)/shard_map/ppermute | solution.py:514
  120.7 1.7 %collective-permute-start.14 = (f32[64,256]{1,0:T(8,128)S(1)}, f32[64,256]{1,0:T(8,128)S(1)}, u32[]{:S(2)}, u32[]{:S(2)}) collective-permute-start(f32[64,256]{1,0:T(8,128)S(1)} %divide_multiply_fusion.refs_0_), channel_id=1, source_target_pairs={{0,192},{32,224},{64,128},{96,160},{128,64},{160,96},{192,0},{224,... | collective-permute-start | bytes 196616 | tf_op jit(solution)/shard_map/ppermute | solution.py:514
  122.4 1.3 collective-permute-start.13
  124.4 1.5 %collective-permute-done.14.refs_3_ = f32[64,256]{1,0:T(8,128)S(1)} collective-permute-done((f32[64,256]{1,0:T(8,128)S(1)}, f32[64,256]{1,0:T(8,128)S(1)}, u32[]{:S(2)}, u32[]{:S(2)}) %collective-permute-start.14) | collective-permute-done | bytes 65568 | tf_op jit(solution)/shard_map/ppermute | solution.py:514
  125.9 3.7 %collective-permute-done.13.refs_2_ = f32[64,256]{1,0:T(8,128)S(1)} collective-permute-done((f32[64,256]{1,0:T(8,128)S(1)}, f32[64,256]{1,0:T(8,128)S(1)}, u32[]{:S(2)}, u32[]{:S(2)}) %collective-permute-start.13) | collective-permute-done | bytes 65568 | tf_op jit(solution)/shard_map/ppermute | solution.py:514
  129.6 1.5 %collective-permute-start.15 = (f32[4,64,256]{2,1,0:T(8,128)S(1)}, f32[4,64,256]{2,1,0:T(8,128)S(1)}, u32[]{:S(2)}, u32[]{:S(2)}) collective-permute-start(f32[4,64,256]{2,1,0:T(8,128)S(1)} %pad_maximum_fusion), channel_id=1, source_target_pairs={{0,32},{32,0},{64,96},{96,64},{128,160},{160,128},{192,224},{224,1... | collective-permute-start | bytes 786440 | tf_op jit(solution)/shard_map/ppermute | solution.py:514
  131.1 1.2 collective-permute-done.15.refs_4_
  (54 shorter events, 9.5 us)
Async XLA Ops:
  0.0 1.4 %slice-start = ((f32[4,8,2,32,384]{4,3,2,1,0:T(8,128)}), f32[4,4,2,32,384]{4,3,2,1,0:T(8,128)S(1)}, s32[]{:S(2)}) async-start(f32[4,8,2,32,384]{4,3,2,1,0:T(8,128)} %refs_2_.4), calls=%async_computation.2 | async-start | bytes 3145728 | tf_op jit(solution)/shard_map/slice | solution.py:538
  2.4 45.5 %collective-permute-start = (f32[4,4,2,16,384]{4,3,2,1,0:T(8,128)}, f32[4,4,2,16,384]{4,3,2,1,0:T(8,128)S(1)}, u32[]{:S(2)}, u32[]{:S(2)}) collective-permute-start(f32[4,4,2,16,384]{4,3,2,1,0:T(8,128)} %constant_dynamic-slice_fusion), channel_id=1, source_target_pairs={{0,16},{1,17},{2,18},{3,19},{4,20},{5,21},{6,22},{7,23},{8,24},{9,... | collective-permute-start | bytes 2359304 | tf_op jit(solution)/shard_map/ppermute | solution.py:531
  7.4 30.8 %collective-permute-start.3 = (f32[4,2048]{1,0:T(4,128)S(1)}, f32[4,2048]{1,0:T(4,128)}, u32[]{:S(2)}, u32[]{:S(2)}) collective-permute-start(f32[4,2048]{1,0:T(4,128)S(1)} %slice_select_fusion), channel_id=1, source_target_pairs={{0,1},{1,2},{2,3},{3,4},{4,5},{5,6},{6,7},{7,8},{8,9},{9,10},{10,1... | collective-permute-start | bytes 98312 | tf_op jit(solution)/shard_map/ppermute | solution.py:522
  19.3 28.6 %all-to-all-start = ((f32[16,8,8,384]{3,2,1,0:T(8,128)}), f32[16,8,8,384]{3,2,1,0:T(8,128)}, u32[]{:S(2)}, u32[]{:S(2)}) async-start(f32[16,8,8,384]{3,2,1,0:T(8,128)} %shard_map.83), calls=%async_computation | async-start | bytes 3145728 | tf_op jit(solution)/shard_map/all_to_all | solution.py:535
  23.8 3.9 %copy-start.9 = (s32[2,8,384]{2,1,0:T(8,128)S(1)}, s32[2,8,384]{2,1,0:T(8,128)}, u32[]{:S(2)}) copy-start(s32[2,8,384]{2,1,0:T(8,128)} %param.14) | copy-start | bytes 73732
  23.8 3.9 %copy-start.8 = (s32[65536]{0:T(1024)S(1)}, s32[65536]{0:T(1024)}, u32[]{:S(2)}) copy-start(s32[65536]{0:T(1024)} %param.13) | copy-start | bytes 786436
  23.8 4.1 %copy-start.5 = (f32[16,9]{1,0:T(8,128)S(1)}, f32[16,9]{1,0:T(8,128)}, u32[]{:S(2)}) copy-start(f32[16,9]{1,0:T(8,128)} %k_ref.1) | copy-start | bytes 1732
  26.4 1.2 copy-start.2
  38.2 11.9 %collective-permute-start.4 = (f32[4,2048]{1,0:T(4,128)}, f32[4,2048]{1,0:T(4,128)}, u32[]{:S(2)}, u32[]{:S(2)}) collective-permute-start(f32[4,2048]{1,0:T(4,128)} %collective-permute-done.3), channel_id=1, source_target_pairs={{0,32},{32,0},{64,96},{96,64},{128,160},{160,128},{192,224},{224,1... | collective-permute-start | bytes 98312 | tf_op jit(solution)/shard_map/ppermute | solution.py:514
  47.9 3.1 %copy-start.7 = (f32[64,2048]{1,0:T(8,128)S(1)}, f32[64,2048]{1,0:T(8,128)}, u32[]{:S(2)}) copy-start(f32[64,2048]{1,0:T(8,128)} %param.8) | copy-start | bytes 1572868
  47.9 3.1 %copy-start.10 = (f32[80]{0:T(128)S(1)}, f32[80]{0:T(128)}, u32[]{:S(2)}) copy-start(f32[80]{0:T(128)} %pad.7.clone) | copy-start | bytes 964
  50.1 3.6 %copy-start.6 = (f32[12,2,8,384]{3,2,1,0:T(8,128)}, f32[12,2,8,384]{3,2,1,0:T(8,128)S(1)}, u32[]{:S(2)}) copy-start(f32[12,2,8,384]{3,2,1,0:T(8,128)S(1)} %get-tuple-element.38) | copy-start | bytes 884740
  50.1 22.9 %collective-permute-start.2 = (f32[40,8,384]{2,1,0:T(8,128)}, f32[40,8,384]{2,1,0:T(8,128)}, u32[]{:S(2)}, u32[]{:S(2)}) collective-permute-start(f32[40,8,384]{2,1,0:T(8,128)} %get-tuple-element.39), channel_id=1, source_target_pairs={{0,16},{1,17},{2,18},{3,19},{4,20},{5,21},{6,22},{7,23},{8,24},{9,... | collective-permute-start | bytes 1474568 | tf_op jit(solution)/shard_map/ppermute | solution.py:531
  53.7 10.1 %copy-start = (s32[4,8,64,384]{3,2,1,0:T(8,128)S(1)}, s32[4,8,64,384]{3,2,1,0:T(8,128)}, u32[]{:S(2)}) copy-start(s32[4,8,64,384]{3,2,1,0:T(8,128)} %refs_2_.5) | copy-start | bytes 9437188
  53.7 31.4 %all-to-all-start.1 = ((f32[16,8,8,384]{3,2,1,0:T(8,128)}), f32[16,8,8,384]{3,2,1,0:T(8,128)}, u32[]{:S(2)}, u32[]{:S(2)}) async-start(f32[16,8,8,384]{3,2,1,0:T(8,128)} %shard_map.87), calls=%async_computation.1 | async-start | bytes 3145728 | tf_op jit(solution)/shard_map/all_to_all | solution.py:535
  58.3 39.4 %collective-permute-start.1 = (f32[12,2,8,384]{3,2,1,0:T(8,128)}, f32[12,2,8,384]{3,2,1,0:T(8,128)}, u32[]{:S(2)}, u32[]{:S(2)}) collective-permute-start(f32[12,2,8,384]{3,2,1,0:T(8,128)} %copy-done.6), channel_id=1, source_target_pairs={{0,16},{1,17},{2,18},{3,19},{4,20},{5,21},{6,22},{7,23},{8,24},{9,... | collective-permute-start | bytes 884744 | tf_op jit(solution)/shard_map/ppermute | solution.py:531
  63.8 1.1 copy-start.4
  73.0 1.7 %copy-start.1 = (f32[8,2,16,8,384]{4,3,2,1,0:T(8,128)}, f32[8,2,16,8,384]{4,3,2,1,0:T(8,128)S(1)}, u32[]{:S(2)}) copy-start(f32[8,2,16,8,384]{4,3,2,1,0:T(8,128)S(1)} %shard_map.88.factor_hbm) | copy-start | bytes 9437188
  85.1 12.7 %copy-start.3 = (bf16[2,2048,384]{2,1,0:T(8,128)(2,1)S(1)}, bf16[2,2048,384]{2,1,0:T(8,128)(2,1)}, u32[]{:S(2)}) copy-start(bf16[2,2048,384]{2,1,0:T(8,128)(2,1)} %slice.22.foot_ref) | copy-start | bytes 9437188
  89.9 1.7 %collective-permute-start.6 = (f32[2,4,4,256]{3,2,1,0:T(4,128)S(1)}, f32[2,4,4,256]{3,2,1,0:T(4,128)S(1)}, u32[]{:S(2)}, u32[]{:S(2)}) collective-permute-start(f32[2,4,4,256]{3,2,1,0:T(4,128)S(1)} %get-tuple-element.54), channel_id=1, source_target_pairs={{0,32},{32,0},{64,96},{96,64},{128,160},{160,128},{192,224},{224,1... | collective-permute-start | bytes 98312 | tf_op jit(solution)/shard_map/ppermute | solution.py:514
  91.7 8.7 %collective-permute-start.7 = (f32[2,4,4,256]{3,2,1,0:T(4,128)S(1)}, f32[2,4,4,256]{3,2,1,0:T(4,128)S(1)}, u32[]{:S(2)}, u32[]{:S(2)}) collective-permute-start(f32[2,4,4,256]{3,2,1,0:T(4,128)S(1)} %reverse_add_fusion), channel_id=1, source_target_pairs={{0,1},{1,2},{2,3},{3,4},{4,5},{5,6},{6,7},{7,8},{8,9},{9,10},{10,1... | collective-permute-start | bytes 98312 | tf_op jit(solution)/shard_map/ppermute | solution.py:522
  100.1 6.7 %collective-permute-start.5 = (f32[4,64,256]{2,1,0:T(8,128)S(1)}, f32[4,64,256]{2,1,0:T(8,128)S(1)}, u32[]{:S(2)}, u32[]{:S(2)}) collective-permute-start(f32[4,64,256]{2,1,0:T(8,128)S(1)} %get-tuple-element.52), channel_id=1, source_target_pairs={{0,32},{32,0},{64,96},{96,64},{128,160},{160,128},{192,224},{224,1... | collective-permute-start | bytes 786440 | tf_op jit(solution)/shard_map/ppermute | solution.py:514
  100.4 6.4 %collective-permute-start.8 = (f32[4,4,256]{2,1,0:T(4,128)S(1)}, f32[4,4,256]{2,1,0:T(4,128)S(1)}, u32[]{:S(2)}, u32[]{:S(2)}) collective-permute-start(f32[4,4,256]{2,1,0:T(4,128)S(1)} %slice_bitcast_fusion), channel_id=1, source_target_pairs={{0,32},{32,0},{64,96},{96,64},{128,160},{160,128},{192,224},{224,1... | collective-permute-start | bytes 49160 | tf_op jit(solution)/shard_map/ppermute | solution.py:514
  106.9 7.9 %collective-permute-start.9 = (f32[64,256]{1,0:T(8,128)S(1)}, f32[64,256]{1,0:T(8,128)S(1)}, u32[]{:S(2)}, u32[]{:S(2)}) collective-permute-start(f32[64,256]{1,0:T(8,128)S(1)} %get-tuple-element.56), channel_id=1, source_target_pairs={{0,64},{32,96},{64,0},{96,32},{128,192},{160,224},{192,128},{224,1... | collective-permute-start | bytes 196616 | tf_op jit(solution)/shard_map/ppermute | solution.py:514
  112.5 7.3 %collective-permute-start.10 = (f32[64,256]{1,0:T(8,128)S(1)}, f32[64,256]{1,0:T(8,128)S(1)}, u32[]{:S(2)}, u32[]{:S(2)}) collective-permute-start(f32[64,256]{1,0:T(8,128)S(1)} %get-tuple-element.57), channel_id=1, source_target_pairs={{0,128},{32,160},{64,192},{96,224},{128,0},{160,32},{192,64},{224,... | collective-permute-start | bytes 196616 | tf_op jit(solution)/shard_map/ppermute | solution.py:514
  113.1 6.7 %collective-permute-start.11 = (f32[64,256]{1,0:T(8,128)S(1)}, f32[64,256]{1,0:T(8,128)S(1)}, u32[]{:S(2)}, u32[]{:S(2)}) collective-permute-start(f32[64,256]{1,0:T(8,128)S(1)} %get-tuple-element.58), channel_id=1, source_target_pairs={{0,192},{32,224},{64,128},{96,160},{128,64},{160,96},{192,0},{224,... | collective-permute-start | bytes 196616 | tf_op jit(solution)/shard_map/ppermute | solution.py:514
  120.7 5.1 %collective-permute-start.14 = (f32[64,256]{1,0:T(8,128)S(1)}, f32[64,256]{1,0:T(8,128)S(1)}, u32[]{:S(2)}, u32[]{:S(2)}) collective-permute-start(f32[64,256]{1,0:T(8,128)S(1)} %divide_multiply_fusion.refs_0_), channel_id=1, source_target_pairs={{0,192},{32,224},{64,128},{96,160},{128,64},{160,96},{192,0},{224,... | collective-permute-start | bytes 196616 | tf_op jit(solution)/shard_map/ppermute | solution.py:514
  122.4 7.1 %collective-permute-start.13 = (f32[64,256]{1,0:T(8,128)S(1)}, f32[64,256]{1,0:T(8,128)S(1)}, u32[]{:S(2)}, u32[]{:S(2)}) collective-permute-start(f32[64,256]{1,0:T(8,128)S(1)} %divide_multiply_fusion.refs_0_), channel_id=1, source_target_pairs={{0,128},{32,160},{64,192},{96,224},{128,0},{160,32},{192,64},{224,... | collective-permute-start | bytes 196616 | tf_op jit(solution)/shard_map/ppermute | solution.py:514
  123.7 5.8 %collective-permute-start.12 = (f32[64,256]{1,0:T(8,128)S(1)}, f32[64,256]{1,0:T(8,128)S(1)}, u32[]{:S(2)}, u32[]{:S(2)}) collective-permute-start(f32[64,256]{1,0:T(8,128)S(1)} %divide_multiply_fusion.refs_0_), channel_id=1, source_target_pairs={{0,64},{32,96},{64,0},{96,32},{128,192},{160,224},{192,128},{224,1... | collective-permute-start | bytes 196616 | tf_op jit(solution)/shard_map/ppermute | solution.py:514
  129.6 2.7 %collective-permute-start.15 = (f32[4,64,256]{2,1,0:T(8,128)S(1)}, f32[4,64,256]{2,1,0:T(8,128)S(1)}, u32[]{:S(2)}, u32[]{:S(2)}) collective-permute-start(f32[4,64,256]{2,1,0:T(8,128)S(1)} %pad_maximum_fusion), channel_id=1, source_target_pairs={{0,32},{32,0},{64,96},{96,64},{128,160},{160,128},{192,224},{224,1... | collective-permute-start | bytes 786440 | tf_op jit(solution)/shard_map/ppermute | solution.py:514

commit v3 on v2

--- a/solution.py
+++ b/solution.py
@@ -10,6 +10,7 @@
 f32 = jnp.float32
 bf16 = jnp.bfloat16
 LANES = 128
+MIRROR = 6
 VMEM = pl.BlockSpec(memory_space=pltpu.VMEM)
 SMEM = pl.BlockSpec(memory_space=pltpu.SMEM)
 HBM = pl.BlockSpec(memory_space=pltpu.HBM)
@@ -39,7 +40,7 @@
                 o_ref[s, slot, :, cols] = flat[pl.ds(first + s, rows, stride=slabs), :]
 
 
-def relay(half, measured, sides, first_view, views, count, into=None, slot=0, slots=None, after=None, cost=SMALL):
+def relay(half, measured, sides, first_view, views, count, into=None, slot=0, slots=None, after=(), cost=SMALL):
     segs, _, inner, slabs, bins = measured.shape
     rows = segs * inner
     slots = len(sides) if slots is None else slots
@@ -53,8 +54,7 @@
     if into is not None:
         aliases = {len(operands): 0}
         operands.append(into)
-    if after is not None:
-        operands.append(after)
+    operands += after
     specs = [SMEM] + specs + [pl.BlockSpec(memory_space=pl.ANY)] * (len(operands) - 1 - lanes)
     return pl.pallas_call(
         functools.partial(relay_kernel, sides, lanes),
@@ -156,12 +156,13 @@
     )(me, kernel, table, crystals.reshape(2, views, 1, bins))
 
 
-def forward_kernel(op_ref, ext_ref, foot_hbm, eff_ref, _, *refs):
-    lanes = (len(refs) - 4) // 2
+def forward_kernel(op_ref, act_ref, above_ref, below_ref, foot_hbm, eff_ref, *refs):
+    lanes = (len(refs) - 5) // 2
     rand_refs, o_ref, foot_ref, rows_ref = refs[:lanes], refs[lanes], refs[lanes + 1], refs[lanes + 2]
-    order_refs, sems = refs[lanes + 3 : -1], refs[-1]
+    order_refs, ext_ref, sems = refs[lanes + 3 : -2], refs[-2], refs[-1]
     segs, _, slices, _ = rand_refs[0].shape
     pixels = ext_ref.shape[1]
+    margin = above_ref.shape[0]
     inner = 2
     count = slices // inner
     view = pl.program_id(0)
@@ -173,6 +174,10 @@
     def _():
         for v in range(foot_ref.shape[0]):
             fetch(v).start()
+        ext_ref[...] = jnp.zeros_like(ext_ref)
+        ext_ref[:slices] = act_ref[...]
+        ext_ref[slices : slices + margin] = above_ref[...]
+        ext_ref[slices + margin : slices + 2 * margin] = below_ref[...]
         rows_ref[...] = jnp.dot(
             op_ref[...], ext_ref[...], preferred_element_type=f32, precision=lax.Precision.HIGHEST
         ).astype(bf16)
@@ -192,7 +197,7 @@
         o_ref[0, :, :, :, cols] = value.reshape(*o_ref.shape[1:4], LANES)
 
 
-def forward(operator, extended, footprint, randoms, efficiency, after):
+def forward(operator, activity, above, below, footprint, randoms, efficiency):
     segs, views, slices, bins = randoms.shape
     pixels = footprint.shape[1]
     rows = segs * slices
@@ -207,19 +212,20 @@
         in_specs=[
             VMEM,
             VMEM,
-            pl.BlockSpec(memory_space=pltpu.HBM),
+            VMEM,
+            VMEM,
+            HBM,
             pl.BlockSpec((1, 1, bins), lambda v: (v, 0, 0)),
-            pl.BlockSpec(memory_space=pl.ANY),
         ]
         + lanes,
         out_specs=pl.BlockSpec((1, 2, rows // inner // 2, inner, bins), lambda v: (v, 0, 0, 0, 0)),
         out_shape=jax.ShapeDtypeStruct((views, 2, rows // inner // 2, inner, bins), f32),
         scratch_shapes=[pltpu.VMEM(footprint.shape, footprint.dtype), pltpu.VMEM((rows, pixels), bf16)]
         + [pltpu.VMEM((rows, LANES), f32)] * len(lanes)
-        + [pltpu.SemaphoreType.DMA((views,))],
+        + [pltpu.VMEM((operator.shape[1], pixels), f32), pltpu.SemaphoreType.DMA((views,))],
         compiler_params=params(40),
         cost_estimate=SMALL,
-    )(operator, extended, footprint, efficiency, after, *[randoms] * len(lanes))
+    )(operator, activity, above, below, footprint, efficiency, *[randoms] * len(lanes))
 
 
 def back_project(operator, weighted, foot):
@@ -244,28 +250,48 @@
 
 
 def back_staged_kernel(
-    edge, half_ref, op_ref, staged_hbm, part_ref, factor_hbm, foot_hbm, acc_ref, own_ref, factor_ref, foot_ref, sems
+    edge,
+    half_ref,
+    op_ref,
+    staged_hbm,
+    part_ref,
+    factor_hbm,
+    foot_hbm,
+    acc_ref,
+    last_factor_ref,
+    last_foot_ref,
+    own_ref,
+    factor_ref,
+    foot_ref,
+    sems,
 ):
     half = half_ref[0]
     views, count, inner, bins = own_ref.shape
     firsts = factor_hbm.shape[0] - views
+    middles = foot_ref.shape[0]
+
+    def place(v):
+        if v < middles:
+            return factor_ref.at[v], foot_ref.at[v]
+        return last_factor_ref.at[v - middles], last_foot_ref.at[v - middles]
 
     def copies(v):
+        factor, foot = place(v)
         return [
             pltpu.make_async_copy(staged_hbm.at[:, 2 * v], own_ref.at[v], sems.at[v, 0]),
-            pltpu.make_async_copy(factor_hbm.at[firsts + v], factor_ref.at[v], sems.at[v, 1]),
-            pltpu.make_async_copy(foot_hbm.at[firsts + v], foot_ref.at[v], sems.at[v, 2]),
+            pltpu.make_async_copy(factor_hbm.at[firsts + v], factor, sems.at[v, 1]),
+            pltpu.make_async_copy(foot_hbm.at[firsts + v], foot, sems.at[v, 2]),
         ]
 
     for v in range(views):
         start_all(copies(v))
-    middles = (part_ref.shape[0] - 2 * edge * views) // (count - 2 * edge)
     operator = jnp.concatenate([op_ref[half], op_ref[1 - half]], axis=1)
     for v in range(views):
         for copy in copies(v):
             copy.wait()
-        far = factor_ref[v, 1 - half]
-        own = ratio(factor_ref[v, half], own_ref[v])
+        factor, foot = place(v)
+        far = factor[1 - half]
+        own = ratio(factor[half], own_ref[v])
         low = ratio(far[:edge], part_ref[2 * edge * v : 2 * edge * v + edge])
         high = ratio(far[count - edge :], part_ref[2 * edge * v + edge : 2 * edge * (v + 1)])
         if v < middles:
@@ -273,14 +299,14 @@
             middle = ratio(far[edge : count - edge], part_ref[first : first + count - 2 * edge])
         else:
             middle = jnp.zeros(((count - 2 * edge) * inner, bins), bf16)
-        spread = back_project(operator, jnp.concatenate([own, low, middle, high], axis=0), foot_ref[v])
+        spread = back_project(operator, jnp.concatenate([own, low, middle, high], axis=0), foot[...])
         if v == 0:
             acc_ref[...] = spread
         else:
             acc_ref[...] += spread
 
 
-def back_staged(half, operator, staged, part, factor, footprint, edge):
+def back_staged(half, operator, staged, part, factor, footprint, edge, lasts):
     ext = operator.shape[1]
     count, slots, inner, bins = staged.shape
     views = slots // 2
@@ -288,12 +314,16 @@
     return pl.pallas_call(
         functools.partial(back_staged_kernel, edge),
         in_specs=[SMEM, VMEM, HBM, VMEM, HBM, HBM],
-        out_specs=VMEM,
-        out_shape=jax.ShapeDtypeStruct((ext, pixels), f32),
+        out_specs=[VMEM] * 3,
+        out_shape=[
+            jax.ShapeDtypeStruct((ext, pixels), f32),
+            pltpu.VMEM((lasts, 2, count, inner, bins), f32),
+            pltpu.VMEM((lasts, pixels, bins), bf16),
+        ],
         scratch_shapes=[
             pltpu.VMEM((views, count, inner, bins), f32),
-            pltpu.VMEM((views, 2, count, inner, bins), f32),
-            pltpu.VMEM((views, pixels, bins), bf16),
+            pltpu.VMEM((views - lasts, 2, count, inner, bins), f32),
+            pltpu.VMEM((views - lasts, pixels, bins), bf16),
             pltpu.SemaphoreType.DMA((views, 3)),
         ],
         compiler_params=params(52),
@@ -361,44 +391,91 @@
     )(half, me, operator, near, factor, footprint, acc)
 
 
-def pieces_kernel(edge, views, staged_hbm, part_ref, last_ref, sems):
+def part_kernel(edge, views, staged_hbm, part_ref, sems):
     count = staged_hbm.shape[0]
     middle = count - 2 * edge
     copies = []
 
-    def add(slices, v, target):
-        copies.append(pltpu.make_async_copy(staged_hbm.at[slices, 2 * v + 1], target, sems.at[len(copies)]))
-
-    lasts = last_ref.shape[1]
+    def add(first, size, v, place):
+        copies.append(
+            pltpu.make_async_copy(
+                staged_hbm.at[pl.ds(first, size), 2 * v + 1],
+                part_ref.at[pl.ds(place, size)],
+                sems.at[len(copies)],
+            )
+        )
+
     for v in range(views):
-        add(pl.ds(0, edge), v, part_ref.at[pl.ds(2 * edge * v, edge)])
-        add(pl.ds(count - edge, edge), v, part_ref.at[pl.ds(2 * edge * v + edge, edge)])
-        if v < views - lasts:
-            add(pl.ds(edge, middle), v, part_ref.at[pl.ds(2 * edge * views + middle * v, middle)])
-        else:
-            add(pl.ds(edge, middle), v, last_ref.at[:, v - views + lasts])
+        add(0, edge, v, 2 * edge * v)
+        add(count - edge, edge, v, 2 * edge * v + edge)
+    for v in range((part_ref.shape[0] - 2 * edge * views) // middle):
+        add(edge, middle, v, 2 * edge * views + middle * v)
     start_all(copies)
     for copy in copies:
         copy.wait()
 
 
-def pieces(staged, edge, lasts):
+def part_of(staged, edge, lasts):
     count, slots, inner, bins = staged.shape
     views = slots // 2
-    middle = count - 2 * edge
-    part = 2 * edge * views + middle * (views - lasts)
-    return pl.pallas_call(
-        functools.partial(pieces_kernel, edge, views),
+    part = 2 * edge * views + (count - 2 * edge) * (views - lasts)
+    return pl.pallas_call(
+        functools.partial(part_kernel, edge, views),
         in_specs=[HBM],
-        out_specs=[VMEM] * 2,
-        out_shape=[
-            pltpu.VMEM((part, inner, bins), f32),
-            pltpu.VMEM((middle, lasts, inner, bins), f32),
-        ],
+        out_specs=VMEM,
+        out_shape=pltpu.VMEM((part, inner, bins), f32),
         scratch_shapes=[pltpu.SemaphoreType.DMA((3 * views,))],
         compiler_params=params(16),
         cost_estimate=SMALL,
     )(staged)
+
+
+def last_kernel(edge, staged_hbm, _, last_ref, sems):
+    views = staged_hbm.shape[1] // 2
+    middle, lasts = last_ref.shape[:2]
+    copies = [
+        pltpu.make_async_copy(
+            staged_hbm.at[pl.ds(edge, middle), 2 * (views - lasts + v) + 1], last_ref.at[:, v], sems.at[v]
+        )
+        for v in range(lasts)
+    ]
+    start_all(copies)
+    for copy in copies:
+        copy.wait()
+
+
+def last_of(staged, edge, lasts, after):
+    count, _, inner, bins = staged.shape
+    return pl.pallas_call(
+        functools.partial(last_kernel, edge),
+        in_specs=[HBM, pl.BlockSpec(memory_space=pl.ANY)],
+        out_specs=VMEM,
+        out_shape=pltpu.VMEM((count - 2 * edge, lasts, inner, bins), f32),
+        scratch_shapes=[pltpu.SemaphoreType.DMA((lasts,))],
+        compiler_params=params(16),
+        cost_estimate=SMALL,
+    )(staged, after)
+
+
+def crossing_kernel(half_ref, m_hbm, o_ref, sem):
+    views, count = o_ref.shape[1], o_ref.shape[3]
+    first = pl.multiple_of((1 - half_ref[0]) * count, count)
+    copy = pltpu.make_async_copy(m_hbm.at[:, pl.ds(0, views), :, pl.ds(first, count)], o_ref, sem)
+    copy.start()
+    copy.wait()
+
+
+def crossing(half, measured, views):
+    segs, _, inner, slabs, bins = measured.shape
+    return pl.pallas_call(
+        crossing_kernel,
+        in_specs=[SMEM, HBM],
+        out_specs=VMEM,
+        out_shape=pltpu.VMEM((segs, views, inner, slabs // 2, bins), f32),
+        scratch_shapes=[pltpu.SemaphoreType.DMA],
+        compiler_params=params(52),
+        cost_estimate=SMALL,
+    )(half, measured)
 
 
 def mark_kernel(x_ref, o_ref):
@@ -454,13 +531,13 @@
     )(half, me, operator, rows_in, factor, footprint, acc)
 
 
-def pair_kernel(me_ref, *refs):
+def pair_kernel(me_ref, flip_ref, *refs):
     mine_refs, theirs_ref, halo_ref, across_ref, out_refs = refs[:4], refs[4], refs[5], refs[6], refs[7:]
     core = me_ref[0] % 2
     slices, _ = mine_refs[0].shape
     margin = halo_ref.shape[2]
     for k in range(4):
-        here, there = halo_ref[0, k], across_ref[k]
+        here, there = halo_ref[0, k ^ flip_ref[0]], across_ref[k ^ flip_ref[1]]
         above = jnp.where(core == 0, here, there)
         below = jnp.where(core == 0, there, here)
         out_refs[k][...] = mine_refs[k][...] + theirs_ref[k]
@@ -468,15 +545,15 @@
         out_refs[k][slices - margin :] += below
 
 
-def pair_sum(me, mine, theirs, halo, across):
+def pair_sum(me, flip, mine, theirs, halo, across):
     return pl.pallas_call(
         pair_kernel,
-        in_specs=[SMEM] + [VMEM] * 7,
+        in_specs=[SMEM] * 2 + [VMEM] * 7,
         out_specs=[VMEM] * 4,
         out_shape=[pltpu.VMEM(x.shape, f32) for x in mine],
         compiler_params=params(16),
         cost_estimate=SMALL,
-    )(me, *mine, theirs, halo, across)
+    )(me, flip, *mine, theirs, halo, across)
 
 
 def assemble_kernel(me_ref, *refs):
@@ -513,16 +590,18 @@
     def swap(x, k):
         return lax.ppermute(x, "seg", [(i, i ^ k) for i in range(2 * halves)])
 
-    def outward(x):
+    def shift(x, ups):
         pairs = []
         for j in range(2 * halves):
             for i in range(slabs - 1):
-                source, target = (i, i + 1) if j % 2 == 0 else (i + 1, i)
-                pairs.append((j * slabs + source, j * slabs + target))
+                source, target = (i + 1, i) if j % 2 in ups else (i, i + 1)
+                to = j ^ MIRROR if i + 1 == slabs // 2 else j
+                pairs.append((j * slabs + source, to * slabs + target))
         return lax.ppermute(x, ("seg", "slab"), pairs)
 
     count = slabs // 2
-    half = (lax.axis_index("slab").astype(jnp.int32) // count).reshape(1)
+    slab = lax.axis_index("slab").astype(jnp.int32)
+    half = (slab // count).reshape(1)
     edge = margin // inner
     firsts = views // 2
     lasts = 2
@@ -535,43 +614,34 @@
         return lax.all_to_all(x, "slab", split_axis=0, concat_axis=0, tiled=True, axis_index_groups=groups)
 
     ext = slices + 2 * margin
-    early = lax.dynamic_slice_in_dim(measured[:, :firsts], (1 - half[0]) * count, count, 3)
-    early = cross(early)
+    early = cross(crossing(half, measured, firsts))
     staged = relay(half, measured, (0, 1), firsts, views - firsts, count)
     staged, near_activity = lax.optimization_barrier((staged, activity))
     staged = exchange(staged)
     near = relay(half, measured, (0,), 0, firsts, count, slots=2, cost=SMALL)
     efficiency, operator, operator_t = setup(me, kernel, dead_counts, crystals, slices, segs, inner, halves)
     even = group % 2 == 0
-    halo = outward(jnp.where(even, near_activity[slices - margin :], near_activity[:margin]))
-    across = swap(halo, 1)
-    extended = jnp.concatenate(
-        [
-            activity,
-            jnp.where(even, halo, across),
-            jnp.where(even, across, halo),
-            jnp.zeros((8, pixels), f32),
-        ],
-        axis=0,
+    above = shift(near_activity[slices - margin :], ())
+    below = shift(near_activity[:margin], (0, 1))
+    staged, near, begun, efficiency, operator, operator_t, above, below = lax.optimization_barrier(
+        (staged, near, mark(early), efficiency, operator, operator_t, above, below)
     )
-
-    staged, near, begun = lax.optimization_barrier((staged, near, mark(early)))
-    part, rows_last = pieces(staged, edge, lasts)
-    part = cross(part)
-    near = relay(half, early, (1,), 0, firsts, count, into=near, slot=1, slots=2, after=begun)
-    rows_last, near = lax.optimization_barrier((rows_last, near))
-    rows_last = cross(rows_last)
+    part = cross(part_of(staged, edge, lasts))
+    near = relay(half, early, (1,), 0, firsts, count, into=near, slot=1, slots=2, after=[begun])
+    rows_last = cross(last_of(staged, edge, lasts, near))
     near = exchange(near)
-    factor = forward(operator, extended, footprint, randoms, efficiency, begun)
-
-    last_factor, last_foot = factor[views - lasts :], footprint[views - lasts :]
-    acc = back_staged(half, operator_t, staged, part, factor, footprint, edge)
-    acc, last_factor, last_foot = lax.optimization_barrier((acc, last_factor, last_foot))
+    factor = forward(operator, activity, above, below, footprint, randoms, efficiency)
+
+    acc, last_factor, last_foot = back_staged(
+        half, operator_t, staged, part, factor, footprint, edge, lasts
+    )
     acc, keep, give = back_near(half, me, operator_t, near, factor, footprint, acc, slices, margin)
-    halo = outward(keep + swap(give, 1)[::-1])
+    halo = shift(keep + swap(give, 1)[::-1], (1,))
     across = swap(halo[1], 1)
     *mine, other = back_last(half, me, operator_t, rows_last, last_factor, last_foot, acc)
-    pair = pair_sum(me, mine, swap(other, 1), halo, across)
+    sides = [jnp.where(even, slab == count, slab == count - 1), jnp.where(even, slab == count - 1, slab == count)]
+    flip = jnp.where(jnp.stack(sides), MIRROR // 2, 0).astype(jnp.int32)
+    pair = pair_sum(me, flip, mine, swap(other, 1), halo, across)
     total = pair[0]
     for k in range(1, 4):
         total = total + swap(pair[k], 2 * k)

time: 134 us -> 130 us (0.970)
  the two profiles are of different devices: /device:TPU:129 before, /device:TPU:31 now
where the time goes in v3:
time: 130 us; the launch traced here: 129 us
  starting transfers between devices  59.3 us (46%)
  Pallas kernels  43.2 us (33%)
  waiting for transfers between devices  13.7 us (11%)
  local copies, waits for them, and re-layouts  11.4 us (9%)
    all_to_all x2, starting transfers between devices, exchange(): lax.all_to_all(x, 'slab', split_axis=0, concat_axis=0, tiled=True, axis_i...  20.4 us
    ppermute x10, starting transfers between devices, swap(): return lax.ppermute(x, 'seg', [(i, i ^ k) for i in range(2 * halves)])  18.9 us
    ppermute x3, starting transfers between devices, shift(): return lax.ppermute(x, ('seg', 'slab'), pairs)  12.8 us
    ppermute x10, waiting for transfers between devices, swap(): return lax.ppermute(x, 'seg', [(i, i ^ k) for i in range(2 * halves)])  11.4 us
    unnamed x30, local copies, waits for them, and re-layouts  9.77 us
    pallas_call x1, Pallas kernels, forward(): pl.pallas_call(forward_kernel, grid=(views,), in_specs=[VMEM, VMEM, VMEM,...  8.87 us
    pallas_call x3, Pallas kernels, relay(): pl.pallas_call(functools.partial(relay_kernel, sides, lanes), grid=(views...  8.44 us
    ppermute x3, starting transfers between devices, cross(): lax.ppermute(x, 'slab', [(i, (i + count) % slabs) for i in range(slabs)])  7.21 us
  transfers between devices with their start and end apart: 18, of which 9 were waited for; matrix products, arithmetic and copies ran while one was open for 1% of the time, Pallas kernels for 30%

profile of v3, /device:TPU:31, one launch (start us, length us, event | category | flops | bytes accessed | tf_op | source)
XLA Modules:
  0.0 128.9 jit_solution(13454361754497914224)
XLA Ops:
  1.2 7.0 %collective-permute-start = (f32[4,4,2,16,384]{4,3,2,1,0:T(8,128)S(1)}, f32[4,4,2,16,384]{4,3,2,1,0:T(8,128)S(1)}, u32[]{:S(2)}, u32[]{:S(2)}) collective-permute-start(f32[4,4,2,16,384]{4,3,2,1,0:T(8,128)S(1)} %shard_map.84), channel_id=1, source_target_pairs={{0,16},{1,17},{2,18},{3,19},{4,20},{5,21},{6,22},{7,23},{8,24},{9,... | collective-permute-start | bytes 2359304 | tf_op jit(solution)/shard_map/ppermute | solution.py:610
  8.1 4.1 %shard_map.82 = f32[16,8,8,384]{3,2,1,0:T(8,128)} custom-call(s32[1]{0:T(128)} %bitcast.3.half_ref, f32[4,8,2,32,384]{4,3,2,1,0:T(8,128)} %m_hbm.1, f32[4,8,2,32,384]{4,3,2,1,0:T(8,128)} %m_hbm.1, f32[4,8,2,32,384]{4,3,2,1,0:T(8,128)} %m_hbm.1), custom_call_target="tpu_custom_call" | custom-call | flops 1 | bytes 1 | tf_op jit(solution)/shard_map/pallas_call | solution.py:59
  12.3 6.5 %all-to-all-start = ((f32[16,8,8,384]{3,2,1,0:T(8,128)}), f32[16,8,8,384]{3,2,1,0:T(8,128)}, u32[]{:S(2)}, u32[]{:S(2)}) async-start(f32[16,8,8,384]{3,2,1,0:T(8,128)} %shard_map.82), calls=%async_computation | async-start | bytes 3145728 | tf_op jit(solution)/shard_map/all_to_all | solution.py:614
  18.8 1.5 %fusion = (f32[4,2048]{1,0:T(4,128)}, f32[4,2048]{1,0:T(4,128)}) fusion(f32[64,2048]{1,0:T(8,128)} %act_ref.1), kind=kLoop, calls=%fused_computation.5 | loop fusion | bytes 131072 | tf_op jit(solution)/shard_map/slice | solution.py:625
  20.3 2.5 %collective-permute-start.2 = (f32[4,2048]{1,0:T(4,128)}, f32[4,2048]{1,0:T(4,128)}, u32[]{:S(2)}, u32[]{:S(2)}) collective-permute-start(f32[4,2048]{1,0:T(4,128)} %get-tuple-element.61), channel_id=1, source_target_pairs={{1,0},{2,1},{3,2},{4,3},{5,4},{6,5},{7,6},{8,7},{9,8},{10,9},{11,1... | collective-permute-start | bytes 98312 | tf_op jit(solution)/shard_map/ppermute | solution.py:600
  22.8 8.4 %collective-permute-start.1 = (f32[4,2048]{1,0:T(4,128)}, f32[4,2048]{1,0:T(4,128)}, u32[]{:S(2)}, u32[]{:S(2)}) collective-permute-start(f32[4,2048]{1,0:T(4,128)} %get-tuple-element.62), channel_id=1, source_target_pairs={{0,1},{1,2},{2,3},{3,4},{4,5},{5,6},{6,7},{7,8},{8,9},{9,10},{10,1... | collective-permute-start | bytes 98312 | tf_op jit(solution)/shard_map/ppermute | solution.py:600
  31.2 2.6 %shard_map.83.refs_3_ = f32[16,8,8,384]{3,2,1,0:T(8,128)S(1)} custom-call(s32[1]{0:T(128)} %bitcast.3.half_ref, f32[4,8,2,32,384]{4,3,2,1,0:T(8,128)} %m_hbm.1, f32[4,8,2,32,384]{4,3,2,1,0:T(8,128)} %m_hbm.1, f32[4,8,2,32,384]{4,3,2,1,0:T(8,128)} %m_hbm.1), custom_call_target="tpu_custom_call" | custom-call | flops 1 | bytes 1 | tf_op jit(solution)/shard_map/pallas_call | solution.py:59
  33.8 1.2 copy-done.1
  35.1 6.0 %shard_map.86 = (f32[8,1,384]{2,1,0:T(1,128)S(1)}, f32[256,80]{1,0:T(8,128)S(1)}, f32[2,80,128]{2,1,0:T(8,128)S(1)}) custom-call(s32[1]{0:T(128)} %bitcast.me_ref, f32[16,9]{1,0:T(8,128)S(1)} %copy-done.12, s32[128,512]{1,0:T(8,128)S(1)} %bitcast.12, s32[2,8,1,384]{3,2,1,0:T(1,128)S(1)} %reshape.15.c_ref), custom_call_target="tpu_custom_call" | custom-call | flops 1 | bytes 1 | tf_op jit(solution)/shard_map/pallas_call | solution.py:145
  41.7 1.7 %collective-permute-done.2.below_ref = f32[4,2048]{1,0:T(4,128)} collective-permute-done((f32[4,2048]{1,0:T(4,128)}, f32[4,2048]{1,0:T(4,128)}, u32[]{:S(2)}, u32[]{:S(2)}) %collective-permute-start.2) | collective-permute-done | bytes 32800 | tf_op jit(solution)/shard_map/ppermute | solution.py:600
  44.1 2.0 %shard_map.89 = f32[40,8,384]{2,1,0:T(8,128)} custom-call(f32[16,8,8,384]{3,2,1,0:T(8,128)} %all-to-all-done.staged_hbm), custom_call_target="tpu_custom_call" | custom-call | flops 1 | bytes 1 | tf_op jit(solution)/shard_map/pallas_call | solution.py:422
  46.2 1.7 %shard_map.87._ = f32[16,8,8,384]{3,2,1,0:T(8,128)} custom-call(s32[1]{0:T(128)} %bitcast.3.half_ref, f32[4,4,2,16,384]{4,3,2,1,0:T(8,128)S(1)} %collective-permute-done.x_ref.refs_0_.refs_1_.refs_2_, f32[4,4,2,16,384]{4,3,2,1,0:T(8,128)S(1)} %collective-permute-done.x_ref.refs_0_.refs_1_.refs_2_, ...), custom_call_target="tpu_custom_call", output_to_operand_aliasing={{}: (4, {})} | custom-call | flops 1 | bytes 1 | tf_op jit(solution)/shard_map/pallas_call | solution.py:59
  47.9 13.9 %all-to-all-start.1 = ((f32[16,8,8,384]{3,2,1,0:T(8,128)}), f32[16,8,8,384]{3,2,1,0:T(8,128)}, u32[]{:S(2)}, u32[]{:S(2)}) async-start(f32[16,8,8,384]{3,2,1,0:T(8,128)} %shard_map.87._), calls=%async_computation.1 | async-start | bytes 3145728 | tf_op jit(solution)/shard_map/all_to_all | solution.py:614
  61.8 1.4 %copy-done.2 = f32[16,8,8,384]{3,2,1,0:T(8,128)S(1)} copy-done((f32[16,8,8,384]{3,2,1,0:T(8,128)S(1)}, f32[16,8,8,384]{3,2,1,0:T(8,128)}, u32[]{:S(2)}) %copy-start.2) | copy-done | bytes 1572888
  63.3 1.8 %shard_map.88 = f32[12,2,8,384]{3,2,1,0:T(8,128)} custom-call(f32[16,8,8,384]{3,2,1,0:T(8,128)} %all-to-all-done.staged_hbm, f32[16,8,8,384]{3,2,1,0:T(8,128)S(1)} %copy-done.2), custom_call_target="tpu_custom_call" | custom-call | flops 1 | bytes 1 | tf_op jit(solution)/shard_map/pallas_call | solution.py:449
  65.2 8.9 %shard_map.90.factor_hbm = f32[8,2,16,8,384]{4,3,2,1,0:T(8,128)S(1)} custom-call(f32[256,80]{1,0:T(8,128)S(1)} %get-tuple-element.42.op_ref, f32[64,2048]{1,0:T(8,128)S(1)} %copy-done.4, f32[4,2048]{1,0:T(4,128)} %collective-permute-done.1.above_ref, f32[4,2048]{1,0:T(4,128)} %collective-permute-done.2.below_ref, bf16[8,2048,384]{2,1,0:T(8,128)(2,1)} %foot_hbm.5, ...), custom_call_target="tpu_custom_call" | custom-call | flops 1 | bytes 1 | tf_op jit(solution)/shard_map/pallas_call | solution.py:209
  74.1 1.6 %copy-done.3 = f32[8,2,16,8,384]{4,3,2,1,0:T(8,128)} copy-done((f32[8,2,16,8,384]{4,3,2,1,0:T(8,128)}, f32[8,2,16,8,384]{4,3,2,1,0:T(8,128)S(1)}, u32[]{:S(2)}) %copy-start.3) | copy-done | bytes 3145752
  75.7 6.5 %shard_map.91 = (f32[80,2048]{1,0:T(8,128)}, f32[2,2,16,8,384]{4,3,2,1,0:T(8,128)S(1)}, bf16[2,2048,384]{2,1,0:T(8,128)(2,1)S(1)}) custom-call(s32[1]{0:T(128)} %bitcast.3.half_ref, f32[2,80,128]{2,1,0:T(8,128)} %copy-done.10, f32[16,8,8,384]{3,2,1,0:T(8,128)} %all-to-all-done.staged_hbm, f32[40,8,384]{2,1,0:T(8,128)} %collective-permute-done.4.part_ref, ...), custom_call_target="tpu_custom_call" | custom-call | flops 999999995904 | bytes 1048576 | tf_op jit(solution)/shard_map/pallas_call | solution.py:314
  84.2 4.7 %shard_map.92 = (f32[64,2048]{1,0:T(8,128)S(1)}, f32[2,4,4,256]{3,2,1,0:T(4,128)S(1)}, f32[2,4,4,256]{3,2,1,0:T(4,128)S(1)}) custom-call(s32[1]{0:T(128)} %bitcast.3.half_ref, s32[1]{0:T(128)} %bitcast.me_ref, f32[2,80,128]{2,1,0:T(8,128)S(1)} %copy-done.11, f32[16,8,8,384]{3,2,1,0:T(8,128)} %all-to-all-done.1.near_hbm, f32[8,2,16,8,384]{4,3,2,1,0:T(8,128)} %copy-done.3, ...), custom_call_target="tpu_custom_call" | custom-call | flops 1 | bytes 1 | tf_op jit(solution)/shard_map/pallas_call | solution.py:377
  89.7 5.5 %collective-permute-start.6 = (f32[2,4,4,256]{3,2,1,0:T(4,128)S(1)}, f32[2,4,4,256]{3,2,1,0:T(4,128)S(1)}, u32[]{:S(2)}, u32[]{:S(2)}) collective-permute-start(f32[2,4,4,256]{3,2,1,0:T(4,128)S(1)} %get-tuple-element.56), channel_id=1, source_target_pairs={{0,32},{32,0},{64,96},{96,64},{128,160},{160,128},{192,224},{224,1... | collective-permute-start | bytes 98312 | tf_op jit(solution)/shard_map/ppermute | solution.py:591
  96.1 1.9 %collective-permute-start.7 = (f32[2,4,4,256]{3,2,1,0:T(4,128)S(1)}, f32[2,4,4,256]{3,2,1,0:T(4,128)S(1)}, u32[]{:S(2)}, u32[]{:S(2)}) collective-permute-start(f32[2,4,4,256]{3,2,1,0:T(4,128)S(1)} %reverse_add_fusion), channel_id=1, source_target_pairs={{0,1},{1,2},{2,3},{3,4},{4,5},{5,6},{6,7},{7,8},{8,9},{9,10},{10,1... | collective-permute-start | bytes 98312 | tf_op jit(solution)/shard_map/ppermute | solution.py:600
  100.2 2.3 %shard_map.93 = (f32[64,256]{1,0:T(8,128)S(1)}, f32[64,256]{1,0:T(8,128)S(1)}, f32[64,256]{1,0:T(8,128)S(1)}, f32[64,256]{1,0:T(8,128)S(1)}, f32[4,64,256]{2,1,0:T(8,128)S(1)}) custom-call(s32[1]{0:T(128)} %bitcast.3.half_ref, s32[1]{0:T(128)} %bitcast.me_ref, f32[2,80,128]{2,1,0:T(8,128)S(1)} %copy-done.11, f32[12,2,8,384]{3,2,1,0:T(8,128)} %collective-permute-done.3.x_ref, ...), custom_call_target="tpu_custom_call" | custom-call | flops 1 | bytes 1 | tf_op jit(solution)/shard_map/pallas_call | solution.py:523
  102.6 3.8 %collective-permute-start.5 = (f32[4,64,256]{2,1,0:T(8,128)S(1)}, f32[4,64,256]{2,1,0:T(8,128)S(1)}, u32[]{:S(2)}, u32[]{:S(2)}) collective-permute-start(f32[4,64,256]{2,1,0:T(8,128)S(1)} %get-tuple-element.54), channel_id=1, source_target_pairs={{0,32},{32,0},{64,96},{96,64},{128,160},{160,128},{192,224},{224,1... | collective-permute-start | bytes 786440 | tf_op jit(solution)/shard_map/ppermute | solution.py:591
  110.0 1.8 %collective-permute-start.11 = (f32[64,256]{1,0:T(8,128)S(1)}, f32[64,256]{1,0:T(8,128)S(1)}, u32[]{:S(2)}, u32[]{:S(2)}) collective-permute-start(f32[64,256]{1,0:T(8,128)S(1)} %get-tuple-element.60), channel_id=1, source_target_pairs={{0,192},{32,224},{64,128},{96,160},{128,64},{160,96},{192,0},{224,... | collective-permute-start | bytes 196616 | tf_op jit(solution)/shard_map/ppermute | solution.py:591
  111.8 2.2 %collective-permute-done.10 = f32[64,256]{1,0:T(8,128)S(1)} collective-permute-done((f32[64,256]{1,0:T(8,128)S(1)}, f32[64,256]{1,0:T(8,128)S(1)}, u32[]{:S(2)}, u32[]{:S(2)}) %collective-permute-start.10) | collective-permute-done | bytes 65568 | tf_op jit(solution)/shard_map/ppermute | solution.py:591
  114.0 1.3 collective-permute-done.11
  116.2 1.7 %collective-permute-start.14 = (f32[64,256]{1,0:T(8,128)S(1)}, f32[64,256]{1,0:T(8,128)S(1)}, u32[]{:S(2)}, u32[]{:S(2)}) collective-permute-start(f32[64,256]{1,0:T(8,128)S(1)} %divide_multiply_fusion.refs_0_), channel_id=1, source_target_pairs={{0,192},{32,224},{64,128},{96,160},{128,64},{160,96},{192,0},{224,... | collective-permute-start | bytes 196616 | tf_op jit(solution)/shard_map/ppermute | solution.py:591
  117.9 2.1 %collective-permute-start.13 = (f32[64,256]{1,0:T(8,128)S(1)}, f32[64,256]{1,0:T(8,128)S(1)}, u32[]{:S(2)}, u32[]{:S(2)}) collective-permute-start(f32[64,256]{1,0:T(8,128)S(1)} %divide_multiply_fusion.refs_0_), channel_id=1, source_target_pairs={{0,128},{32,160},{64,192},{96,224},{128,0},{160,32},{192,64},{224,... | collective-permute-start | bytes 196616 | tf_op jit(solution)/shard_map/ppermute | solution.py:591
  120.0 1.2 collective-permute-done.14.refs_3_
  121.2 3.9 %collective-permute-done.13.refs_2_ = f32[64,256]{1,0:T(8,128)S(1)} collective-permute-done((f32[64,256]{1,0:T(8,128)S(1)}, f32[64,256]{1,0:T(8,128)S(1)}, u32[]{:S(2)}, u32[]{:S(2)}) %collective-permute-start.13) | collective-permute-done | bytes 65568 | tf_op jit(solution)/shard_map/ppermute | solution.py:591
  125.1 1.8 %collective-permute-start.15 = (f32[4,64,256]{2,1,0:T(8,128)S(1)}, f32[4,64,256]{2,1,0:T(8,128)S(1)}, u32[]{:S(2)}, u32[]{:S(2)}) collective-permute-start(f32[4,64,256]{2,1,0:T(8,128)S(1)} %pad_maximum_fusion), channel_id=1, source_target_pairs={{0,32},{32,0},{64,96},{96,64},{128,160},{160,128},{192,224},{224,1... | collective-permute-start | bytes 786440 | tf_op jit(solution)/shard_map/ppermute | solution.py:591
  126.9 1.2 collective-permute-done.15.refs_4_
  (56 shorter events, 13.9 us)
Async XLA Ops:
  1.2 40.0 %collective-permute-start = (f32[4,4,2,16,384]{4,3,2,1,0:T(8,128)S(1)}, f32[4,4,2,16,384]{4,3,2,1,0:T(8,128)S(1)}, u32[]{:S(2)}, u32[]{:S(2)}) collective-permute-start(f32[4,4,2,16,384]{4,3,2,1,0:T(8,128)S(1)} %shard_map.84), channel_id=1, source_target_pairs={{0,16},{1,17},{2,18},{3,19},{4,20},{5,21},{6,22},{7,23},{8,24},{9,... | collective-permute-start | bytes 2359304 | tf_op jit(solution)/shard_map/ppermute | solution.py:610
  12.3 31.8 %all-to-all-start = ((f32[16,8,8,384]{3,2,1,0:T(8,128)}), f32[16,8,8,384]{3,2,1,0:T(8,128)}, u32[]{:S(2)}, u32[]{:S(2)}) async-start(f32[16,8,8,384]{3,2,1,0:T(8,128)} %shard_map.82), calls=%async_computation | async-start | bytes 3145728 | tf_op jit(solution)/shard_map/all_to_all | solution.py:614
  20.3 23.2 %collective-permute-start.2 = (f32[4,2048]{1,0:T(4,128)}, f32[4,2048]{1,0:T(4,128)}, u32[]{:S(2)}, u32[]{:S(2)}) collective-permute-start(f32[4,2048]{1,0:T(4,128)} %get-tuple-element.61), channel_id=1, source_target_pairs={{1,0},{2,1},{3,2},{4,3},{5,4},{6,5},{7,6},{8,7},{9,8},{10,9},{11,1... | collective-permute-start | bytes 98312 | tf_op jit(solution)/shard_map/ppermute | solution.py:600
  22.8 12.2 %copy-start.14 = (s32[2,8,384]{2,1,0:T(8,128)S(1)}, s32[2,8,384]{2,1,0:T(8,128)}, u32[]{:S(2)}) copy-start(s32[2,8,384]{2,1,0:T(8,128)} %param.14) | copy-start | bytes 73732
  22.8 12.2 %copy-start.13 = (s32[65536]{0:T(1024)S(1)}, s32[65536]{0:T(1024)}, u32[]{:S(2)}) copy-start(s32[65536]{0:T(1024)} %param.13) | copy-start | bytes 786436
  22.8 12.3 %copy-start.12 = (f32[16,9]{1,0:T(8,128)S(1)}, f32[16,9]{1,0:T(8,128)}, u32[]{:S(2)}) copy-start(f32[16,9]{1,0:T(8,128)} %k_ref.1) | copy-start | bytes 1732
  22.8 21.3 %collective-permute-start.1 = (f32[4,2048]{1,0:T(4,128)}, f32[4,2048]{1,0:T(4,128)}, u32[]{:S(2)}, u32[]{:S(2)}) collective-permute-start(f32[4,2048]{1,0:T(4,128)} %get-tuple-element.62), channel_id=1, source_target_pairs={{0,1},{1,2},{2,3},{3,4},{4,5},{5,6},{6,7},{7,8},{8,9},{9,10},{10,1... | collective-permute-start | bytes 98312 | tf_op jit(solution)/shard_map/ppermute | solution.py:600
  33.8 1.2 copy-start.1
  46.1 29.6 %collective-permute-start.4 = (f32[40,8,384]{2,1,0:T(8,128)}, f32[40,8,384]{2,1,0:T(8,128)}, u32[]{:S(2)}, u32[]{:S(2)}) collective-permute-start(f32[40,8,384]{2,1,0:T(8,128)} %shard_map.89), channel_id=1, source_target_pairs={{0,16},{1,17},{2,18},{3,19},{4,20},{5,21},{6,22},{7,23},{8,24},{9,... | collective-permute-start | bytes 1474568 | tf_op jit(solution)/shard_map/ppermute | solution.py:610
  47.9 17.2 %copy-start = (s32[4,8,64,384]{3,2,1,0:T(8,128)S(1)}, s32[4,8,64,384]{3,2,1,0:T(8,128)}, u32[]{:S(2)}) copy-start(s32[4,8,64,384]{3,2,1,0:T(8,128)} %refs_2_.5) | copy-start | bytes 9437188
  47.9 35.2 %all-to-all-start.1 = ((f32[16,8,8,384]{3,2,1,0:T(8,128)}), f32[16,8,8,384]{3,2,1,0:T(8,128)}, u32[]{:S(2)}, u32[]{:S(2)}) async-start(f32[16,8,8,384]{3,2,1,0:T(8,128)} %shard_map.87._), calls=%async_computation.1 | async-start | bytes 3145728 | tf_op jit(solution)/shard_map/all_to_all | solution.py:614
  61.8 1.4 %copy-start.2 = (f32[16,8,8,384]{3,2,1,0:T(8,128)S(1)}, f32[16,8,8,384]{3,2,1,0:T(8,128)}, u32[]{:S(2)}) copy-start(f32[16,8,8,384]{3,2,1,0:T(8,128)} %shard_map.87._) | copy-start | bytes 4718596
  63.3 1.9 %copy-start.4 = (f32[64,2048]{1,0:T(8,128)S(1)}, f32[64,2048]{1,0:T(8,128)}, u32[]{:S(2)}) copy-start(f32[64,2048]{1,0:T(8,128)} %act_ref.1) | copy-start | bytes 1572868
  65.0 33.0 %collective-permute-start.3 = (f32[12,2,8,384]{3,2,1,0:T(8,128)}, f32[12,2,8,384]{3,2,1,0:T(8,128)}, u32[]{:S(2)}, u32[]{:S(2)}) collective-permute-start(f32[12,2,8,384]{3,2,1,0:T(8,128)} %shard_map.88), channel_id=1, source_target_pairs={{0,16},{1,17},{2,18},{3,19},{4,20},{5,21},{6,22},{7,23},{8,24},{9,... | collective-permute-start | bytes 884744 | tf_op jit(solution)/shard_map/ppermute | solution.py:610
  74.1 1.6 %copy-start.3 = (f32[8,2,16,8,384]{4,3,2,1,0:T(8,128)}, f32[8,2,16,8,384]{4,3,2,1,0:T(8,128)S(1)}, u32[]{:S(2)}) copy-start(f32[8,2,16,8,384]{4,3,2,1,0:T(8,128)S(1)} %shard_map.90.factor_hbm) | copy-start | bytes 9437188
  75.7 7.4 %copy-start.11 = (f32[2,80,128]{2,1,0:T(8,128)S(1)}, f32[2,80,128]{2,1,0:T(8,128)}, u32[]{:S(2)}) copy-start(f32[2,80,128]{2,1,0:T(8,128)} %copy-done.10) | copy-start | bytes 245764
  82.2 0.9 copy-start.5
  83.1 1.1 copy-start.7
  88.9 0.8 copy-start.8
  89.7 6.4 %collective-permute-start.6 = (f32[2,4,4,256]{3,2,1,0:T(4,128)S(1)}, f32[2,4,4,256]{3,2,1,0:T(4,128)S(1)}, u32[]{:S(2)}, u32[]{:S(2)}) collective-permute-start(f32[2,4,4,256]{3,2,1,0:T(4,128)S(1)} %get-tuple-element.56), channel_id=1, source_target_pairs={{0,32},{32,0},{64,96},{96,64},{128,160},{160,128},{192,224},{224,1... | collective-permute-start | bytes 98312 | tf_op jit(solution)/shard_map/ppermute | solution.py:591
  96.1 10.3 %collective-permute-start.7 = (f32[2,4,4,256]{3,2,1,0:T(4,128)S(1)}, f32[2,4,4,256]{3,2,1,0:T(4,128)S(1)}, u32[]{:S(2)}, u32[]{:S(2)}) collective-permute-start(f32[2,4,4,256]{3,2,1,0:T(4,128)S(1)} %reverse_add_fusion), channel_id=1, source_target_pairs={{0,1},{1,2},{2,3},{3,4},{4,5},{5,6},{6,7},{7,8},{8,9},{9,10},{10,1... | collective-permute-start | bytes 98312 | tf_op jit(solution)/shard_map/ppermute | solution.py:600
  98.1 1.1 copy-start.6
  99.2 1.0 copy-start.9
  102.6 5.0 %collective-permute-start.5 = (f32[4,64,256]{2,1,0:T(8,128)S(1)}, f32[4,64,256]{2,1,0:T(8,128)S(1)}, u32[]{:S(2)}, u32[]{:S(2)}) collective-permute-start(f32[4,64,256]{2,1,0:T(8,128)S(1)} %get-tuple-element.54), channel_id=1, source_target_pairs={{0,32},{32,0},{64,96},{96,64},{128,160},{160,128},{192,224},{224,1... | collective-permute-start | bytes 786440 | tf_op jit(solution)/shard_map/ppermute | solution.py:591
  106.4 1.2 collective-permute-start.8
  108.2 3.6 %collective-permute-start.9 = (f32[64,256]{1,0:T(8,128)S(1)}, f32[64,256]{1,0:T(8,128)S(1)}, u32[]{:S(2)}, u32[]{:S(2)}) collective-permute-start(f32[64,256]{1,0:T(8,128)S(1)} %get-tuple-element.58), channel_id=1, source_target_pairs={{0,64},{32,96},{64,0},{96,32},{128,192},{160,224},{192,128},{224,1... | collective-permute-start | bytes 196616 | tf_op jit(solution)/shard_map/ppermute | solution.py:591
  109.0 5.0 %collective-permute-start.10 = (f32[64,256]{1,0:T(8,128)S(1)}, f32[64,256]{1,0:T(8,128)S(1)}, u32[]{:S(2)}, u32[]{:S(2)}) collective-permute-start(f32[64,256]{1,0:T(8,128)S(1)} %get-tuple-element.59), channel_id=1, source_target_pairs={{0,128},{32,160},{64,192},{96,224},{128,0},{160,32},{192,64},{224,... | collective-permute-start | bytes 196616 | tf_op jit(solution)/shard_map/ppermute | solution.py:591
  110.0 5.3 %collective-permute-start.11 = (f32[64,256]{1,0:T(8,128)S(1)}, f32[64,256]{1,0:T(8,128)S(1)}, u32[]{:S(2)}, u32[]{:S(2)}) collective-permute-start(f32[64,256]{1,0:T(8,128)S(1)} %get-tuple-element.60), channel_id=1, source_target_pairs={{0,192},{32,224},{64,128},{96,160},{128,64},{160,96},{192,0},{224,... | collective-permute-start | bytes 196616 | tf_op jit(solution)/shard_map/ppermute | solution.py:591
  116.2 5.0 %collective-permute-start.14 = (f32[64,256]{1,0:T(8,128)S(1)}, f32[64,256]{1,0:T(8,128)S(1)}, u32[]{:S(2)}, u32[]{:S(2)}) collective-permute-start(f32[64,256]{1,0:T(8,128)S(1)} %divide_multiply_fusion.refs_0_), channel_id=1, source_target_pairs={{0,192},{32,224},{64,128},{96,160},{128,64},{160,96},{192,0},{224,... | collective-permute-start | bytes 196616 | tf_op jit(solution)/shard_map/ppermute | solution.py:591
  117.9 7.2 %collective-permute-start.13 = (f32[64,256]{1,0:T(8,128)S(1)}, f32[64,256]{1,0:T(8,128)S(1)}, u32[]{:S(2)}, u32[]{:S(2)}) collective-permute-start(f32[64,256]{1,0:T(8,128)S(1)} %divide_multiply_fusion.refs_0_), channel_id=1, source_target_pairs={{0,128},{32,160},{64,192},{96,224},{128,0},{160,32},{192,64},{224,... | collective-permute-start | bytes 196616 | tf_op jit(solution)/shard_map/ppermute | solution.py:591
  120.0 5.1 %collective-permute-start.12 = (f32[64,256]{1,0:T(8,128)S(1)}, f32[64,256]{1,0:T(8,128)S(1)}, u32[]{:S(2)}, u32[]{:S(2)}) collective-permute-start(f32[64,256]{1,0:T(8,128)S(1)} %divide_multiply_fusion.refs_0_), channel_id=1, source_target_pairs={{0,64},{32,96},{64,0},{96,32},{128,192},{160,224},{192,128},{224,1... | collective-permute-start | bytes 196616 | tf_op jit(solution)/shard_map/ppermute | solution.py:591
  125.1 3.0 %collective-permute-start.15 = (f32[4,64,256]{2,1,0:T(8,128)S(1)}, f32[4,64,256]{2,1,0:T(8,128)S(1)}, u32[]{:S(2)}, u32[]{:S(2)}) collective-permute-start(f32[4,64,256]{2,1,0:T(8,128)S(1)} %pad_maximum_fusion), channel_id=1, source_target_pairs={{0,32},{32,0},{64,96},{96,64},{128,160},{160,128},{192,224},{224,1... | collective-permute-start | bytes 786440 | tf_op jit(solution)/shard_map/ppermute | solution.py:591
  (1 other events, 0.6 us)

commit v4 on v3

--- a/solution.py
+++ b/solution.py
@@ -11,6 +11,7 @@
 bf16 = jnp.bfloat16
 LANES = 128
 MIRROR = 6
+LASTS = 4
 VMEM = pl.BlockSpec(memory_space=pltpu.VMEM)
 SMEM = pl.BlockSpec(memory_space=pltpu.SMEM)
 HBM = pl.BlockSpec(memory_space=pltpu.HBM)
@@ -40,10 +41,9 @@
                 o_ref[s, slot, :, cols] = flat[pl.ds(first + s, rows, stride=slabs), :]
 
 
-def relay(half, measured, sides, first_view, views, count, into=None, slot=0, slots=None, after=(), cost=SMALL):
+def relay(half, measured, sides, first_view, views, count, slots, into=None, slot=0, step=1, after=()):
     segs, _, inner, slabs, bins = measured.shape
     rows = segs * inner
-    slots = len(sides) if slots is None else slots
     specs = [
         pl.BlockSpec((segs, 1, inner, slabs, LANES), lambda v, lane=lane: (0, first_view + v, 0, 0, lane))
         for lane in range(lane_blocks(bins))
@@ -60,11 +60,11 @@
         functools.partial(relay_kernel, sides, lanes),
         grid=(views,),
         in_specs=specs,
-        out_specs=pl.BlockSpec((count, len(sides), rows, bins), lambda v: (0, v * slots // len(sides) + slot, 0, 0)),
-        out_shape=jax.ShapeDtypeStruct((count, views * slots, rows, bins), f32),
+        out_specs=pl.BlockSpec((count, len(sides), rows, bins), lambda v: (0, slot + step * v, 0, 0)),
+        out_shape=jax.ShapeDtypeStruct((count, slots, rows, bins), f32),
         input_output_aliases=aliases,
         compiler_params=params(52),
-        cost_estimate=cost,
+        cost_estimate=SMALL,
     )(*operands)
 
 
@@ -219,7 +219,7 @@
         ]
         + lanes,
         out_specs=pl.BlockSpec((1, 2, rows // inner // 2, inner, bins), lambda v: (v, 0, 0, 0, 0)),
-        out_shape=jax.ShapeDtypeStruct((views, 2, rows // inner // 2, inner, bins), f32),
+        out_shape=pltpu.HBM((views, 2, rows // inner // 2, inner, bins), f32),
         scratch_shapes=[pltpu.VMEM(footprint.shape, footprint.dtype), pltpu.VMEM((rows, pixels), bf16)]
         + [pltpu.VMEM((rows, LANES), f32)] * len(lanes)
         + [pltpu.VMEM((operator.shape[1], pixels), f32), pltpu.SemaphoreType.DMA((views,))],
@@ -258,29 +258,25 @@
     factor_hbm,
     foot_hbm,
     acc_ref,
-    last_factor_ref,
-    last_foot_ref,
     own_ref,
     factor_ref,
     foot_ref,
     sems,
 ):
     half = half_ref[0]
-    views, count, inner, bins = own_ref.shape
+    views, _, count, inner, bins = factor_ref.shape
+    bare = views - own_ref.shape[0]
     firsts = factor_hbm.shape[0] - views
-    middles = foot_ref.shape[0]
-
-    def place(v):
-        if v < middles:
-            return factor_ref.at[v], foot_ref.at[v]
-        return last_factor_ref.at[v - middles], last_foot_ref.at[v - middles]
+    middles = (part_ref.shape[0] - 2 * edge * views) // (count - 2 * edge)
 
     def copies(v):
-        factor, foot = place(v)
-        return [
-            pltpu.make_async_copy(staged_hbm.at[:, 2 * v], own_ref.at[v], sems.at[v, 0]),
-            pltpu.make_async_copy(factor_hbm.at[firsts + v], factor, sems.at[v, 1]),
-            pltpu.make_async_copy(foot_hbm.at[firsts + v], foot, sems.at[v, 2]),
+        own = []
+        if v >= bare:
+            slot = bare + 2 * (v - bare)
+            own = [pltpu.make_async_copy(staged_hbm.at[:, slot], own_ref.at[v - bare], sems.at[v, 0])]
+        return own + [
+            pltpu.make_async_copy(factor_hbm.at[firsts + v], factor_ref.at[v], sems.at[v, 1]),
+            pltpu.make_async_copy(foot_hbm.at[firsts + v], foot_ref.at[v], sems.at[v, 2]),
         ]
 
     for v in range(views):
@@ -289,9 +285,11 @@
     for v in range(views):
         for copy in copies(v):
             copy.wait()
-        factor, foot = place(v)
-        far = factor[1 - half]
-        own = ratio(factor[half], own_ref[v])
+        far = factor_ref[v, 1 - half]
+        if v >= bare:
+            own = ratio(factor_ref[v, half], own_ref[v - bare])
+        else:
+            own = jnp.zeros((count * inner, bins), bf16)
         low = ratio(far[:edge], part_ref[2 * edge * v : 2 * edge * v + edge])
         high = ratio(far[count - edge :], part_ref[2 * edge * v + edge : 2 * edge * (v + 1)])
         if v < middles:
@@ -299,31 +297,26 @@
             middle = ratio(far[edge : count - edge], part_ref[first : first + count - 2 * edge])
         else:
             middle = jnp.zeros(((count - 2 * edge) * inner, bins), bf16)
-        spread = back_project(operator, jnp.concatenate([own, low, middle, high], axis=0), foot[...])
+        spread = back_project(operator, jnp.concatenate([own, low, middle, high], axis=0), foot_ref[v])
         if v == 0:
             acc_ref[...] = spread
         else:
             acc_ref[...] += spread
 
 
-def back_staged(half, operator, staged, part, factor, footprint, edge, lasts):
+def back_staged(half, operator, staged, part, factor, footprint, edge, views):
     ext = operator.shape[1]
     count, slots, inner, bins = staged.shape
-    views = slots // 2
     pixels = footprint.shape[1]
     return pl.pallas_call(
         functools.partial(back_staged_kernel, edge),
         in_specs=[SMEM, VMEM, HBM, VMEM, HBM, HBM],
-        out_specs=[VMEM] * 3,
-        out_shape=[
-            jax.ShapeDtypeStruct((ext, pixels), f32),
-            pltpu.VMEM((lasts, 2, count, inner, bins), f32),
-            pltpu.VMEM((lasts, pixels, bins), bf16),
-        ],
+        out_specs=VMEM,
+        out_shape=pltpu.VMEM((ext, pixels), f32),
         scratch_shapes=[
-            pltpu.VMEM((views, count, inner, bins), f32),
-            pltpu.VMEM((views - lasts, 2, count, inner, bins), f32),
-            pltpu.VMEM((views - lasts, pixels, bins), bf16),
+            pltpu.VMEM((slots - views, count, inner, bins), f32),
+            pltpu.VMEM((views, 2, count, inner, bins), f32),
+            pltpu.VMEM((views, pixels, bins), bf16),
             pltpu.SemaphoreType.DMA((views, 3)),
         ],
         compiler_params=params(52),
@@ -336,11 +329,15 @@
 ):
     near_ref, factor_ref, foot_ref, sum_ref, sems = scratch
     half = half_ref[0]
-    views = near_ref.shape[0]
+    views = factor_ref.shape[0]
+    firsts = near_hbm.shape[1] - views
 
     def copies(v):
+        slot, size = (2 * v, 2) if v < firsts else (firsts + v, 1)
         return [
-            pltpu.make_async_copy(near_hbm.at[:, pl.ds(2 * v, 2)], near_ref.at[v], sems.at[v, 0]),
+            pltpu.make_async_copy(
+                near_hbm.at[:, pl.ds(slot, size)], near_ref.at[:, pl.ds(slot, size)], sems.at[v, 0]
+            ),
             pltpu.make_async_copy(factor_hbm.at[v], factor_ref.at[v], sems.at[v, 1]),
             pltpu.make_async_copy(foot_hbm.at[v], foot_ref.at[v], sems.at[v, 2]),
         ]
@@ -352,8 +349,12 @@
     for v in range(views):
         for copy in copies(v):
             copy.wait()
-        own = ratio(factor_ref[v, half], near_ref[v, :, 0])
-        far = ratio(factor_ref[v, 1 - half], near_ref[v, :, 1])
+        if v < firsts:
+            own = ratio(factor_ref[v, half], near_ref[:, 2 * v])
+            far = ratio(factor_ref[v, 1 - half], near_ref[:, 2 * v + 1])
+        else:
+            own = ratio(factor_ref[v, half], near_ref[:, firsts + v])
+            far = jnp.zeros_like(own)
         sum_ref[...] += back_project(operator, jnp.concatenate([own, far], axis=0), foot_ref[v])
     slices, pixels = acc_ref.shape
     margin, width = keep_ref.shape[2:]
@@ -369,9 +370,8 @@
             give_ref[c, k] = jnp.where(core == 0, up, down)
 
 
-def back_near(half, me, operator, near, factor, footprint, acc, slices, margin):
+def back_near(half, me, operator, near, factor, footprint, acc, slices, margin, views):
     count, slots, inner, bins = near.shape
-    views = slots // 2
     pixels = footprint.shape[1]
     halo = jax.ShapeDtypeStruct((2, 4, margin, pixels // 8), f32)
     return pl.pallas_call(
@@ -380,7 +380,7 @@
         out_specs=[VMEM] * 3,
         out_shape=[jax.ShapeDtypeStruct((slices, pixels), f32), halo, halo],
         scratch_shapes=[
-            pltpu.VMEM((views, count, 2, inner, bins), f32),
+            pltpu.VMEM((count, slots, inner, bins), f32),
             pltpu.VMEM((views, 2, count, inner, bins), f32),
             pltpu.VMEM((views, pixels, bins), bf16),
             pltpu.VMEM(acc.shape, f32),
@@ -391,15 +391,20 @@
     )(half, me, operator, near, factor, footprint, acc)
 
 
+def far_slot(v, views, slots):
+    bare = 2 * views - slots
+    return v if v < bare else bare + 2 * (v - bare) + 1
+
+
 def part_kernel(edge, views, staged_hbm, part_ref, sems):
-    count = staged_hbm.shape[0]
+    count, slots = staged_hbm.shape[:2]
     middle = count - 2 * edge
     copies = []
 
     def add(first, size, v, place):
         copies.append(
             pltpu.make_async_copy(
-                staged_hbm.at[pl.ds(first, size), 2 * v + 1],
+                staged_hbm.at[pl.ds(first, size), far_slot(v, views, slots)],
                 part_ref.at[pl.ds(place, size)],
                 sems.at[len(copies)],
             )
@@ -415,9 +420,8 @@
         copy.wait()
 
 
-def part_of(staged, edge, lasts):
+def part_of(staged, edge, views, lasts):
     count, slots, inner, bins = staged.shape
-    views = slots // 2
     part = 2 * edge * views + (count - 2 * edge) * (views - lasts)
     return pl.pallas_call(
         functools.partial(part_kernel, edge, views),
@@ -430,12 +434,14 @@
     )(staged)
 
 
-def last_kernel(edge, staged_hbm, _, last_ref, sems):
-    views = staged_hbm.shape[1] // 2
+def last_kernel(edge, views, staged_hbm, _, last_ref, sems):
+    slots = staged_hbm.shape[1]
     middle, lasts = last_ref.shape[:2]
     copies = [
         pltpu.make_async_copy(
-            staged_hbm.at[pl.ds(edge, middle), 2 * (views - lasts + v) + 1], last_ref.at[:, v], sems.at[v]
+            staged_hbm.at[pl.ds(edge, middle), far_slot(views - lasts + v, views, slots)],
+            last_ref.at[:, v],
+            sems.at[v],
         )
         for v in range(lasts)
     ]
@@ -444,10 +450,10 @@
         copy.wait()
 
 
-def last_of(staged, edge, lasts, after):
+def last_of(staged, edge, views, lasts, after):
     count, _, inner, bins = staged.shape
     return pl.pallas_call(
-        functools.partial(last_kernel, edge),
+        functools.partial(last_kernel, edge, views),
         in_specs=[HBM, pl.BlockSpec(memory_space=pl.ANY)],
         out_specs=VMEM,
         out_shape=pltpu.VMEM((count - 2 * edge, lasts, inner, bins), f32),
@@ -493,18 +499,30 @@
     )(x)
 
 
-def back_last_kernel(half_ref, me_ref, op_ref, x_ref, factor_ref, foot_ref, in_ref, *refs):
-    mine_refs, other_ref, acc_ref = refs[:4], refs[4], refs[5]
+def back_last_kernel(half_ref, me_ref, op_ref, x_ref, factor_hbm, foot_hbm, in_ref, *refs):
+    mine_refs, (other_ref, acc_ref, factor_ref, foot_ref, sems) = refs[:4], refs[4:]
     slices, pixels = acc_ref.shape
     middle, views, inner, bins = x_ref.shape
-    count = factor_ref.shape[2]
+    count = factor_ref.shape[1]
     edge = (count - middle) // 2
     far = 1 - half_ref[0]
+    first = factor_hbm.shape[0] - views
+
+    def copies(v):
+        return [
+            pltpu.make_async_copy(factor_hbm.at[first + v, far], factor_ref.at[v], sems.at[v, 0]),
+            pltpu.make_async_copy(foot_hbm.at[first + v], foot_ref.at[v], sems.at[v, 1]),
+        ]
+
+    for v in range(views):
+        start_all(copies(v))
     gap = jnp.zeros((edge * inner, bins), bf16)
     operator = op_ref[far, :slices]
     acc_ref[...] = in_ref[...]
     for v in range(views):
-        weighted = ratio(factor_ref[v, far, edge : count - edge], x_ref[:, v])
+        for copy in copies(v):
+            copy.wait()
+        weighted = ratio(factor_ref[v, edge : count - edge], x_ref[:, v])
         acc_ref[...] += back_project(operator, jnp.concatenate([gap, weighted, gap], axis=0), foot_ref[v])
     width = mine_refs[0].shape[1]
     for k in range(4):
@@ -520,13 +538,19 @@
 def back_last(half, me, operator, rows_in, factor, footprint, acc):
     slices, pixels = acc.shape
     width = pixels // 8
+    _, views, inner, bins = rows_in.shape
     return pl.pallas_call(
         back_last_kernel,
-        in_specs=[SMEM, SMEM] + [VMEM] * 5,
+        in_specs=[SMEM, SMEM, VMEM, VMEM, HBM, HBM, VMEM],
         out_specs=[VMEM] * 5,
         out_shape=[pltpu.VMEM((slices, width), f32)] * 4 + [pltpu.VMEM((4, slices, width), f32)],
-        scratch_shapes=[pltpu.VMEM((slices, pixels), f32)],
-        compiler_params=params(24),
+        scratch_shapes=[
+            pltpu.VMEM((slices, pixels), f32),
+            pltpu.VMEM((views, factor.shape[2], inner, bins), f32),
+            pltpu.VMEM((views, pixels, bins), bf16),
+            pltpu.SemaphoreType.DMA((views, 2)),
+        ],
+        compiler_params=params(52),
         cost_estimate=SMALL,
     )(half, me, operator, rows_in, factor, footprint, acc)
 
@@ -603,8 +627,8 @@
     slab = lax.axis_index("slab").astype(jnp.int32)
     half = (slab // count).reshape(1)
     edge = margin // inner
-    firsts = views // 2
-    lasts = 2
+    firsts, bare, lasts = 3, 2, LASTS
+    behind = views - firsts
 
     def cross(x):
         return lax.ppermute(x, "slab", [(i, (i + count) % slabs) for i in range(slabs)])
@@ -615,10 +639,14 @@
 
     ext = slices + 2 * margin
     early = cross(crossing(half, measured, firsts))
-    staged = relay(half, measured, (0, 1), firsts, views - firsts, count)
+    staged = relay(half, measured, (1,), firsts, bare, count, 2 * behind - bare)
+    staged = relay(
+        half, measured, (0, 1), firsts + bare, behind - bare, count, 2 * behind - bare, into=staged, slot=bare // 2
+    )
     staged, near_activity = lax.optimization_barrier((staged, activity))
     staged = exchange(staged)
-    near = relay(half, measured, (0,), 0, firsts, count, slots=2, cost=SMALL)
+    near = relay(half, measured, (0,), 0, firsts, count, 2 * firsts + bare, step=2)
+    near = relay(half, measured, (0,), firsts, bare, count, 2 * firsts + bare, into=near, slot=2 * firsts)
     efficiency, operator, operator_t = setup(me, kernel, dead_counts, crystals, slices, segs, inner, halves)
     even = group % 2 == 0
     above = shift(near_activity[slices - margin :], ())
@@ -626,19 +654,19 @@
     staged, near, begun, efficiency, operator, operator_t, above, below = lax.optimization_barrier(
         (staged, near, mark(early), efficiency, operator, operator_t, above, below)
     )
-    part = cross(part_of(staged, edge, lasts))
-    near = relay(half, early, (1,), 0, firsts, count, into=near, slot=1, slots=2, after=[begun])
-    rows_last = cross(last_of(staged, edge, lasts, near))
+    part = cross(part_of(staged, edge, behind, lasts))
+    near = relay(
+        half, early, (1,), 0, firsts, count, 2 * firsts + bare, into=near, slot=1, step=2, after=[begun]
+    )
+    rows_last = cross(last_of(staged, edge, behind, lasts, near))
     near = exchange(near)
     factor = forward(operator, activity, above, below, footprint, randoms, efficiency)
 
-    acc, last_factor, last_foot = back_staged(
-        half, operator_t, staged, part, factor, footprint, edge, lasts
-    )
-    acc, keep, give = back_near(half, me, operator_t, near, factor, footprint, acc, slices, margin)
+    acc = back_staged(half, operator_t, staged, part, factor, footprint, edge, behind)
+    acc, keep, give = back_near(half, me, operator_t, near, factor, footprint, acc, slices, margin, firsts + bare)
     halo = shift(keep + swap(give, 1)[::-1], (1,))
     across = swap(halo[1], 1)
-    *mine, other = back_last(half, me, operator_t, rows_last, last_factor, last_foot, acc)
+    *mine, other = back_last(half, me, operator_t, rows_last, factor, footprint, acc)
     sides = [jnp.where(even, slab == count, slab == count - 1), jnp.where(even, slab == count - 1, slab == count)]
     flip = jnp.where(jnp.stack(sides), MIRROR // 2, 0).astype(jnp.int32)
     pair = pair_sum(me, flip, mine, swap(other, 1), halo, across)

time: 130 us -> 126 us (0.969)
  local copies, waits for them, and re-layouts: 11.4 us -> 2.81 us
  Pallas kernels: 43.2 us -> 48.3 us
    unnamed x30 -> x14, local copies, waits for them, and re-layouts: 9.77 us -> 1.17 us
    all_to_all x2, starting transfers between devices: 20.4 us -> 12.7 us  [exchange(): lax.all_to_all(x, 'slab', split_axis=0, concat_axis=0, tiled=True, axis_i...]
    ppermute x3, starting transfers between devices: 7.21 us -> 12.5 us  [cross(): lax.ppermute(x, 'slab', [(i, (i + count) % slabs) for i in range(slabs)])]
    pallas_call x2, Pallas kernels: 4.09 us -> 7.36 us  [the longest x1 5.19 us: back_last(): pl.pallas_call(back_last_kernel, in_specs=[SMEM, SMEM, VMEM, VMEM, HBM, H...]
    pallas_call x3 -> x5, Pallas kernels: 8.44 us -> 11 us  [relay(): pl.pallas_call(functools.partial(relay_kernel, sides, lanes), grid=(views...]
    ppermute x10, starting transfers between devices: 18.9 us -> 20.9 us  [swap(): return lax.ppermute(x, 'seg', [(i, i ^ k) for i in range(2 * halves)])]
    pallas_call x1, Pallas kernels: 6.53 us -> 5.17 us  [back_staged(): pl.pallas_call(functools.partial(back_staged_kernel, edge), in_specs=[SME...]
  transfers between devices with their start and end apart: 18 -> 18, of which waited for: 9 -> 8; matrix products, arithmetic and copies ran while one was open for 1% -> 1% of each run, Pallas kernels for 30% -> 35%
where the time goes in v4:
time: 126 us
  starting transfers between devices  59.1 us (47%)
  Pallas kernels  48.3 us (38%)
  waiting for transfers between devices  14.2 us (11%)
  local copies, waits for them, and re-layouts  2.81 us (2%)
    ppermute x10, starting transfers between devices, swap(): return lax.ppermute(x, 'seg', [(i, i ^ k) for i in range(2 * halves)])  20.9 us
    ppermute x3, starting transfers between devices, shift(): return lax.ppermute(x, ('seg', 'slab'), pairs)  12.9 us
    all_to_all x2, starting transfers between devices, exchange(): lax.all_to_all(x, 'slab', split_axis=0, concat_axis=0, tiled=True, axis_i...  12.7 us
    ppermute x3, starting transfers between devices, cross(): lax.ppermute(x, 'slab', [(i, (i + count) % slabs) for i in range(slabs)])  12.5 us
    ppermute x10, waiting for transfers between devices, swap(): return lax.ppermute(x, 'seg', [(i, i ^ k) for i in range(2 * halves)])  11.8 us
    pallas_call x5, Pallas kernels, relay(): pl.pallas_call(functools.partial(relay_kernel, sides, lanes), grid=(views...  11 us
    pallas_call x1, Pallas kernels, forward(): pl.pallas_call(forward_kernel, grid=(views,), in_specs=[VMEM, VMEM, VMEM,...  9.7 us
    pallas_call x1, Pallas kernels, setup(): pl.pallas_call(functools.partial(setup_kernel, slices, segs, inner, halve...  5.97 us
  transfers between devices with their start and end apart: 18, of which 8 were waited for; matrix products, arithmetic and copies ran while one was open for 1% of the time, Pallas kernels for 35%

profile of v4, /device:TPU:31, one launch (start us, length us, event | category | flops | bytes accessed | tf_op | source)
XLA Modules:
  0.0 125.7 jit_solution(8982641705961792036)
XLA Ops:
  1.1 7.0 %collective-permute-start = (f32[4,3,2,16,384]{4,3,2,1,0:T(8,128)S(1)}, f32[4,3,2,16,384]{4,3,2,1,0:T(8,128)S(1)}, u32[]{:S(2)}, u32[]{:S(2)}) collective-permute-start(f32[4,3,2,16,384]{4,3,2,1,0:T(8,128)S(1)} %shard_map.86), channel_id=1, source_target_pairs={{0,16},{1,17},{2,18},{3,19},{4,20},{5,21},{6,22},{7,23},{8,24},{9,... | collective-permute-start | bytes 1769480 | tf_op jit(solution)/shard_map/ppermute | solution.py:634
  8.1 2.0 %shard_map.82.refs_3_ = f32[16,8,8,384]{3,2,1,0:T(8,128)} custom-call(s32[1]{0:T(128)} %bitcast.3.half_ref, f32[4,8,2,32,384]{4,3,2,1,0:T(8,128)} %m_hbm.1, f32[4,8,2,32,384]{4,3,2,1,0:T(8,128)} %m_hbm.1, f32[4,8,2,32,384]{4,3,2,1,0:T(8,128)} %m_hbm.1), custom_call_target="tpu_custom_call" | custom-call | flops 1 | bytes 1 | tf_op jit(solution)/shard_map/pallas_call | solution.py:59
  10.1 3.6 %shard_map.83 = f32[16,8,8,384]{3,2,1,0:T(8,128)} custom-call(s32[1]{0:T(128)} %bitcast.3.half_ref, f32[4,8,2,32,384]{4,3,2,1,0:T(8,128)} %m_hbm.1, f32[4,8,2,32,384]{4,3,2,1,0:T(8,128)} %m_hbm.1, f32[4,8,2,32,384]{4,3,2,1,0:T(8,128)} %m_hbm.1, f32[16,8,8,384]{3,2,1,0:T(8,128)} %shard_map.82.refs_3_), custom_call_target="tpu_custom_call", output_to_operand_aliasing={{}: (4, {})} | custom-call | flops 1 | bytes 1 | tf_op jit(solution)/shard_map/pallas_call | solution.py:59
  13.7 6.5 %all-to-all-start = ((f32[16,8,8,384]{3,2,1,0:T(8,128)}), f32[16,8,8,384]{3,2,1,0:T(8,128)}, u32[]{:S(2)}, u32[]{:S(2)}) async-start(f32[16,8,8,384]{3,2,1,0:T(8,128)} %shard_map.83), calls=%async_computation | async-start | bytes 3145728 | tf_op jit(solution)/shard_map/all_to_all | solution.py:638
  20.2 1.5 %fusion = (f32[4,2048]{1,0:T(4,128)}, f32[4,2048]{1,0:T(4,128)}) fusion(f32[64,2048]{1,0:T(8,128)} %act_ref.1), kind=kLoop, calls=%fused_computation.5 | loop fusion | bytes 131072 | tf_op jit(solution)/shard_map/slice | solution.py:653
  21.7 2.5 %collective-permute-start.2 = (f32[4,2048]{1,0:T(4,128)}, f32[4,2048]{1,0:T(4,128)}, u32[]{:S(2)}, u32[]{:S(2)}) collective-permute-start(f32[4,2048]{1,0:T(4,128)} %get-tuple-element.55), channel_id=1, source_target_pairs={{1,0},{2,1},{3,2},{4,3},{5,4},{6,5},{7,6},{8,7},{9,8},{10,9},{11,1... | collective-permute-start | bytes 98312 | tf_op jit(solution)/shard_map/ppermute | solution.py:624
  24.2 2.4 %shard_map.84.refs_3_ = f32[16,8,8,384]{3,2,1,0:T(8,128)S(1)} custom-call(s32[1]{0:T(128)} %bitcast.3.half_ref, f32[4,8,2,32,384]{4,3,2,1,0:T(8,128)} %m_hbm.1, f32[4,8,2,32,384]{4,3,2,1,0:T(8,128)} %m_hbm.1, f32[4,8,2,32,384]{4,3,2,1,0:T(8,128)} %m_hbm.1), custom_call_target="tpu_custom_call" | custom-call | flops 1 | bytes 1 | tf_op jit(solution)/shard_map/pallas_call | solution.py:59
  26.7 8.4 %collective-permute-start.1 = (f32[4,2048]{1,0:T(4,128)}, f32[4,2048]{1,0:T(4,128)}, u32[]{:S(2)}, u32[]{:S(2)}) collective-permute-start(f32[4,2048]{1,0:T(4,128)} %get-tuple-element.56), channel_id=1, source_target_pairs={{0,1},{1,2},{2,3},{3,4},{4,5},{5,6},{6,7},{7,8},{8,9},{9,10},{10,1... | collective-permute-start | bytes 98312 | tf_op jit(solution)/shard_map/ppermute | solution.py:624
  35.0 1.4 %shard_map.85.refs_3_ = f32[16,8,8,384]{3,2,1,0:T(8,128)S(1)} custom-call(s32[1]{0:T(128)} %bitcast.3.half_ref, f32[4,8,2,32,384]{4,3,2,1,0:T(8,128)} %m_hbm.1, f32[4,8,2,32,384]{4,3,2,1,0:T(8,128)} %m_hbm.1, f32[4,8,2,32,384]{4,3,2,1,0:T(8,128)} %m_hbm.1, f32[16,8,8,384]{3,2,1,0:T(8,128)S(1)} %shard_map.84.refs_3_), custom_call_target="tpu_custom_call", output_to_operand_aliasing={{}: (4, {})} | custom-call | flops 1 | bytes 1 | tf_op jit(solution)/shard_map/pallas_call | solution.py:59
  36.4 1.1 copy-done
  37.8 6.0 %shard_map.88 = (f32[8,1,384]{2,1,0:T(1,128)S(1)}, f32[256,80]{1,0:T(8,128)S(1)}, f32[2,80,128]{2,1,0:T(8,128)S(1)}) custom-call(s32[1]{0:T(128)} %bitcast.me_ref, f32[16,9]{1,0:T(8,128)S(1)} %copy-done.4, s32[128,512]{1,0:T(8,128)S(1)} %bitcast.12, s32[2,8,1,384]{3,2,1,0:T(1,128)S(1)} %reshape.15.c_ref), custom_call_target="tpu_custom_call" | custom-call | flops 1 | bytes 1 | tf_op jit(solution)/shard_map/pallas_call | solution.py:145
  43.8 1.2 shard_map.92
  45.1 1.6 %shard_map.89._ = f32[16,8,8,384]{3,2,1,0:T(8,128)} custom-call(s32[1]{0:T(128)} %bitcast.3.half_ref, f32[4,3,2,16,384]{4,3,2,1,0:T(8,128)S(1)} %collective-permute-done.x_ref.refs_0_.refs_1_.refs_2_, f32[4,3,2,16,384]{4,3,2,1,0:T(8,128)S(1)} %collective-permute-done.x_ref.refs_0_.refs_1_.refs_2_, ...), custom_call_target="tpu_custom_call", output_to_operand_aliasing={{}: (4, {})} | custom-call | flops 1 | bytes 1 | tf_op jit(solution)/shard_map/pallas_call | solution.py:59
  46.7 6.2 %all-to-all-start.1 = ((f32[16,8,8,384]{3,2,1,0:T(8,128)}), f32[16,8,8,384]{3,2,1,0:T(8,128)}, u32[]{:S(2)}, u32[]{:S(2)}) async-start(f32[16,8,8,384]{3,2,1,0:T(8,128)} %shard_map.89._), calls=%async_computation.1 | async-start | bytes 3145728 | tf_op jit(solution)/shard_map/all_to_all | solution.py:638
  53.0 2.2 %shard_map.90 = f32[12,4,8,384]{3,2,1,0:T(8,128)} custom-call(f32[16,8,8,384]{3,2,1,0:T(8,128)} %all-to-all-done.staged_hbm, f32[16,8,8,384]{3,2,1,0:T(8,128)S(1)} %copy-done.1), custom_call_target="tpu_custom_call" | custom-call | flops 1 | bytes 1 | tf_op jit(solution)/shard_map/pallas_call | solution.py:455
  55.1 5.4 %collective-permute-start.3 = (f32[12,4,8,384]{3,2,1,0:T(8,128)}, f32[12,4,8,384]{3,2,1,0:T(8,128)}, u32[]{:S(2)}, u32[]{:S(2)}) collective-permute-start(f32[12,4,8,384]{3,2,1,0:T(8,128)} %shard_map.90), channel_id=1, source_target_pairs={{0,16},{1,17},{2,18},{3,19},{4,20},{5,21},{6,22},{7,23},{8,24},{9,... | collective-permute-start | bytes 1769480 | tf_op jit(solution)/shard_map/ppermute | solution.py:634
  60.6 9.7 %shard_map.91.factor_hbm = f32[8,2,16,8,384]{4,3,2,1,0:T(8,128)} custom-call(f32[256,80]{1,0:T(8,128)S(1)} %get-tuple-element.39.op_ref, f32[64,2048]{1,0:T(8,128)S(1)} %copy-done.3, f32[4,2048]{1,0:T(4,128)} %collective-permute-done.1.above_ref, f32[4,2048]{1,0:T(4,128)} %collective-permute-done.2.below_ref, bf16[8,2048,384]{2,1,0:T(8,128)(2,1)} %foot_hbm.7, ...), custom_call_target="tpu_custom_call" | custom-call | flops 1 | bytes 1 | tf_op jit(solution)/shard_map/pallas_call | solution.py:209
  70.3 5.2 %shard_map.93.in_ref = f32[80,2048]{1,0:T(8,128)S(1)} custom-call(s32[1]{0:T(128)} %bitcast.3.half_ref, f32[2,80,128]{2,1,0:T(8,128)S(1)} %get-tuple-element.35.op_ref, f32[16,8,8,384]{3,2,1,0:T(8,128)} %all-to-all-done.staged_hbm, f32[32,8,384]{2,1,0:T(8,128)S(1)} %collective-permute-done.4.part_ref, f32[8,2,16,8,384]{4,3,2,1,0:T(8,128)} %shard_map.91.factor_hbm, ...), custom_call_target="tpu_custom_call" | custom-call | flops 999999995904 | bytes 1048576 | tf_op jit(solution)/shard_map/pallas_call | solution.py:311
  75.5 5.3 %shard_map.94 = (f32[64,2048]{1,0:T(8,128)S(1)}, f32[2,4,4,256]{3,2,1,0:T(4,128)S(1)}, f32[2,4,4,256]{3,2,1,0:T(4,128)S(1)}) custom-call(s32[1]{0:T(128)} %bitcast.3.half_ref, s32[1]{0:T(128)} %bitcast.me_ref, f32[2,80,128]{2,1,0:T(8,128)S(1)} %get-tuple-element.35.op_ref, f32[16,8,8,384]{3,2,1,0:T(8,128)} %all-to-all-done.1.near_hbm, ...), custom_call_target="tpu_custom_call" | custom-call | flops 1 | bytes 1 | tf_op jit(solution)/shard_map/pallas_call | solution.py:377
  80.8 11.6 %collective-permute-start.6 = (f32[2,4,4,256]{3,2,1,0:T(4,128)S(1)}, f32[2,4,4,256]{3,2,1,0:T(4,128)S(1)}, u32[]{:S(2)}, u32[]{:S(2)}) collective-permute-start(f32[2,4,4,256]{3,2,1,0:T(4,128)S(1)} %get-tuple-element.50), channel_id=1, source_target_pairs={{0,32},{32,0},{64,96},{96,64},{128,160},{160,128},{192,224},{224,1... | collective-permute-start | bytes 98312 | tf_op jit(solution)/shard_map/ppermute | solution.py:615
  93.2 2.1 %collective-permute-start.7 = (f32[2,4,4,256]{3,2,1,0:T(4,128)S(1)}, f32[2,4,4,256]{3,2,1,0:T(4,128)S(1)}, u32[]{:S(2)}, u32[]{:S(2)}) collective-permute-start(f32[2,4,4,256]{3,2,1,0:T(4,128)S(1)} %reverse_add_fusion), channel_id=1, source_target_pairs={{0,1},{1,2},{2,3},{3,4},{4,5},{5,6},{6,7},{7,8},{8,9},{9,10},{10,1... | collective-permute-start | bytes 98312 | tf_op jit(solution)/shard_map/ppermute | solution.py:624
  95.4 5.2 %shard_map.95 = (f32[64,256]{1,0:T(8,128)S(1)}, f32[64,256]{1,0:T(8,128)S(1)}, f32[64,256]{1,0:T(8,128)S(1)}, f32[64,256]{1,0:T(8,128)S(1)}, f32[4,64,256]{2,1,0:T(8,128)S(1)}) custom-call(s32[1]{0:T(128)} %bitcast.3.half_ref, s32[1]{0:T(128)} %bitcast.me_ref, f32[2,80,128]{2,1,0:T(8,128)S(1)} %get-tuple-element.35.op_ref, ...), custom_call_target="tpu_custom_call" | custom-call | flops 1 | bytes 1 | tf_op jit(solution)/shard_map/pallas_call | solution.py:542
  101.0 2.3 %collective-permute-done.7.refs_5_ = f32[2,4,4,256]{3,2,1,0:T(4,128)S(1)} collective-permute-done((f32[2,4,4,256]{3,2,1,0:T(4,128)S(1)}, f32[2,4,4,256]{3,2,1,0:T(4,128)S(1)}, u32[]{:S(2)}, u32[]{:S(2)}) %collective-permute-start.7) | collective-permute-done | bytes 32800 | tf_op jit(solution)/shard_map/ppermute | solution.py:624
  105.2 1.9 %collective-permute-start.10 = (f32[64,256]{1,0:T(8,128)S(1)}, f32[64,256]{1,0:T(8,128)S(1)}, u32[]{:S(2)}, u32[]{:S(2)}) collective-permute-start(f32[64,256]{1,0:T(8,128)S(1)} %get-tuple-element.53), channel_id=1, source_target_pairs={{0,128},{32,160},{64,192},{96,224},{128,0},{160,32},{192,64},{224,... | collective-permute-start | bytes 196616 | tf_op jit(solution)/shard_map/ppermute | solution.py:615
  107.1 1.6 %collective-permute-start.11 = (f32[64,256]{1,0:T(8,128)S(1)}, f32[64,256]{1,0:T(8,128)S(1)}, u32[]{:S(2)}, u32[]{:S(2)}) collective-permute-start(f32[64,256]{1,0:T(8,128)S(1)} %get-tuple-element.54), channel_id=1, source_target_pairs={{0,192},{32,224},{64,128},{96,160},{128,64},{160,96},{192,0},{224,... | collective-permute-start | bytes 196616 | tf_op jit(solution)/shard_map/ppermute | solution.py:615
  109.7 2.3 %collective-permute-done.11 = f32[64,256]{1,0:T(8,128)S(1)} collective-permute-done((f32[64,256]{1,0:T(8,128)S(1)}, f32[64,256]{1,0:T(8,128)S(1)}, u32[]{:S(2)}, u32[]{:S(2)}) %collective-permute-start.11) | collective-permute-done | bytes 65568 | tf_op jit(solution)/shard_map/ppermute | solution.py:615
  113.0 1.7 %collective-permute-start.14 = (f32[64,256]{1,0:T(8,128)S(1)}, f32[64,256]{1,0:T(8,128)S(1)}, u32[]{:S(2)}, u32[]{:S(2)}) collective-permute-start(f32[64,256]{1,0:T(8,128)S(1)} %divide_multiply_fusion.refs_0_), channel_id=1, source_target_pairs={{0,192},{32,224},{64,128},{96,160},{128,64},{160,96},{192,0},{224,... | collective-permute-start | bytes 196616 | tf_op jit(solution)/shard_map/ppermute | solution.py:615
  114.7 1.8 %collective-permute-start.13 = (f32[64,256]{1,0:T(8,128)S(1)}, f32[64,256]{1,0:T(8,128)S(1)}, u32[]{:S(2)}, u32[]{:S(2)}) collective-permute-start(f32[64,256]{1,0:T(8,128)S(1)} %divide_multiply_fusion.refs_0_), channel_id=1, source_target_pairs={{0,128},{32,160},{64,192},{96,224},{128,0},{160,32},{192,64},{224,... | collective-permute-start | bytes 196616 | tf_op jit(solution)/shard_map/ppermute | solution.py:615
  116.6 1.4 %collective-permute-done.14.refs_3_ = f32[64,256]{1,0:T(8,128)S(1)} collective-permute-done((f32[64,256]{1,0:T(8,128)S(1)}, f32[64,256]{1,0:T(8,128)S(1)}, u32[]{:S(2)}, u32[]{:S(2)}) %collective-permute-start.14) | collective-permute-done | bytes 65568 | tf_op jit(solution)/shard_map/ppermute | solution.py:615
  118.0 4.0 %collective-permute-done.13.refs_2_ = f32[64,256]{1,0:T(8,128)S(1)} collective-permute-done((f32[64,256]{1,0:T(8,128)S(1)}, f32[64,256]{1,0:T(8,128)S(1)}, u32[]{:S(2)}, u32[]{:S(2)}) %collective-permute-start.13) | collective-permute-done | bytes 65568 | tf_op jit(solution)/shard_map/ppermute | solution.py:615
  122.0 1.7 %collective-permute-start.15 = (f32[4,64,256]{2,1,0:T(8,128)S(1)}, f32[4,64,256]{2,1,0:T(8,128)S(1)}, u32[]{:S(2)}, u32[]{:S(2)}) collective-permute-start(f32[4,64,256]{2,1,0:T(8,128)S(1)} %pad_maximum_fusion), channel_id=1, source_target_pairs={{0,32},{32,0},{64,96},{96,64},{128,160},{160,128},{192,224},{224,1... | collective-permute-start | bytes 786440 | tf_op jit(solution)/shard_map/ppermute | solution.py:615
  123.7 1.2 collective-permute-done.15.refs_4_
  (42 shorter events, 7.5 us)
Async XLA Ops:
  1.1 42.7 %collective-permute-start = (f32[4,3,2,16,384]{4,3,2,1,0:T(8,128)S(1)}, f32[4,3,2,16,384]{4,3,2,1,0:T(8,128)S(1)}, u32[]{:S(2)}, u32[]{:S(2)}) collective-permute-start(f32[4,3,2,16,384]{4,3,2,1,0:T(8,128)S(1)} %shard_map.86), channel_id=1, source_target_pairs={{0,16},{1,17},{2,18},{3,19},{4,20},{5,21},{6,22},{7,23},{8,24},{9,... | collective-permute-start | bytes 1769480 | tf_op jit(solution)/shard_map/ppermute | solution.py:634
  13.7 30.1 %all-to-all-start = ((f32[16,8,8,384]{3,2,1,0:T(8,128)}), f32[16,8,8,384]{3,2,1,0:T(8,128)}, u32[]{:S(2)}, u32[]{:S(2)}) async-start(f32[16,8,8,384]{3,2,1,0:T(8,128)} %shard_map.83), calls=%async_computation | async-start | bytes 3145728 | tf_op jit(solution)/shard_map/all_to_all | solution.py:638
  21.7 22.0 %collective-permute-start.2 = (f32[4,2048]{1,0:T(4,128)}, f32[4,2048]{1,0:T(4,128)}, u32[]{:S(2)}, u32[]{:S(2)}) collective-permute-start(f32[4,2048]{1,0:T(4,128)} %get-tuple-element.55), channel_id=1, source_target_pairs={{1,0},{2,1},{3,2},{4,3},{5,4},{6,5},{7,6},{8,7},{9,8},{10,9},{11,1... | collective-permute-start | bytes 98312 | tf_op jit(solution)/shard_map/ppermute | solution.py:624
  26.6 11.0 %copy-start.6 = (s32[2,8,384]{2,1,0:T(8,128)S(1)}, s32[2,8,384]{2,1,0:T(8,128)}, u32[]{:S(2)}) copy-start(s32[2,8,384]{2,1,0:T(8,128)} %param.14) | copy-start | bytes 73732
  26.6 11.0 %copy-start.5 = (s32[65536]{0:T(1024)S(1)}, s32[65536]{0:T(1024)}, u32[]{:S(2)}) copy-start(s32[65536]{0:T(1024)} %param.13) | copy-start | bytes 786436
  26.6 11.1 %copy-start.4 = (f32[16,9]{1,0:T(8,128)S(1)}, f32[16,9]{1,0:T(8,128)}, u32[]{:S(2)}) copy-start(f32[16,9]{1,0:T(8,128)} %k_ref.1) | copy-start | bytes 1732
  26.7 17.1 %collective-permute-start.1 = (f32[4,2048]{1,0:T(4,128)}, f32[4,2048]{1,0:T(4,128)}, u32[]{:S(2)}, u32[]{:S(2)}) collective-permute-start(f32[4,2048]{1,0:T(4,128)} %get-tuple-element.56), channel_id=1, source_target_pairs={{0,1},{1,2},{2,3},{3,4},{4,5},{5,6},{6,7},{7,8},{8,9},{9,10},{10,1... | collective-permute-start | bytes 98312 | tf_op jit(solution)/shard_map/ppermute | solution.py:624
  36.4 1.1 copy-start
  45.0 25.3 %collective-permute-start.4 = (f32[32,8,384]{2,1,0:T(8,128)S(1)}, f32[32,8,384]{2,1,0:T(8,128)S(1)}, u32[]{:S(2)}, u32[]{:S(2)}) collective-permute-start(f32[32,8,384]{2,1,0:T(8,128)S(1)} %shard_map.92), channel_id=1, source_target_pairs={{0,16},{1,17},{2,18},{3,19},{4,20},{5,21},{6,22},{7,23},{8,24},{9,... | collective-permute-start | bytes 1179656 | tf_op jit(solution)/shard_map/ppermute | solution.py:634
  46.7 6.2 %copy-start.1 = (f32[16,8,8,384]{3,2,1,0:T(8,128)S(1)}, f32[16,8,8,384]{3,2,1,0:T(8,128)}, u32[]{:S(2)}) copy-start(f32[16,8,8,384]{3,2,1,0:T(8,128)} %shard_map.89._) | copy-start | bytes 4718596
  46.7 28.8 %all-to-all-start.1 = ((f32[16,8,8,384]{3,2,1,0:T(8,128)}), f32[16,8,8,384]{3,2,1,0:T(8,128)}, u32[]{:S(2)}, u32[]{:S(2)}) async-start(f32[16,8,8,384]{3,2,1,0:T(8,128)} %shard_map.89._), calls=%async_computation.1 | async-start | bytes 3145728 | tf_op jit(solution)/shard_map/all_to_all | solution.py:638
  52.9 7.6 %copy-start.2 = (s32[4,8,64,384]{3,2,1,0:T(8,128)S(1)}, s32[4,8,64,384]{3,2,1,0:T(8,128)}, u32[]{:S(2)}) copy-start(s32[4,8,64,384]{3,2,1,0:T(8,128)} %refs_2_.9) | copy-start | bytes 9437188
  53.0 7.6 %copy-start.3 = (f32[64,2048]{1,0:T(8,128)S(1)}, f32[64,2048]{1,0:T(8,128)}, u32[]{:S(2)}) copy-start(f32[64,2048]{1,0:T(8,128)} %act_ref.1) | copy-start | bytes 1572868
  55.1 40.2 %collective-permute-start.3 = (f32[12,4,8,384]{3,2,1,0:T(8,128)}, f32[12,4,8,384]{3,2,1,0:T(8,128)}, u32[]{:S(2)}, u32[]{:S(2)}) collective-permute-start(f32[12,4,8,384]{3,2,1,0:T(8,128)} %shard_map.90), channel_id=1, source_target_pairs={{0,16},{1,17},{2,18},{3,19},{4,20},{5,21},{6,22},{7,23},{8,24},{9,... | collective-permute-start | bytes 1769480 | tf_op jit(solution)/shard_map/ppermute | solution.py:634
  80.8 12.4 %collective-permute-start.6 = (f32[2,4,4,256]{3,2,1,0:T(4,128)S(1)}, f32[2,4,4,256]{3,2,1,0:T(4,128)S(1)}, u32[]{:S(2)}, u32[]{:S(2)}) collective-permute-start(f32[2,4,4,256]{3,2,1,0:T(4,128)S(1)} %get-tuple-element.50), channel_id=1, source_target_pairs={{0,32},{32,0},{64,96},{96,64},{128,160},{160,128},{192,224},{224,1... | collective-permute-start | bytes 98312 | tf_op jit(solution)/shard_map/ppermute | solution.py:615
  93.2 10.1 %collective-permute-start.7 = (f32[2,4,4,256]{3,2,1,0:T(4,128)S(1)}, f32[2,4,4,256]{3,2,1,0:T(4,128)S(1)}, u32[]{:S(2)}, u32[]{:S(2)}) collective-permute-start(f32[2,4,4,256]{3,2,1,0:T(4,128)S(1)} %reverse_add_fusion), channel_id=1, source_target_pairs={{0,1},{1,2},{2,3},{3,4},{4,5},{5,6},{6,7},{7,8},{8,9},{9,10},{10,1... | collective-permute-start | bytes 98312 | tf_op jit(solution)/shard_map/ppermute | solution.py:624
  100.6 3.9 %collective-permute-start.5 = (f32[4,64,256]{2,1,0:T(8,128)S(1)}, f32[4,64,256]{2,1,0:T(8,128)S(1)}, u32[]{:S(2)}, u32[]{:S(2)}) collective-permute-start(f32[4,64,256]{2,1,0:T(8,128)S(1)} %get-tuple-element.48), channel_id=1, source_target_pairs={{0,32},{32,0},{64,96},{96,64},{128,160},{160,128},{192,224},{224,1... | collective-permute-start | bytes 786440 | tf_op jit(solution)/shard_map/ppermute | solution.py:615
  103.3 1.2 collective-permute-start.8
  105.1 3.6 %collective-permute-start.9 = (f32[64,256]{1,0:T(8,128)S(1)}, f32[64,256]{1,0:T(8,128)S(1)}, u32[]{:S(2)}, u32[]{:S(2)}) collective-permute-start(f32[64,256]{1,0:T(8,128)S(1)} %get-tuple-element.52), channel_id=1, source_target_pairs={{0,64},{32,96},{64,0},{96,32},{128,192},{160,224},{192,128},{224,1... | collective-permute-start | bytes 196616 | tf_op jit(solution)/shard_map/ppermute | solution.py:615
  105.2 4.5 %collective-permute-start.10 = (f32[64,256]{1,0:T(8,128)S(1)}, f32[64,256]{1,0:T(8,128)S(1)}, u32[]{:S(2)}, u32[]{:S(2)}) collective-permute-start(f32[64,256]{1,0:T(8,128)S(1)} %get-tuple-element.53), channel_id=1, source_target_pairs={{0,128},{32,160},{64,192},{96,224},{128,0},{160,32},{192,64},{224,... | collective-permute-start | bytes 196616 | tf_op jit(solution)/shard_map/ppermute | solution.py:615
  107.1 4.9 %collective-permute-start.11 = (f32[64,256]{1,0:T(8,128)S(1)}, f32[64,256]{1,0:T(8,128)S(1)}, u32[]{:S(2)}, u32[]{:S(2)}) collective-permute-start(f32[64,256]{1,0:T(8,128)S(1)} %get-tuple-element.54), channel_id=1, source_target_pairs={{0,192},{32,224},{64,128},{96,160},{128,64},{160,96},{192,0},{224,... | collective-permute-start | bytes 196616 | tf_op jit(solution)/shard_map/ppermute | solution.py:615
  113.0 5.1 %collective-permute-start.14 = (f32[64,256]{1,0:T(8,128)S(1)}, f32[64,256]{1,0:T(8,128)S(1)}, u32[]{:S(2)}, u32[]{:S(2)}) collective-permute-start(f32[64,256]{1,0:T(8,128)S(1)} %divide_multiply_fusion.refs_0_), channel_id=1, source_target_pairs={{0,192},{32,224},{64,128},{96,160},{128,64},{160,96},{192,0},{224,... | collective-permute-start | bytes 196616 | tf_op jit(solution)/shard_map/ppermute | solution.py:615
  114.7 7.3 %collective-permute-start.13 = (f32[64,256]{1,0:T(8,128)S(1)}, f32[64,256]{1,0:T(8,128)S(1)}, u32[]{:S(2)}, u32[]{:S(2)}) collective-permute-start(f32[64,256]{1,0:T(8,128)S(1)} %divide_multiply_fusion.refs_0_), channel_id=1, source_target_pairs={{0,128},{32,160},{64,192},{96,224},{128,0},{160,32},{192,64},{224,... | collective-permute-start | bytes 196616 | tf_op jit(solution)/shard_map/ppermute | solution.py:615
  116.4 5.6 %collective-permute-start.12 = (f32[64,256]{1,0:T(8,128)S(1)}, f32[64,256]{1,0:T(8,128)S(1)}, u32[]{:S(2)}, u32[]{:S(2)}) collective-permute-start(f32[64,256]{1,0:T(8,128)S(1)} %divide_multiply_fusion.refs_0_), channel_id=1, source_target_pairs={{0,64},{32,96},{64,0},{96,32},{128,192},{160,224},{192,128},{224,1... | collective-permute-start | bytes 196616 | tf_op jit(solution)/shard_map/ppermute | solution.py:615
  122.0 2.8 %collective-permute-start.15 = (f32[4,64,256]{2,1,0:T(8,128)S(1)}, f32[4,64,256]{2,1,0:T(8,128)S(1)}, u32[]{:S(2)}, u32[]{:S(2)}) collective-permute-start(f32[4,64,256]{2,1,0:T(8,128)S(1)} %pad_maximum_fusion), channel_id=1, source_target_pairs={{0,32},{32,0},{64,96},{96,64},{128,160},{160,128},{192,224},{224,1... | collective-permute-start | bytes 786440 | tf_op jit(solution)/shard_map/ppermute | solution.py:615

commit v5 on v4

--- a/solution.py
+++ b/solution.py
@@ -11,7 +11,7 @@
 bf16 = jnp.bfloat16
 LANES = 128
 MIRROR = 6
-LASTS = 4
+LASTS = 5
 VMEM = pl.BlockSpec(memory_space=pltpu.VMEM)
 SMEM = pl.BlockSpec(memory_space=pltpu.SMEM)
 HBM = pl.BlockSpec(memory_space=pltpu.HBM)
@@ -499,29 +499,44 @@
     )(x)
 
 
-def back_last_kernel(half_ref, me_ref, op_ref, x_ref, factor_hbm, foot_hbm, in_ref, *refs):
-    mine_refs, (other_ref, acc_ref, factor_ref, foot_ref, sems) = refs[:4], refs[4:]
+def fetch_kernel(half_ref, factor_hbm, foot_hbm, _, factor_ref, foot_ref, sems):
+    views = foot_ref.shape[0]
+    first = foot_hbm.shape[0] - views
+    far = 1 - half_ref[0]
+    copies = [
+        pltpu.make_async_copy(factor_hbm.at[pl.ds(first, views), far], factor_ref, sems.at[views])
+    ] + [pltpu.make_async_copy(foot_hbm.at[first + v], foot_ref.at[v], sems.at[v]) for v in range(views)]
+    start_all(copies)
+    for copy in copies:
+        copy.wait()
+
+
+def fetch_last(half, factor, footprint, after, views):
+    return pl.pallas_call(
+        fetch_kernel,
+        in_specs=[SMEM, HBM, HBM, pl.BlockSpec(memory_space=pl.ANY)],
+        out_specs=[VMEM] * 2,
+        out_shape=[
+            pltpu.VMEM((views,) + factor.shape[2:], f32),
+            pltpu.VMEM((views,) + footprint.shape[1:], footprint.dtype),
+        ],
+        scratch_shapes=[pltpu.SemaphoreType.DMA((views + 1,))],
+        compiler_params=params(45),
+        cost_estimate=SMALL,
+    )(half, factor, footprint, after)
+
+
+def back_last_kernel(half_ref, me_ref, op_ref, x_ref, factor_ref, foot_ref, in_ref, *refs):
+    mine_refs, (other_ref, acc_ref) = refs[:4], refs[4:]
     slices, pixels = acc_ref.shape
     middle, views, inner, bins = x_ref.shape
     count = factor_ref.shape[1]
     edge = (count - middle) // 2
     far = 1 - half_ref[0]
-    first = factor_hbm.shape[0] - views
-
-    def copies(v):
-        return [
-            pltpu.make_async_copy(factor_hbm.at[first + v, far], factor_ref.at[v], sems.at[v, 0]),
-            pltpu.make_async_copy(foot_hbm.at[first + v], foot_ref.at[v], sems.at[v, 1]),
-        ]
-
-    for v in range(views):
-        start_all(copies(v))
     gap = jnp.zeros((edge * inner, bins), bf16)
     operator = op_ref[far, :slices]
     acc_ref[...] = in_ref[...]
     for v in range(views):
-        for copy in copies(v):
-            copy.wait()
         weighted = ratio(factor_ref[v, edge : count - edge], x_ref[:, v])
         acc_ref[...] += back_project(operator, jnp.concatenate([gap, weighted, gap], axis=0), foot_ref[v])
     width = mine_refs[0].shape[1]
@@ -538,19 +553,13 @@
 def back_last(half, me, operator, rows_in, factor, footprint, acc):
     slices, pixels = acc.shape
     width = pixels // 8
-    _, views, inner, bins = rows_in.shape
     return pl.pallas_call(
         back_last_kernel,
-        in_specs=[SMEM, SMEM, VMEM, VMEM, HBM, HBM, VMEM],
+        in_specs=[SMEM, SMEM] + [VMEM] * 5,
         out_specs=[VMEM] * 5,
         out_shape=[pltpu.VMEM((slices, width), f32)] * 4 + [pltpu.VMEM((4, slices, width), f32)],
-        scratch_shapes=[
-            pltpu.VMEM((slices, pixels), f32),
-            pltpu.VMEM((views, factor.shape[2], inner, bins), f32),
-            pltpu.VMEM((views, pixels, bins), bf16),
-            pltpu.SemaphoreType.DMA((views, 2)),
-        ],
-        compiler_params=params(52),
+        scratch_shapes=[pltpu.VMEM((slices, pixels), f32)],
+        compiler_params=params(24),
         cost_estimate=SMALL,
     )(half, me, operator, rows_in, factor, footprint, acc)
 
@@ -664,9 +673,11 @@
 
     acc = back_staged(half, operator_t, staged, part, factor, footprint, edge, behind)
     acc, keep, give = back_near(half, me, operator_t, near, factor, footprint, acc, slices, margin, firsts + bare)
-    halo = shift(keep + swap(give, 1)[::-1], (1,))
+    joined = keep + swap(give, 1)[::-1]
+    halo = shift(joined, (1,))
+    last_factor, last_foot = fetch_last(half, factor, footprint, joined, lasts)
     across = swap(halo[1], 1)
-    *mine, other = back_last(half, me, operator_t, rows_last, factor, footprint, acc)
+    *mine, other = back_last(half, me, operator_t, rows_last, last_factor, last_foot, acc)
     sides = [jnp.where(even, slab == count, slab == count - 1), jnp.where(even, slab == count - 1, slab == count)]
     flip = jnp.where(jnp.stack(sides), MIRROR // 2, 0).astype(jnp.int32)
     pair = pair_sum(me, flip, mine, swap(other, 1), halo, across)

time: 126 us -> 125 us (level)
  starting transfers between devices: 59.1 us -> 51.9 us
  local copies, waits for them, and re-layouts: 2.81 us -> 7.7 us
  Pallas kernels: 48.3 us -> 50.7 us
  waiting for transfers between devices: 14.2 us -> 12.6 us
    ppermute x10, starting transfers between devices: 20.9 us -> 15.1 us  [swap(): return lax.ppermute(x, 'seg', [(i, i ^ k) for i in range(2 * halves)])]
    ppermute x3, starting transfers between devices: 12.9 us -> 8.04 us  [shift(): return lax.ppermute(x, ('seg', 'slab'), pairs)]
    unnamed x14 -> x20, local copies, waits for them, and re-layouts: 1.17 us -> 6.05 us
    all_to_all x2, starting transfers between devices: 12.7 us -> 17.2 us  [exchange(): lax.all_to_all(x, 'slab', split_axis=0, concat_axis=0, tiled=True, axis_i...]
    pallas_call x1 -> x2, Pallas kernels: 5.19 us -> 7.81 us  [the longest x1 4.18 us: back_last(): pl.pallas_call(back_last_kernel, in_specs=[SMEM, SMEM] + [VMEM] * 5, out_...]
    ppermute x3, waiting for transfers between devices: 2.31 us -> 0.01 us  [shift(): return lax.ppermute(x, ('seg', 'slab'), pairs)]
  transfers between devices with their start and end apart: 18 -> 18, of which waited for: 8 -> 7; matrix products, arithmetic and copies ran while one was open for 1% -> 1% of each run, Pallas kernels for 35% -> 38%
where the time goes in v5:
time: 125 us; the launch traced here: 124 us
  starting transfers between devices  51.9 us (42%)
  Pallas kernels  50.7 us (41%)
  waiting for transfers between devices  12.6 us (10%)
  local copies, waits for them, and re-layouts  7.7 us (6%)
    all_to_all x2, starting transfers between devices, exchange(): lax.all_to_all(x, 'slab', split_axis=0, concat_axis=0, tiled=True, axis_i...  17.2 us
    ppermute x10, starting transfers between devices, swap(): return lax.ppermute(x, 'seg', [(i, i ^ k) for i in range(2 * halves)])  15.1 us
    ppermute x10, waiting for transfers between devices, swap(): return lax.ppermute(x, 'seg', [(i, i ^ k) for i in range(2 * halves)])  12.6 us
    ppermute x3, starting transfers between devices, cross(): lax.ppermute(x, 'slab', [(i, (i + count) % slabs) for i in range(slabs)])  11.5 us
    pallas_call x5, Pallas kernels, relay(): pl.pallas_call(functools.partial(relay_kernel, sides, lanes), grid=(views...  11.1 us
    pallas_call x1, Pallas kernels, forward(): pl.pallas_call(forward_kernel, grid=(views,), in_specs=[VMEM, VMEM, VMEM,...  9.69 us
    ppermute x3, starting transfers between devices, shift(): return lax.ppermute(x, ('seg', 'slab'), pairs)  8.04 us
    pallas_call x1, Pallas kernels, back_staged(): pl.pallas_call(functools.partial(back_staged_kernel, edge), in_specs=[SME...  6.1 us
  transfers between devices with their start and end apart: 18, of which 7 were waited for; matrix products, arithmetic and copies ran while one was open for 1% of the time, Pallas kernels for 38%

profile of v5, /device:TPU:31, one launch (start us, length us, event | category | flops | bytes accessed | tf_op | source)
XLA Modules:
  0.0 124.2 jit_solution(16386082612370359565)
XLA Ops:
  1.1 7.0 %collective-permute-start = (f32[4,3,2,16,384]{4,3,2,1,0:T(8,128)S(1)}, f32[4,3,2,16,384]{4,3,2,1,0:T(8,128)S(1)}, u32[]{:S(2)}, u32[]{:S(2)}) collective-permute-start(f32[4,3,2,16,384]{4,3,2,1,0:T(8,128)S(1)} %shard_map.86), channel_id=1, source_target_pairs={{0,16},{1,17},{2,18},{3,19},{4,20},{5,21},{6,22},{7,23},{8,24},{9,... | collective-permute-start | bytes 1769480 | tf_op jit(solution)/shard_map/ppermute | solution.py:643
  8.1 2.1 %shard_map.82.refs_3_ = f32[16,8,8,384]{3,2,1,0:T(8,128)} custom-call(s32[1]{0:T(128)} %bitcast.3.half_ref, f32[4,8,2,32,384]{4,3,2,1,0:T(8,128)} %m_hbm.1, f32[4,8,2,32,384]{4,3,2,1,0:T(8,128)} %m_hbm.1, f32[4,8,2,32,384]{4,3,2,1,0:T(8,128)} %m_hbm.1), custom_call_target="tpu_custom_call" | custom-call | flops 1 | bytes 1 | tf_op jit(solution)/shard_map/pallas_call | solution.py:59
  10.1 3.6 %shard_map.83 = f32[16,8,8,384]{3,2,1,0:T(8,128)} custom-call(s32[1]{0:T(128)} %bitcast.3.half_ref, f32[4,8,2,32,384]{4,3,2,1,0:T(8,128)} %m_hbm.1, f32[4,8,2,32,384]{4,3,2,1,0:T(8,128)} %m_hbm.1, f32[4,8,2,32,384]{4,3,2,1,0:T(8,128)} %m_hbm.1, f32[16,8,8,384]{3,2,1,0:T(8,128)} %shard_map.82.refs_3_), custom_call_target="tpu_custom_call", output_to_operand_aliasing={{}: (4, {})} | custom-call | flops 1 | bytes 1 | tf_op jit(solution)/shard_map/pallas_call | solution.py:59
  13.8 6.5 %all-to-all-start = ((f32[16,8,8,384]{3,2,1,0:T(8,128)}), f32[16,8,8,384]{3,2,1,0:T(8,128)}, u32[]{:S(2)}, u32[]{:S(2)}) async-start(f32[16,8,8,384]{3,2,1,0:T(8,128)} %shard_map.83), calls=%async_computation | async-start | bytes 3145728 | tf_op jit(solution)/shard_map/all_to_all | solution.py:647
  20.3 1.5 %fusion = (f32[4,2048]{1,0:T(4,128)}, f32[4,2048]{1,0:T(4,128)}) fusion(f32[64,2048]{1,0:T(8,128)} %act_ref.1), kind=kLoop, calls=%fused_computation.5 | loop fusion | bytes 131072 | tf_op jit(solution)/shard_map/slice | solution.py:662
  21.8 1.9 %collective-permute-start.1 = (f32[4,2048]{1,0:T(4,128)}, f32[4,2048]{1,0:T(4,128)}, u32[]{:S(2)}, u32[]{:S(2)}) collective-permute-start(f32[4,2048]{1,0:T(4,128)} %get-tuple-element.60), channel_id=1, source_target_pairs={{0,1},{1,2},{2,3},{3,4},{4,5},{5,6},{6,7},{7,8},{8,9},{9,10},{10,1... | collective-permute-start | bytes 98312 | tf_op jit(solution)/shard_map/ppermute | solution.py:633
  23.7 2.4 %shard_map.84.refs_3_ = f32[16,8,8,384]{3,2,1,0:T(8,128)S(1)} custom-call(s32[1]{0:T(128)} %bitcast.3.half_ref, f32[4,8,2,32,384]{4,3,2,1,0:T(8,128)} %m_hbm.1, f32[4,8,2,32,384]{4,3,2,1,0:T(8,128)} %m_hbm.1, f32[4,8,2,32,384]{4,3,2,1,0:T(8,128)} %m_hbm.1), custom_call_target="tpu_custom_call" | custom-call | flops 1 | bytes 1 | tf_op jit(solution)/shard_map/pallas_call | solution.py:59
  26.1 3.5 %collective-permute-start.2 = (f32[4,2048]{1,0:T(4,128)}, f32[4,2048]{1,0:T(4,128)}, u32[]{:S(2)}, u32[]{:S(2)}) collective-permute-start(f32[4,2048]{1,0:T(4,128)} %get-tuple-element.59), channel_id=1, source_target_pairs={{1,0},{2,1},{3,2},{4,3},{5,4},{6,5},{7,6},{8,7},{9,8},{10,9},{11,1... | collective-permute-start | bytes 98312 | tf_op jit(solution)/shard_map/ppermute | solution.py:633
  29.6 1.4 %shard_map.85.refs_3_ = f32[16,8,8,384]{3,2,1,0:T(8,128)S(1)} custom-call(s32[1]{0:T(128)} %bitcast.3.half_ref, f32[4,8,2,32,384]{4,3,2,1,0:T(8,128)} %m_hbm.1, f32[4,8,2,32,384]{4,3,2,1,0:T(8,128)} %m_hbm.1, f32[4,8,2,32,384]{4,3,2,1,0:T(8,128)} %m_hbm.1, f32[16,8,8,384]{3,2,1,0:T(8,128)S(1)} %shard_map.84.refs_3_), custom_call_target="tpu_custom_call", output_to_operand_aliasing={{}: (4, {})} | custom-call | flops 1 | bytes 1 | tf_op jit(solution)/shard_map/pallas_call | solution.py:59
  32.4 6.0 %shard_map.88 = (f32[8,1,384]{2,1,0:T(1,128)S(1)}, f32[256,80]{1,0:T(8,128)S(1)}, f32[2,80,128]{2,1,0:T(8,128)S(1)}) custom-call(s32[1]{0:T(128)} %bitcast.me_ref, f32[16,9]{1,0:T(8,128)S(1)} %copy-done.7, s32[128,512]{1,0:T(8,128)S(1)} %bitcast.12, s32[2,8,1,384]{3,2,1,0:T(1,128)S(1)} %reshape.15.c_ref), custom_call_target="tpu_custom_call" | custom-call | flops 1 | bytes 1 | tf_op jit(solution)/shard_map/pallas_call | solution.py:145
  41.1 1.6 %shard_map.89._ = f32[16,8,8,384]{3,2,1,0:T(8,128)} custom-call(s32[1]{0:T(128)} %bitcast.3.half_ref, f32[4,3,2,16,384]{4,3,2,1,0:T(8,128)S(1)} %collective-permute-done.x_ref.refs_0_.refs_1_.refs_2_, f32[4,3,2,16,384]{4,3,2,1,0:T(8,128)S(1)} %collective-permute-done.x_ref.refs_0_.refs_1_.refs_2_, ...), custom_call_target="tpu_custom_call", output_to_operand_aliasing={{}: (4, {})} | custom-call | flops 1 | bytes 1 | tf_op jit(solution)/shard_map/pallas_call | solution.py:59
  42.7 1.4 %copy-done.1 = f32[16,8,8,384]{3,2,1,0:T(8,128)S(1)} copy-done((f32[16,8,8,384]{3,2,1,0:T(8,128)S(1)}, f32[16,8,8,384]{3,2,1,0:T(8,128)}, u32[]{:S(2)}) %copy-start.1) | copy-done | bytes 1572888
  44.1 1.2 %shard_map.90 = f32[12,5,8,384]{3,2,1,0:T(8,128)S(1)} custom-call(f32[16,8,8,384]{3,2,1,0:T(8,128)} %all-to-all-done.staged_hbm, f32[16,8,8,384]{3,2,1,0:T(8,128)S(1)} %copy-done.1), custom_call_target="tpu_custom_call" | custom-call | flops 1 | bytes 1 | tf_op jit(solution)/shard_map/pallas_call | solution.py:455
  46.3 10.6 %all-to-all-start.1 = ((f32[16,8,8,384]{3,2,1,0:T(8,128)}), f32[16,8,8,384]{3,2,1,0:T(8,128)}, u32[]{:S(2)}, u32[]{:S(2)}) async-start(f32[16,8,8,384]{3,2,1,0:T(8,128)} %shard_map.89._), calls=%async_computation.1 | async-start | bytes 3145728 | tf_op jit(solution)/shard_map/all_to_all | solution.py:647
  56.9 3.5 %collective-permute-start.3 = (f32[12,5,8,384]{3,2,1,0:T(8,128)}, f32[12,5,8,384]{3,2,1,0:T(8,128)}, u32[]{:S(2)}, u32[]{:S(2)}) collective-permute-start(f32[12,5,8,384]{3,2,1,0:T(8,128)} %copy-done.4), channel_id=1, source_target_pairs={{0,16},{1,17},{2,18},{3,19},{4,20},{5,21},{6,22},{7,23},{8,24},{9,... | collective-permute-start | bytes 2211848 | tf_op jit(solution)/shard_map/ppermute | solution.py:643
  62.3 9.7 %shard_map.91.factor_hbm = f32[8,2,16,8,384]{4,3,2,1,0:T(8,128)} custom-call(f32[256,80]{1,0:T(8,128)S(1)} %copy-done.6, f32[64,2048]{1,0:T(8,128)S(1)} %copy-done.3, f32[4,2048]{1,0:T(4,128)} %collective-permute-done.1.above_ref, f32[4,2048]{1,0:T(4,128)} %collective-permute-done.2.below_ref, bf16[8,2048,384]{2,1,0:T(8,128)(2,1)} %foot_hbm.7, ...), custom_call_target="tpu_custom_call" | custom-call | flops 1 | bytes 1 | tf_op jit(solution)/shard_map/pallas_call | solution.py:209
  72.0 6.1 %shard_map.93.in_ref = f32[80,2048]{1,0:T(8,128)S(1)} custom-call(s32[1]{0:T(128)} %bitcast.3.half_ref, f32[2,80,128]{2,1,0:T(8,128)S(1)} %get-tuple-element.37.op_ref, f32[16,8,8,384]{3,2,1,0:T(8,128)} %all-to-all-done.staged_hbm, f32[20,8,384]{2,1,0:T(8,128)} %collective-permute-done.4.part_ref, f32[8,2,16,8,384]{4,3,2,1,0:T(8,128)} %shard_map.91.factor_hbm, ...), custom_call_target="tpu_custom_call" | custom-call | flops 999999995904 | bytes 1048576 | tf_op jit(solution)/shard_map/pallas_call | solution.py:311
  78.2 5.3 %shard_map.94 = (f32[64,2048]{1,0:T(8,128)S(1)}, f32[2,4,4,256]{3,2,1,0:T(4,128)S(1)}, f32[2,4,4,256]{3,2,1,0:T(4,128)S(1)}) custom-call(s32[1]{0:T(128)} %bitcast.3.half_ref, s32[1]{0:T(128)} %bitcast.me_ref, f32[2,80,128]{2,1,0:T(8,128)S(1)} %get-tuple-element.37.op_ref, f32[16,8,8,384]{3,2,1,0:T(8,128)} %all-to-all-done.1.near_hbm, ...), custom_call_target="tpu_custom_call" | custom-call | flops 1 | bytes 1 | tf_op jit(solution)/shard_map/pallas_call | solution.py:377
  83.5 2.4 %collective-permute-start.5 = (f32[2,4,4,256]{3,2,1,0:T(4,128)S(1)}, f32[2,4,4,256]{3,2,1,0:T(4,128)S(1)}, u32[]{:S(2)}, u32[]{:S(2)}) collective-permute-start(f32[2,4,4,256]{3,2,1,0:T(4,128)S(1)} %get-tuple-element.46), channel_id=1, source_target_pairs={{0,32},{32,0},{64,96},{96,64},{128,160},{160,128},{192,224},{224,1... | collective-permute-start | bytes 98312 | tf_op jit(solution)/shard_map/ppermute | solution.py:624
  86.8 2.6 %collective-permute-start.7 = (f32[2,4,4,256]{3,2,1,0:T(4,128)S(1)}, f32[2,4,4,256]{3,2,1,0:T(4,128)S(1)}, u32[]{:S(2)}, u32[]{:S(2)}) collective-permute-start(f32[2,4,4,256]{3,2,1,0:T(4,128)S(1)} %reverse_add_fusion._), channel_id=1, source_target_pairs={{0,1},{1,2},{2,3},{3,4},{4,5},{5,6},{6,7},{7,8},{8,9},{9,10},{10,1... | collective-permute-start | bytes 98312 | tf_op jit(solution)/shard_map/ppermute | solution.py:633
  89.5 3.6 %shard_map.95 = (f32[5,16,8,384]{3,2,1,0:T(8,128)S(1)}, bf16[5,2048,384]{2,1,0:T(8,128)(2,1)S(1)}) custom-call(s32[1]{0:T(128)} %bitcast.3.half_ref, f32[8,2,16,8,384]{4,3,2,1,0:T(8,128)} %shard_map.91.factor_hbm, bf16[8,2048,384]{2,1,0:T(8,128)(2,1)} %foot_hbm.7, f32[2,4,4,256]{3,2,1,0:T(4,128)S(1)} %reverse_add_fusion._), custom_call_target="tpu_custom_call" | custom-call | flops 1 | bytes 1 | tf_op jit(solution)/shard_map/pallas_call | solution.py:515
  93.1 4.2 %shard_map.96 = (f32[64,256]{1,0:T(8,128)S(1)}, f32[64,256]{1,0:T(8,128)S(1)}, f32[64,256]{1,0:T(8,128)S(1)}, f32[64,256]{1,0:T(8,128)S(1)}, f32[4,64,256]{2,1,0:T(8,128)S(1)}) custom-call(s32[1]{0:T(128)} %bitcast.3.half_ref, s32[1]{0:T(128)} %bitcast.me_ref, f32[2,80,128]{2,1,0:T(8,128)S(1)} %get-tuple-element.37.op_ref, ...), custom_call_target="tpu_custom_call" | custom-call | flops 1 | bytes 1 | tf_op jit(solution)/shard_map/pallas_call | solution.py:556
  97.3 3.3 %collective-permute-start.6 = (f32[4,64,256]{2,1,0:T(8,128)S(1)}, f32[4,64,256]{2,1,0:T(8,128)S(1)}, u32[]{:S(2)}, u32[]{:S(2)}) collective-permute-start(f32[4,64,256]{2,1,0:T(8,128)S(1)} %get-tuple-element.54), channel_id=1, source_target_pairs={{0,32},{32,0},{64,96},{96,64},{128,160},{160,128},{192,224},{224,1... | collective-permute-start | bytes 786440 | tf_op jit(solution)/shard_map/ppermute | solution.py:624
  102.4 1.7 %collective-permute-start.11 = (f32[64,256]{1,0:T(8,128)S(1)}, f32[64,256]{1,0:T(8,128)S(1)}, u32[]{:S(2)}, u32[]{:S(2)}) collective-permute-start(f32[64,256]{1,0:T(8,128)S(1)} %get-tuple-element.58), channel_id=1, source_target_pairs={{0,192},{32,224},{64,128},{96,160},{128,64},{160,96},{192,0},{224,... | collective-permute-start | bytes 196616 | tf_op jit(solution)/shard_map/ppermute | solution.py:624
  104.1 1.2 collective-permute-start.10
  106.0 1.5 %collective-permute-done.11 = f32[64,256]{1,0:T(8,128)S(1)} collective-permute-done((f32[64,256]{1,0:T(8,128)S(1)}, f32[64,256]{1,0:T(8,128)S(1)}, u32[]{:S(2)}, u32[]{:S(2)}) %collective-permute-start.11) | collective-permute-done | bytes 65568 | tf_op jit(solution)/shard_map/ppermute | solution.py:624
  107.5 4.1 %collective-permute-done.10 = f32[64,256]{1,0:T(8,128)S(1)} collective-permute-done((f32[64,256]{1,0:T(8,128)S(1)}, f32[64,256]{1,0:T(8,128)S(1)}, u32[]{:S(2)}, u32[]{:S(2)}) %collective-permute-start.10) | collective-permute-done | bytes 65568 | tf_op jit(solution)/shard_map/ppermute | solution.py:624
  112.6 1.9 %collective-permute-start.13 = (f32[64,256]{1,0:T(8,128)S(1)}, f32[64,256]{1,0:T(8,128)S(1)}, u32[]{:S(2)}, u32[]{:S(2)}) collective-permute-start(f32[64,256]{1,0:T(8,128)S(1)} %divide_multiply_fusion.refs_0_), channel_id=1, source_target_pairs={{0,128},{32,160},{64,192},{96,224},{128,0},{160,32},{192,64},{224,... | collective-permute-start | bytes 196616 | tf_op jit(solution)/shard_map/ppermute | solution.py:624
  114.5 1.7 %collective-permute-start.14 = (f32[64,256]{1,0:T(8,128)S(1)}, f32[64,256]{1,0:T(8,128)S(1)}, u32[]{:S(2)}, u32[]{:S(2)}) collective-permute-start(f32[64,256]{1,0:T(8,128)S(1)} %divide_multiply_fusion.refs_0_), channel_id=1, source_target_pairs={{0,192},{32,224},{64,128},{96,160},{128,64},{160,96},{192,0},{224,... | collective-permute-start | bytes 196616 | tf_op jit(solution)/shard_map/ppermute | solution.py:624
  116.7 3.4 %collective-permute-done.14.refs_3_ = f32[64,256]{1,0:T(8,128)S(1)} collective-permute-done((f32[64,256]{1,0:T(8,128)S(1)}, f32[64,256]{1,0:T(8,128)S(1)}, u32[]{:S(2)}, u32[]{:S(2)}) %collective-permute-start.14) | collective-permute-done | bytes 65568 | tf_op jit(solution)/shard_map/ppermute | solution.py:624
  120.2 2.1 %collective-permute-start.15 = (f32[4,64,256]{2,1,0:T(8,128)S(1)}, f32[4,64,256]{2,1,0:T(8,128)S(1)}, u32[]{:S(2)}, u32[]{:S(2)}) collective-permute-start(f32[4,64,256]{2,1,0:T(8,128)S(1)} %pad_maximum_fusion), channel_id=1, source_target_pairs={{0,32},{32,0},{64,96},{96,64},{128,160},{160,128},{192,224},{224,1... | collective-permute-start | bytes 786440 | tf_op jit(solution)/shard_map/ppermute | solution.py:624
  122.2 1.2 collective-permute-done.15.refs_4_
  (49 shorter events, 13.8 us)
Async XLA Ops:
  1.1 37.3 %collective-permute-start = (f32[4,3,2,16,384]{4,3,2,1,0:T(8,128)S(1)}, f32[4,3,2,16,384]{4,3,2,1,0:T(8,128)S(1)}, u32[]{:S(2)}, u32[]{:S(2)}) collective-permute-start(f32[4,3,2,16,384]{4,3,2,1,0:T(8,128)S(1)} %shard_map.86), channel_id=1, source_target_pairs={{0,16},{1,17},{2,18},{3,19},{4,20},{5,21},{6,22},{7,23},{8,24},{9,... | collective-permute-start | bytes 1769480 | tf_op jit(solution)/shard_map/ppermute | solution.py:643
  13.8 25.3 %all-to-all-start = ((f32[16,8,8,384]{3,2,1,0:T(8,128)}), f32[16,8,8,384]{3,2,1,0:T(8,128)}, u32[]{:S(2)}, u32[]{:S(2)}) async-start(f32[16,8,8,384]{3,2,1,0:T(8,128)} %shard_map.83), calls=%async_computation | async-start | bytes 3145728 | tf_op jit(solution)/shard_map/all_to_all | solution.py:647
  21.8 17.3 %collective-permute-start.1 = (f32[4,2048]{1,0:T(4,128)}, f32[4,2048]{1,0:T(4,128)}, u32[]{:S(2)}, u32[]{:S(2)}) collective-permute-start(f32[4,2048]{1,0:T(4,128)} %get-tuple-element.60), channel_id=1, source_target_pairs={{0,1},{1,2},{2,3},{3,4},{4,5},{5,6},{6,7},{7,8},{8,9},{9,10},{10,1... | collective-permute-start | bytes 98312 | tf_op jit(solution)/shard_map/ppermute | solution.py:633
  26.1 6.1 %copy-start.8 = (s32[65536]{0:T(1024)S(1)}, s32[65536]{0:T(1024)}, u32[]{:S(2)}) copy-start(s32[65536]{0:T(1024)} %param.13) | copy-start | bytes 786436
  26.1 6.2 %copy-start.9 = (s32[2,8,384]{2,1,0:T(8,128)S(1)}, s32[2,8,384]{2,1,0:T(8,128)}, u32[]{:S(2)}) copy-start(s32[2,8,384]{2,1,0:T(8,128)} %param.14) | copy-start | bytes 73732
  26.1 6.3 %copy-start.7 = (f32[16,9]{1,0:T(8,128)S(1)}, f32[16,9]{1,0:T(8,128)}, u32[]{:S(2)}) copy-start(f32[16,9]{1,0:T(8,128)} %k_ref.1) | copy-start | bytes 1732
  26.1 12.9 %collective-permute-start.2 = (f32[4,2048]{1,0:T(4,128)}, f32[4,2048]{1,0:T(4,128)}, u32[]{:S(2)}, u32[]{:S(2)}) collective-permute-start(f32[4,2048]{1,0:T(4,128)} %get-tuple-element.59), channel_id=1, source_target_pairs={{1,0},{2,1},{3,2},{4,3},{5,4},{6,5},{7,6},{8,7},{9,8},{10,9},{11,1... | collective-permute-start | bytes 98312 | tf_op jit(solution)/shard_map/ppermute | solution.py:633
  31.1 1.2 copy-start
  38.4 0.7 copy-start.5
  40.1 32.0 %collective-permute-start.4 = (f32[20,8,384]{2,1,0:T(8,128)S(1)}, f32[20,8,384]{2,1,0:T(8,128)}, u32[]{:S(2)}, u32[]{:S(2)}) collective-permute-start(f32[20,8,384]{2,1,0:T(8,128)S(1)} %shard_map.92), channel_id=1, source_target_pairs={{0,16},{1,17},{2,18},{3,19},{4,20},{5,21},{6,22},{7,23},{8,24},{9,... | collective-permute-start | bytes 737288 | tf_op jit(solution)/shard_map/ppermute | solution.py:643
  42.7 1.4 %copy-start.1 = (f32[16,8,8,384]{3,2,1,0:T(8,128)S(1)}, f32[16,8,8,384]{3,2,1,0:T(8,128)}, u32[]{:S(2)}) copy-start(f32[16,8,8,384]{3,2,1,0:T(8,128)} %shard_map.89._) | copy-start | bytes 4718596
  45.4 0.9 copy-start.4
  46.3 14.1 %copy-start.2 = (s32[4,8,64,384]{3,2,1,0:T(8,128)S(1)}, s32[4,8,64,384]{3,2,1,0:T(8,128)}, u32[]{:S(2)}) copy-start(s32[4,8,64,384]{3,2,1,0:T(8,128)} %refs_2_.9) | copy-start | bytes 9437188
  46.3 31.9 %all-to-all-start.1 = ((f32[16,8,8,384]{3,2,1,0:T(8,128)}), f32[16,8,8,384]{3,2,1,0:T(8,128)}, u32[]{:S(2)}, u32[]{:S(2)}) async-start(f32[16,8,8,384]{3,2,1,0:T(8,128)} %shard_map.89._), calls=%async_computation.1 | async-start | bytes 3145728 | tf_op jit(solution)/shard_map/all_to_all | solution.py:647
  56.9 36.2 %collective-permute-start.3 = (f32[12,5,8,384]{3,2,1,0:T(8,128)}, f32[12,5,8,384]{3,2,1,0:T(8,128)}, u32[]{:S(2)}, u32[]{:S(2)}) collective-permute-start(f32[12,5,8,384]{3,2,1,0:T(8,128)} %copy-done.4), channel_id=1, source_target_pairs={{0,16},{1,17},{2,18},{3,19},{4,20},{5,21},{6,22},{7,23},{8,24},{9,... | collective-permute-start | bytes 2211848 | tf_op jit(solution)/shard_map/ppermute | solution.py:643
  60.4 1.0 copy-start.3
  61.4 0.9 copy-start.6
  83.5 3.3 %collective-permute-start.5 = (f32[2,4,4,256]{3,2,1,0:T(4,128)S(1)}, f32[2,4,4,256]{3,2,1,0:T(4,128)S(1)}, u32[]{:S(2)}, u32[]{:S(2)}) collective-permute-start(f32[2,4,4,256]{3,2,1,0:T(4,128)S(1)} %get-tuple-element.46), channel_id=1, source_target_pairs={{0,32},{32,0},{64,96},{96,64},{128,160},{160,128},{192,224},{224,1... | collective-permute-start | bytes 98312 | tf_op jit(solution)/shard_map/ppermute | solution.py:624
  86.8 13.8 %collective-permute-start.7 = (f32[2,4,4,256]{3,2,1,0:T(4,128)S(1)}, f32[2,4,4,256]{3,2,1,0:T(4,128)S(1)}, u32[]{:S(2)}, u32[]{:S(2)}) collective-permute-start(f32[2,4,4,256]{3,2,1,0:T(4,128)S(1)} %reverse_add_fusion._), channel_id=1, source_target_pairs={{0,1},{1,2},{2,3},{3,4},{4,5},{5,6},{6,7},{7,8},{8,9},{9,10},{10,1... | collective-permute-start | bytes 98312 | tf_op jit(solution)/shard_map/ppermute | solution.py:633
  97.3 4.5 %collective-permute-start.6 = (f32[4,64,256]{2,1,0:T(8,128)S(1)}, f32[4,64,256]{2,1,0:T(8,128)S(1)}, u32[]{:S(2)}, u32[]{:S(2)}) collective-permute-start(f32[4,64,256]{2,1,0:T(8,128)S(1)} %get-tuple-element.54), channel_id=1, source_target_pairs={{0,32},{32,0},{64,96},{96,64},{128,160},{160,128},{192,224},{224,1... | collective-permute-start | bytes 786440 | tf_op jit(solution)/shard_map/ppermute | solution.py:624
  100.6 1.2 collective-permute-start.8
  102.4 5.1 %collective-permute-start.11 = (f32[64,256]{1,0:T(8,128)S(1)}, f32[64,256]{1,0:T(8,128)S(1)}, u32[]{:S(2)}, u32[]{:S(2)}) collective-permute-start(f32[64,256]{1,0:T(8,128)S(1)} %get-tuple-element.58), channel_id=1, source_target_pairs={{0,192},{32,224},{64,128},{96,160},{128,64},{160,96},{192,0},{224,... | collective-permute-start | bytes 196616 | tf_op jit(solution)/shard_map/ppermute | solution.py:624
  104.1 7.5 %collective-permute-start.10 = (f32[64,256]{1,0:T(8,128)S(1)}, f32[64,256]{1,0:T(8,128)S(1)}, u32[]{:S(2)}, u32[]{:S(2)}) collective-permute-start(f32[64,256]{1,0:T(8,128)S(1)} %get-tuple-element.57), channel_id=1, source_target_pairs={{0,128},{32,160},{64,192},{96,224},{128,0},{160,32},{192,64},{224,... | collective-permute-start | bytes 196616 | tf_op jit(solution)/shard_map/ppermute | solution.py:624
  105.3 6.3 %collective-permute-start.9 = (f32[64,256]{1,0:T(8,128)S(1)}, f32[64,256]{1,0:T(8,128)S(1)}, u32[]{:S(2)}, u32[]{:S(2)}) collective-permute-start(f32[64,256]{1,0:T(8,128)S(1)} %get-tuple-element.56), channel_id=1, source_target_pairs={{0,64},{32,96},{64,0},{96,32},{128,192},{160,224},{192,128},{224,1... | collective-permute-start | bytes 196616 | tf_op jit(solution)/shard_map/ppermute | solution.py:624
  112.5 3.6 %collective-permute-start.12 = (f32[64,256]{1,0:T(8,128)S(1)}, f32[64,256]{1,0:T(8,128)S(1)}, u32[]{:S(2)}, u32[]{:S(2)}) collective-permute-start(f32[64,256]{1,0:T(8,128)S(1)} %divide_multiply_fusion.refs_0_), channel_id=1, source_target_pairs={{0,64},{32,96},{64,0},{96,32},{128,192},{160,224},{192,128},{224,1... | collective-permute-start | bytes 196616 | tf_op jit(solution)/shard_map/ppermute | solution.py:624
  112.6 4.1 %collective-permute-start.13 = (f32[64,256]{1,0:T(8,128)S(1)}, f32[64,256]{1,0:T(8,128)S(1)}, u32[]{:S(2)}, u32[]{:S(2)}) collective-permute-start(f32[64,256]{1,0:T(8,128)S(1)} %divide_multiply_fusion.refs_0_), channel_id=1, source_target_pairs={{0,128},{32,160},{64,192},{96,224},{128,0},{160,32},{192,64},{224,... | collective-permute-start | bytes 196616 | tf_op jit(solution)/shard_map/ppermute | solution.py:624
  114.5 5.7 %collective-permute-start.14 = (f32[64,256]{1,0:T(8,128)S(1)}, f32[64,256]{1,0:T(8,128)S(1)}, u32[]{:S(2)}, u32[]{:S(2)}) collective-permute-start(f32[64,256]{1,0:T(8,128)S(1)} %divide_multiply_fusion.refs_0_), channel_id=1, source_target_pairs={{0,192},{32,224},{64,128},{96,160},{128,64},{160,96},{192,0},{224,... | collective-permute-start | bytes 196616 | tf_op jit(solution)/shard_map/ppermute | solution.py:624
  120.2 3.3 %collective-permute-start.15 = (f32[4,64,256]{2,1,0:T(8,128)S(1)}, f32[4,64,256]{2,1,0:T(8,128)S(1)}, u32[]{:S(2)}, u32[]{:S(2)}) collective-permute-start(f32[4,64,256]{2,1,0:T(8,128)S(1)} %pad_maximum_fusion), channel_id=1, source_target_pairs={{0,32},{32,0},{64,96},{96,64},{128,160},{160,128},{192,224},{224,1... | collective-permute-start | bytes 786440 | tf_op jit(solution)/shard_map/ppermute | solution.py:624
